TPU v7x, 32 devices: a whole 2x2x4 slice. The times are simulated.
32 devices in a mesh: groups: 2 (over x), row: 8 (over z, y), col: 2 (over core).
Axes of the slice: x: 2, y: 2, z: 4, core: 2. Of those that a mesh axis runs over, the one named last changes fastest.
Arguments:
- node_features: bfloat16 [32768, 256], P(('groups', 'row', 'col')), parts along dimension 0, may hold values from -6 to 6
- tile_rows: int32 [16, 2, 384], P(('groups', 'row'), 'col'), parts along dimension 0, may hold values from 0 to 15, as said below
- tile_cols: int32 [16, 2, 384], P(('groups', 'row'), 'col'), parts along dimension 0, may hold values from 0 to 63
- tile_masks: int32 [16, 2, 384, 128, 8], P(('groups', 'row'), 'col'), parts along dimension 0, may hold values from 0 to 65535
- tile_count: int32 [16, 2], P(('groups', 'row'), 'col'), parts along dimension 0, may hold values from 96 to 384, as said below
- weight_self: bfloat16 [256, 256], replicated, may hold values from -0.375 to 0.375
- weight_neigh: bfloat16 [256, 256], replicated, may hold values from -0.375 to 0.375
- bias_term: float32 [256], replicated, may hold values from -3 to 3
- out_grad: bfloat16 [32768, 256], P(('groups', 'row', 'col')), parts along dimension 0, may hold values from -6 to 6
Outputs:
- node_out: bfloat16 [32768, 256], P(('groups', 'row', 'col')), parts along dimension 0
- feature_grad: bfloat16 [32768, 256], P(('groups', 'row', 'col')), parts along dimension 0
- grad_self: float32 [512, 256], P('groups'), parts along dimension 0
- grad_neigh: float32 [512, 256], P('groups'), parts along dimension 0
- grad_bias: float32 [512], P('groups'), parts along dimension 0
There are 2 independent parts, one for each index of `groups`. A program takes and returns all parts, laid end to end along the dimension named above; an argument that names none is the same for every part. Nothing has to cross between parts.
Inputs may be any that keep to these rules, and one draw needn't show every extreme that they name: The slots of one grid position name distinct (tile_rows, tile_cols) pairs. `tile_count`: in every draw some grid position has all 384 slots live.
All inputs are finite; a program needn't handle non-finite values.
Results may differ from a plain program's by a relative error of at most 0.0065.
Values may be sent and summed in bfloat16 or wider, within the bound.
No kernel may reach another device: no remote copies, remote signals or barrier semaphores. Data moves between devices by JAX's collectives and lax.ppermute only.
A program may use at most 128 MiB of HBM per device.

v0:
```python
from functools import partial
import math

import jax
import jax.numpy as jnp
from jax import lax
from jax.sharding import PartitionSpec as P


def unpack_tiles(mask_words):
    bit_shifts = jnp.arange(16, dtype=jnp.int32)
    bit_values = jnp.bitwise_and(jnp.right_shift(mask_words[..., None], bit_shifts), 1)
    return bit_values.reshape(mask_words.shape[:-2] + (128, 128))


def one_hot_rows(indices, extent):
    return (indices[:, None] == jnp.arange(extent, dtype=jnp.int32)[None, :]).astype(jnp.bfloat16)


def place_terms(placing, values):
    high_part = values.astype(jnp.bfloat16)
    low_part = (values - high_part.astype(jnp.float32)).astype(jnp.bfloat16)
    placed = jnp.einsum("gr,gtf->rtf", placing, high_part, preferred_element_type=jnp.float32)
    return placed + jnp.einsum("gr,gtf->rtf", placing, low_part, preferred_element_type=jnp.float32)


def local(
    node_features,
    tile_rows,
    tile_cols,
    tile_masks,
    tile_count,
    weight_self,
    weight_neigh,
    bias_term,
    out_grad,
):
    node_rows, width = node_features.shape
    grid_rows = lax.axis_size("row")
    grid_cols = lax.axis_size("col")
    slot_total = tile_masks.shape[2]
    group_size = math.gcd(slot_total, 64)
    row_index = tile_rows.reshape(slot_total)
    col_index = tile_cols.reshape(slot_total)
    mask_words = tile_masks.reshape(slot_total, 128, 8)
    live_total = tile_count.reshape(())
    block_rows = grid_cols * node_rows // 128
    block_cols = grid_rows * node_rows // 128
    turns = slot_total // group_size

    def tile_group(turn_index):
        first_slot = turn_index * group_size
        words_here = lax.dynamic_slice_in_dim(mask_words, first_slot, group_size, 0)
        rows_here = lax.dynamic_slice_in_dim(row_index, first_slot, group_size, 0)
        cols_here = lax.dynamic_slice_in_dim(col_index, first_slot, group_size, 0)
        live_flags = (first_slot + jnp.arange(group_size, dtype=jnp.int32) < live_total).astype(
            jnp.int32
        )
        tile_block = (unpack_tiles(words_here) * live_flags[:, None, None]).astype(jnp.bfloat16)
        return (
            tile_block,
            one_hot_rows(rows_here, block_rows),
            one_hot_rows(cols_here, block_cols),
        )

    gathered = lax.all_gather(node_features, "row", axis=0, tiled=True)
    feature_blocks = gathered.reshape(block_cols, 128, width)

    def forward_step(turn_index, carry):
        totals, degrees = carry
        tile_block, pick_rows, pick_cols = tile_group(turn_index)
        chosen = jnp.einsum(
            "gc,cuf->guf", pick_cols, feature_blocks, preferred_element_type=jnp.float32
        ).astype(jnp.bfloat16)
        products = jnp.einsum(
            "gtu,guf->gtf", tile_block, chosen, preferred_element_type=jnp.float32
        )
        totals = totals + place_terms(pick_rows, products)
        row_counts = jnp.sum(tile_block, axis=2, dtype=jnp.float32).astype(jnp.bfloat16)
        degrees = degrees + jnp.einsum(
            "gr,gt->rt", pick_rows, row_counts, preferred_element_type=jnp.float32
        )
        return (totals, degrees)

    start_totals = jnp.zeros((block_rows, 128, width), jnp.float32)
    start_degrees = jnp.zeros((block_rows, 128), jnp.float32)
    totals, degrees = lax.fori_loop(0, turns, forward_step, (start_totals, start_degrees))
    aggregated, degree = (
        lax.psum_scatter(
            totals.reshape(block_rows * 128, width), "col", scatter_dimension=0, tiled=True
        ),
        lax.psum_scatter(degrees.reshape(block_rows * 128), "col", scatter_dimension=0, tiled=True),
    )
    divisor = jnp.maximum(degree, 1.0)[:, None]
    neighbour_mean = (aggregated / divisor).astype(jnp.bfloat16)
    pre = jnp.dot(node_features, weight_self, preferred_element_type=jnp.float32)
    pre = pre + jnp.dot(neighbour_mean, weight_neigh, preferred_element_type=jnp.float32)
    pre = pre + bias_term
    activate = partial(jax.nn.gelu, approximate=True)
    activated, pullback = jax.vjp(activate, pre)
    node_out = activated.astype(jnp.bfloat16)
    pre_grad = pullback(out_grad.astype(jnp.float32))[0]
    grad_b = pre_grad.astype(jnp.bfloat16)
    local_self = jnp.einsum("nf,ng->fg", node_features, grad_b, preferred_element_type=jnp.float32)
    local_neigh = jnp.einsum(
        "nf,ng->fg", neighbour_mean, grad_b, preferred_element_type=jnp.float32
    )
    local_bias = jnp.sum(pre_grad, axis=0)
    mean_grad = (
        jnp.einsum("ng,fg->nf", grad_b, weight_neigh, preferred_element_type=jnp.float32) / divisor
    ).astype(jnp.bfloat16)
    row_grads = lax.all_gather(mean_grad, "col", axis=0, tiled=True)
    grad_blocks = row_grads.reshape(block_rows, 128, width)

    def backward_step(turn_index, column_totals):
        tile_block, pick_rows, pick_cols = tile_group(turn_index)
        chosen = jnp.einsum(
            "gr,rtf->gtf", pick_rows, grad_blocks, preferred_element_type=jnp.float32
        ).astype(jnp.bfloat16)
        products = jnp.einsum(
            "gtu,gtf->guf", tile_block, chosen, preferred_element_type=jnp.float32
        )
        return column_totals + place_terms(pick_cols, products)

    column_totals = lax.fori_loop(
        0, turns, backward_step, jnp.zeros((block_cols, 128, width), jnp.float32)
    )
    neighbour_grad = lax.psum_scatter(
        column_totals.reshape(block_cols * 128, width), "row", scatter_dimension=0, tiled=True
    )
    summed_self, summed_neigh, summed_bias = lax.psum(
        (local_self, local_neigh, local_bias), ("row", "col")
    )
    grad_scale = (node_rows * grid_rows * grid_cols) ** (-0.5)
    self_term = jnp.einsum("ng,fg->nf", grad_b, weight_self, preferred_element_type=jnp.float32)
    feature_grad = (self_term + neighbour_grad).astype(jnp.bfloat16)
    return (
        node_out,
        feature_grad,
        summed_self * grad_scale,
        summed_neigh * grad_scale,
        summed_bias * grad_scale,
    )


def solution(mesh):
    in_specs = (
        P(("groups", "row", "col"), None),
        P(("groups", "row"), "col", None),
        P(("groups", "row"), "col", None),
        P(("groups", "row"), "col", None, None, None),
        P(("groups", "row"), "col"),
        P(),
        P(),
        P(),
        P(("groups", "row", "col"), None),
    )
    out_specs = (
        P(("groups", "row", "col"), None),
        P(("groups", "row", "col"), None),
        P("groups", None),
        P("groups", None),
        P("groups"),
    )
    return jax.shard_map(local, mesh=mesh, in_specs=in_specs, out_specs=out_specs, check_vma=False)
```

profile of v0, /device:TPU:0, one launch (start us, length us, event | category | flops | bytes accessed | tf_op | source)
XLA Modules:
  0.0 500.7 jit_solution(12557847067732766537)
XLA Ops:
  9.4 76.9 %all-gather.3.cloned.1.call-done = bf16[8192,256]{1,0:T(8,128)(2,1)} async-done(((bf16[1024,256]{1,0:T(8,128)(2,1)}), bf16[8192,256]{1,0:T(8,128)(2,1)}) %all-gather.3.cloned.1.call-update) | async-done | bytes 4194320 | tf_op jit(solution)/shard_map/all_gather | solution.py:66
  86.3 6.5 %copy.54 = bf16[64,128,256]{2,0,1:T(8,128)(2,1)} copy(bf16[64,128,256]{2,1,0:T(8,128)(2,1)} %bitcast.88) | data formatting | bytes 8388608
  92.8 97.2 %while.32 = (s32[]{:T(128)}, f32[16,128,256]{2,0,1:T(8,128)S(1)}, f32[16,128]{1,0:T(8,128)S(1)}, s32[384]{0:T(512)S(1)}, s32[384,128,8]{1,2,0:T(8,128)}, /*index...) while((s32[]{:T(128)}, f32[16,128,256]{2,0,1:T(8,128)S(1)}, ...), condition=%wide.region_2.0_spmd.clone, body=%wide.region_0.0_spmd.clone.sunk | while | flops 961285312 | bytes 43045832 | solution.py:87
  97.1 3.5 convolution_convert_fusion.4
  113.3 3.5 convolution_convert_fusion.4
  116.8 3.3 subtract_convert_fusion.4
  129.5 3.5 convolution_convert_fusion.4
  132.9 3.3 subtract_convert_fusion.4
  145.6 3.5 convolution_convert_fusion.4
  149.1 3.3 subtract_convert_fusion.4
  161.8 3.5 convolution_convert_fusion.4
  178.0 3.5 convolution_convert_fusion.4
  196.8 3.9 reduce-scatter.3.cloned.1.call-done
  208.4 8.1 %all-gather.5.cloned.1.call-done = bf16[2048,256]{1,0:T(8,128)(2,1)} async-done(((bf16[1024,256]{1,0:T(8,128)(2,1)}), bf16[2048,256]{1,0:T(8,128)(2,1)}) %all-gather.5.cloned.1.call-update) | async-done | bytes 1048592 | tf_op jit(solution)/shard_map/all_gather | solution.py:112
  218.4 112.0 %while.33 = (s32[]{:T(128)}, f32[64,128,256]{2,0,1:T(8,128)}, s32[384]{0:T(512)S(1)}, s32[384,128,8]{1,2,0:T(8,128)}, s32[]{:T(128)}, /*index=5*/s32[384]{0:T(51...) while((s32[]{:T(128)}, f32[64,128,256]{2,0,1:T(8,128)}, ...), condition=%wide.region_6.0_spmd.clone, body=%wide.region_5.0_spmd.clone.sunk | while | flops 1161831680 | bytes 123474440 | solution.py:125
  229.4 4.5 select_add_fusion.5
  248.1 4.5 select_add_fusion.5
  266.7 4.5 select_add_fusion.5
  285.4 4.5 select_add_fusion.5
  304.1 4.5 select_add_fusion.5
  322.7 4.5 select_add_fusion.5
  330.5 11.5 %copy.57 = f32[64,128,256]{2,1,0:T(8,128)} copy(f32[64,128,256]{2,0,1:T(8,128)} %get-tuple-element.330) | data formatting | bytes 16777216 | tf_op jit(solution)/shard_map/while | solution.py:125
  342.0 35.9 %psum.23 = f32[256]{0:T(256)S(1)} all-reduce(f32[256]{0:T(256)S(1)} %get-tuple-element.468), channel_id=1, replica_groups=mesh['groups'=2,'row'=8,'col'=2] {'row','col'}, use_global_device_ids=true, to_apply=%region_11.0 | all-reduce | flops 256 | bytes 2048 | tf_op jit(solution)/shard_map/psum | solution.py:131
  381.2 110.7 %reduce-scatter.5.cloned.1.call-done = f32[1024,256]{1,0:T(8,128)} async-done(((f32[8192,256]{1,0:T(8,128)}), f32[1024,256]{1,0:T(8,128)}) %reduce-scatter.5.cloned.1.call-update) | async-done | bytes 1048592 | tf_op jit(solution)/shard_map/reduce_scatter | solution.py:128
  (219 shorter events, 173.9 us)
Async XLA Ops:
  7.2 194.9 %copy-start = (bf16[256,256]{1,0:T(8,128)(2,1)S(1)}, bf16[256,256]{1,0:T(8,128)(2,1)}, u32[]{:S(2)}) copy-start(bf16[256,256]{1,0:T(8,128)(2,1)} %param.19) | copy-start | bytes 393220
  7.2 79.1 %all-gather.3.cloned.1.call-start = ((), (), s32[]{:S(2)}) async-start(), calls=%async_computation.2 | async-start | bytes 4718592 | tf_op jit(solution)/shard_map/all_gather | solution.py:66
  7.9 192.8 %reduce-scatter.3.cloned.1.call-start = ((), (), s32[]{:S(2)}) async-start(), calls=%async_computation.3 | async-start | bytes 3145728 | tf_op jit(solution)/shard_map/reduce_scatter | solution.py:89
  190.0 3.9 copy-start.5
  190.1 3.9 copy-start.6
  190.1 12.1 %copy-start.7 = (f32[256]{0:T(256)S(1)}, f32[256]{0:T(256)}, u32[]{:S(2)}) copy-start(f32[256]{0:T(256)} %param.20) | copy-start | bytes 3076
  192.7 23.9 %all-gather.5.cloned.1.call-start = ((), (), s32[]{:S(2)}) async-start(), calls=%async_computation.4 | async-start | bytes 1572864 | tf_op jit(solution)/shard_map/all_gather | solution.py:112
  205.1 13.4 %copy-start.3 = (bf16[1024,256]{1,0:T(8,128)(2,1)}, bf16[1024,256]{1,0:T(8,128)(2,1)S(1)}, u32[]{:S(2)}) copy-start(bf16[1024,256]{1,0:T(8,128)(2,1)S(1)} %get-tuple-element.469) | copy-start | bytes 1572868
  206.2 172.2 %all-reduce.4.cloned.1.call-start = ((), (), s32[]{:S(2)}) async-start(), calls=%async_computation.6 | async-start | bytes 1048576 | tf_op jit(solution)/shard_map/psum | solution.py:131
  208.4 283.4 %reduce-scatter.5.cloned.1.call-start = ((), (), s32[]{:S(2)}) async-start(), calls=%async_computation.5 | async-start | bytes 9437184 | tf_op jit(solution)/shard_map/reduce_scatter | solution.py:128
  221.8 7.6 %slice-start = ((s8[8388608]{0:T(1024)(128)(4,1)}), s8[4194304]{0:T(1024)(128)(4,1)S(1)}, s32[]{:S(2)}) async-start(s8[8388608]{0:T(1024)(128)(4,1)} %bitcast.83), calls=%async_computation.7 | async-start | bytes 8388608 | tf_op jit(solution)/shard_map/while
  223.1 6.3 %slice-start.1 = ((s8[8388608]{0:T(1024)(128)(4,1)}), s8[4194304]{0:T(1024)(128)(4,1)S(1)}, s32[]{:S(2)}) async-start(s8[8388608]{0:T(1024)(128)(4,1)} %bitcast.83), calls=%async_computation.8 | async-start | bytes 8388608 | tf_op jit(solution)/shard_map/while
  240.5 7.6 %slice-start = ((s8[8388608]{0:T(1024)(128)(4,1)}), s8[4194304]{0:T(1024)(128)(4,1)S(1)}, s32[]{:S(2)}) async-start(s8[8388608]{0:T(1024)(128)(4,1)} %bitcast.83), calls=%async_computation.7 | async-start | bytes 8388608 | tf_op jit(solution)/shard_map/while
  241.8 6.3 %slice-start.1 = ((s8[8388608]{0:T(1024)(128)(4,1)}), s8[4194304]{0:T(1024)(128)(4,1)S(1)}, s32[]{:S(2)}) async-start(s8[8388608]{0:T(1024)(128)(4,1)} %bitcast.83), calls=%async_computation.8 | async-start | bytes 8388608 | tf_op jit(solution)/shard_map/while
  259.1 7.6 %slice-start = ((s8[8388608]{0:T(1024)(128)(4,1)}), s8[4194304]{0:T(1024)(128)(4,1)S(1)}, s32[]{:S(2)}) async-start(s8[8388608]{0:T(1024)(128)(4,1)} %bitcast.83), calls=%async_computation.7 | async-start | bytes 8388608 | tf_op jit(solution)/shard_map/while
  260.4 6.3 %slice-start.1 = ((s8[8388608]{0:T(1024)(128)(4,1)}), s8[4194304]{0:T(1024)(128)(4,1)S(1)}, s32[]{:S(2)}) async-start(s8[8388608]{0:T(1024)(128)(4,1)} %bitcast.83), calls=%async_computation.8 | async-start | bytes 8388608 | tf_op jit(solution)/shard_map/while
  277.8 7.6 %slice-start = ((s8[8388608]{0:T(1024)(128)(4,1)}), s8[4194304]{0:T(1024)(128)(4,1)S(1)}, s32[]{:S(2)}) async-start(s8[8388608]{0:T(1024)(128)(4,1)} %bitcast.83), calls=%async_computation.7 | async-start | bytes 8388608 | tf_op jit(solution)/shard_map/while
  279.1 6.3 %slice-start.1 = ((s8[8388608]{0:T(1024)(128)(4,1)}), s8[4194304]{0:T(1024)(128)(4,1)S(1)}, s32[]{:S(2)}) async-start(s8[8388608]{0:T(1024)(128)(4,1)} %bitcast.83), calls=%async_computation.8 | async-start | bytes 8388608 | tf_op jit(solution)/shard_map/while
  296.5 7.6 %slice-start = ((s8[8388608]{0:T(1024)(128)(4,1)}), s8[4194304]{0:T(1024)(128)(4,1)S(1)}, s32[]{:S(2)}) async-start(s8[8388608]{0:T(1024)(128)(4,1)} %bitcast.83), calls=%async_computation.7 | async-start | bytes 8388608 | tf_op jit(solution)/shard_map/while
  297.8 6.3 %slice-start.1 = ((s8[8388608]{0:T(1024)(128)(4,1)}), s8[4194304]{0:T(1024)(128)(4,1)S(1)}, s32[]{:S(2)}) async-start(s8[8388608]{0:T(1024)(128)(4,1)} %bitcast.83), calls=%async_computation.8 | async-start | bytes 8388608 | tf_op jit(solution)/shard_map/while
  315.1 7.6 %slice-start = ((s8[8388608]{0:T(1024)(128)(4,1)}), s8[4194304]{0:T(1024)(128)(4,1)S(1)}, s32[]{:S(2)}) async-start(s8[8388608]{0:T(1024)(128)(4,1)} %bitcast.83), calls=%async_computation.7 | async-start | bytes 8388608 | tf_op jit(solution)/shard_map/while
  316.4 6.3 %slice-start.1 = ((s8[8388608]{0:T(1024)(128)(4,1)}), s8[4194304]{0:T(1024)(128)(4,1)S(1)}, s32[]{:S(2)}) async-start(s8[8388608]{0:T(1024)(128)(4,1)} %bitcast.83), calls=%async_computation.8 | async-start | bytes 8388608 | tf_op jit(solution)/shard_map/while
  341.9 149.9 %copy-start.4 = (bf16[1024,256]{1,0:T(8,128)(2,1)S(1)}, bf16[1024,256]{1,0:T(8,128)(2,1)}, u32[]{:S(2)}) copy-start(bf16[1024,256]{1,0:T(8,128)(2,1)} %copy-done.3) | copy-start | bytes 1572868
  341.9 152.2 %copy-start.1 = (bf16[256,256]{1,0:T(8,128)(2,1)S(1)}, bf16[256,256]{1,0:T(8,128)(2,1)}, u32[]{:S(2)}) copy-start(bf16[256,256]{1,0:T(8,128)(2,1)} %param.19) | copy-start | bytes 393220
  (7 other events, 22.1 us)
Sparse Core Ops, SparseCore 0:
  10.1 76.0 all-gather.2
  192.8 7.8 reduce-scatter.2
  206.3 10.2 all-gather.4
  220.9 91.2 all-reduce.3
  342.1 149.7 reduce-scatter.4
where the time goes:
time: 502 us; the launch traced here: 501 us
  waiting for transfers between devices  200 us (40%)
  matrix products  153 us (30%)
  local copies, waits for them, and re-layouts  58.5 us (12%)
  blocking collectives  38.4 us (8%)
  other arithmetic  35 us (7%)
  between operations  14.6 us (3%)
    reduce_scatter x1, waiting for transfers between devices, local(): lax.psum_scatter(column_totals.reshape(block_cols * 128, width), 'row', s...  111 us
    all_gather x1, waiting for transfers between devices, local(): gathered = lax.all_gather(node_features, 'row', axis=0, tiled=True)  76.9 us
    dot_general x12, matrix products, place_terms(): jnp.einsum('gr,gtf->rtf', placing, high_part, preferred_element_type=jnp....  42.9 us
    psum x1, blocking collectives, local(): lax.psum((local_self, local_neigh, local_bias), ('row', 'col'))  35.9 us
    dot_general x12, matrix products, place_terms(): jnp.einsum('gr,gtf->rtf', placing, low_part, preferred_element_type=jnp.f...  33.8 us
    dot_general x6, matrix products, forward_step(): jnp.einsum('gc,cuf->guf', pick_cols, feature_blocks, preferred_element_ty...  20.8 us
    dot_general x6, matrix products, forward_step(): jnp.einsum('gtu,guf->gtf', tile_block, chosen, preferred_element_type=jnp...  19.8 us
    while x36, local copies, waits for them, and re-layouts  19.4 us
  transfers between devices with their start and end apart: 5, of which 4 were waited for; matrix products, arithmetic and copies ran while one was open for 23% of the time, Pallas kernels for 0%

commit v1 on v0

v1 whole, which is shorter than its diff:
```python
from functools import partial
import math

import jax
import jax.numpy as jnp
from jax import lax
from jax.experimental import pallas as pl
from jax.experimental.pallas import tpu as pltpu
from jax.sharding import PartitionSpec as P

VMEM_LIMIT = 48 * 1024 * 1024
GELU_C = math.sqrt(2.0 / math.pi)
F32 = jnp.float32
BF16 = jnp.bfloat16


def ring_order(n):
    return list(range(0, n, 2)) + list(range(n - 1, 0, -2))


def unpack_kernel(block_rows, table_ref, masks_ref, out_ref):
    c = pl.program_id(0)
    bit = lax.broadcasted_iota(jnp.int32, (16, 128), 0)
    for r in range(block_rows):
        slot = table_ref[c * block_rows + r]
        words = masks_ref[jnp.maximum(slot, 0)]
        words = jnp.where(slot >= 0, words, 0)
        for k in range(8):
            row = jnp.broadcast_to(words[k : k + 1, :], (16, 128))
            bits = jnp.bitwise_and(jnp.right_shift(row, bit), 1)
            out_ref[16 * k : 16 * k + 16, 128 * r : 128 * r + 128] = bits.astype(F32).astype(BF16)


def unpack(table, masks, block_rows, block_cols):
    return pl.pallas_call(
        partial(unpack_kernel, block_rows),
        grid_spec=pltpu.PrefetchScalarGridSpec(
            num_scalar_prefetch=1,
            grid=(block_cols,),
            in_specs=[pl.BlockSpec(masks.shape, lambda c, t: (0, 0, 0))],
            out_specs=pl.BlockSpec((128, block_rows * 128), lambda c, t: (c, 0)),
        ),
        out_shape=jax.ShapeDtypeStruct((block_cols * 128, block_rows * 128), BF16),
        compiler_params=pltpu.CompilerParams(vmem_limit_bytes=VMEM_LIMIT),
        cost_estimate=pl.CostEstimate(
            flops=0,
            bytes_accessed=block_cols * block_rows * 128 * 128 * 2 + masks.size * 4,
            transcendentals=0,
        ),
        name="unpack_tiles",
    )(table, masks)


def forward_kernel(pieces, has_acc, ids_ref, *refs):
    xs = refs[:pieces]
    bs = refs[pieces : 2 * pieces]
    acc_ref = refs[2 * pieces] if has_acc else None
    out_ref = refs[2 * pieces + int(has_acc)]
    turned = refs[2 * pieces + int(has_acc) + 1]

    @pl.when(pl.program_id(0) == 0)
    def _():
        for k in range(pieces):
            turned[k] = xs[k][...].T

    total = jnp.dot(turned[0], bs[0][...], preferred_element_type=F32)
    for k in range(1, pieces):
        total = total + jnp.dot(turned[k], bs[k][...], preferred_element_type=F32)
    if has_acc:
        total = total + acc_ref[...]
    out_ref[...] = total.astype(out_ref.dtype)


def forward_mm(pieces, ids, dense, acc, first_block, blocks, out_dtype, name):
    rows, width = pieces[0].shape
    count = len(pieces)
    tblk = 512
    scalars = jnp.stack([jnp.asarray(i, jnp.int32) for i in ids] + [jnp.asarray(first_block, jnp.int32)])

    def piece_spec(k):
        return pl.BlockSpec((rows, tblk), lambda t, s: (s[k], s[count] + t))

    in_specs = [pl.BlockSpec((rows, width), lambda t, s: (0, 0)) for _ in range(count)]
    in_specs += [piece_spec(k) for k in range(count)]
    args = list(pieces) + [dense] * count
    if acc is not None:
        in_specs.append(pl.BlockSpec((width, tblk), lambda t, s: (0, s[count] + t)))
        args.append(acc)
    return pl.pallas_call(
        partial(forward_kernel, count, acc is not None),
        grid_spec=pltpu.PrefetchScalarGridSpec(
            num_scalar_prefetch=1,
            grid=(blocks,),
            in_specs=in_specs,
            out_specs=pl.BlockSpec((width, tblk), lambda t, s: (0, t)),
            scratch_shapes=[pltpu.VMEM((count, width, rows), BF16)],
        ),
        out_shape=jax.ShapeDtypeStruct((width, blocks * tblk), out_dtype),
        compiler_params=pltpu.CompilerParams(vmem_limit_bytes=VMEM_LIMIT),
        cost_estimate=pl.CostEstimate(
            flops=2 * count * rows * width * blocks * tblk,
            bytes_accessed=count * rows * blocks * tblk * 2 + 8 * width * blocks * tblk,
            transcendentals=0,
        ),
        name=name,
    )(scalars, *args)


def middle_kernel(
    agg_ref, other_ref, div_ref, x_ref, og_ref, ws_ref, wn_ref, b_ref,
    mean_ref, out_ref, gb_ref, mg_ref, bias_ref,
):
    div = div_ref[...]
    rows = div.shape[1]
    width = x_ref.shape[1]
    mean = ((agg_ref[...] + other_ref[...].astype(F32)) / div).T.astype(BF16)
    mean_ref[...] = mean
    pre = jnp.dot(x_ref[...], ws_ref[...], preferred_element_type=F32)
    pre = pre + jnp.dot(mean, wn_ref[...], preferred_element_type=F32)
    pre = pre + b_ref[...]
    square = pre * pre
    bent = jnp.tanh(GELU_C * (pre + 0.044715 * (square * pre)))
    half = 0.5 * (1.0 + bent)
    out_ref[...] = (pre * half).astype(BF16)
    slope = half + 0.5 * pre * (1.0 - bent * bent) * (GELU_C * (1.0 + 3.0 * 0.044715 * square))
    pre_grad = og_ref[...].astype(F32) * slope
    grad_b = pre_grad.astype(BF16)
    gb_ref[...] = grad_b
    div_column = jnp.broadcast_to(div, (128, rows)).T
    div_full = jnp.concatenate([div_column] * (width // 128), axis=1)
    mean_grad = lax.dot_general(
        grad_b, wn_ref[...], (((1,), (1,)), ((), ())), preferred_element_type=F32
    )
    mg_ref[...] = (mean_grad / div_full).astype(BF16)
    part = jnp.sum(pre_grad.reshape(rows // 8, 8, width), axis=0)

    @pl.when(pl.program_id(0) == 0)
    def _():
        bias_ref[...] = part

    @pl.when(pl.program_id(0) != 0)
    def _():
        bias_ref[...] += part


def middle(agg, other, divisor, x, og, ws, wn, bias):
    rows, width = x.shape
    blk = 256
    turned = pl.BlockSpec((width, blk), lambda i: (0, i))
    plain = pl.BlockSpec((blk, width), lambda i: (i, 0))
    weight = pl.BlockSpec((width, width), lambda i: (0, 0))
    act = jax.ShapeDtypeStruct((rows, width), BF16)
    return pl.pallas_call(
        middle_kernel,
        grid=(rows // blk,),
        in_specs=[
            turned, turned, pl.BlockSpec((1, blk), lambda i: (0, i)), plain, plain, weight, weight,
            pl.BlockSpec((1, width), lambda i: (0, 0)),
        ],
        out_specs=[plain] * 4 + [pl.BlockSpec((8, width), lambda i: (0, 0))],
        out_shape=[act] * 4 + [jax.ShapeDtypeStruct((8, width), F32)],
        compiler_params=pltpu.CompilerParams(vmem_limit_bytes=VMEM_LIMIT),
        cost_estimate=pl.CostEstimate(
            flops=6 * rows * width * width, bytes_accessed=18 * rows * width, transcendentals=rows * width
        ),
        name="layer",
    )(agg, other, divisor, x, og, ws, wn, bias)


def backward_kernel(ids_ref, mine_ref, other_ref, b_mine, b_other, out_ref):
    total = jnp.dot(b_mine[...], mine_ref[...], preferred_element_type=F32)
    out_ref[...] = total + jnp.dot(b_other[...], other_ref[...], preferred_element_type=F32)


def backward_mm(ids, dense, mine, other, side, piece_rows, name):
    rows, width = mine.shape
    count = len(ids)
    scalars = jnp.stack([jnp.asarray(i, jnp.int32) for i in ids] + [side, 1 - side])
    grads = pl.BlockSpec((rows, width), lambda i, s: (0, 0))
    return pl.pallas_call(
        backward_kernel,
        grid_spec=pltpu.PrefetchScalarGridSpec(
            num_scalar_prefetch=1,
            grid=(count,),
            in_specs=[
                grads,
                grads,
                pl.BlockSpec((piece_rows, rows), lambda i, s: (s[i], s[count])),
                pl.BlockSpec((piece_rows, rows), lambda i, s: (s[i], s[count + 1])),
            ],
            out_specs=pl.BlockSpec((piece_rows, width), lambda i, s: (i, 0)),
        ),
        out_shape=jax.ShapeDtypeStruct((count * piece_rows, width), F32),
        compiler_params=pltpu.CompilerParams(vmem_limit_bytes=VMEM_LIMIT),
        cost_estimate=pl.CostEstimate(
            flops=4 * count * piece_rows * rows * width,
            bytes_accessed=4 * count * piece_rows * (rows + width),
            transcendentals=0,
        ),
        name=name,
    )(scalars, mine, other, dense, dense)


def local(
    node_features, tile_rows, tile_cols, tile_masks, tile_count,
    weight_self, weight_neigh, bias_term, out_grad,
):
    node_rows, width = node_features.shape
    n = lax.axis_size("row")
    grid_cols = lax.axis_size("col")
    slots = tile_masks.shape[2]
    block_rows = grid_cols * node_rows // 128
    block_cols = n * node_rows // 128
    half = node_rows // 2
    far = n // 2

    order = ring_order(n)
    clockwise = [(order[k], order[(k + 1) % n]) for k in range(n)]
    counter = [(b, a) for a, b in clockwise]
    swap = [(0, 1), (1, 0)]
    row_id = lax.axis_index("row")
    side = lax.axis_index("col").astype(jnp.int32)
    place_of = [order.index(r) for r in range(n)]
    place = jnp.array(place_of, jnp.int32)[row_id]
    ring = jnp.array(order * 3, jnp.int32)

    def shard_at(offset):
        return ring[place + n + offset]

    low, high = node_features[:half], node_features[half:]
    fl, fh, bl, bh = low, high, low, high
    arrivals = []
    for s in range(1, far):
        fl = lax.ppermute(fl, "row", clockwise)
        bh = lax.ppermute(bh, "row", counter)
        fh = lax.ppermute(fh, "row", clockwise)
        bl = lax.ppermute(bl, "row", counter)
        left, right = shard_at(-s), shard_at(s)
        arrivals.append(([fl, bh, fh, bl], [2 * left, 2 * right + 1, 2 * left + 1, 2 * right]))
    fl = lax.ppermute(fl, "row", clockwise)
    bh = lax.ppermute(bh, "row", counter)
    opposite = shard_at(far)
    last = ([fl, bh], [2 * opposite, 2 * opposite + 1])

    row_index = tile_rows.reshape(slots)
    col_index = tile_cols.reshape(slots)
    masks = jnp.transpose(tile_masks.reshape(slots, 128, 8), (0, 2, 1))
    slot_ids = jnp.arange(slots, dtype=jnp.int32)
    live = slot_ids < tile_count.reshape(())
    keys = jnp.where(live, col_index * block_rows + row_index, -1)
    spots = jnp.arange(block_rows * block_cols, dtype=jnp.int32)
    table = jnp.max(jnp.where(keys[None, :] == spots[:, None], slot_ids[None, :], -1), axis=1)
    dense = unpack(table, masks, block_rows, block_cols)
    counts = jnp.sum(lax.population_count(masks), axis=1).astype(BF16)
    pick = ((jnp.arange(block_rows, dtype=jnp.int32)[:, None] == row_index[None, :]) & live[None, :])
    degree = jnp.dot(pick.astype(BF16), counts, preferred_element_type=F32).reshape(2, 1, node_rows)
    sent_degree = lax.ppermute(lax.dynamic_index_in_dim(degree, 1 - side, 0, False), "col", swap)
    degree = lax.dynamic_index_in_dim(degree, side, 0, False) + sent_degree
    divisor = jnp.maximum(degree, 1.0)

    total_blocks = block_rows * 128 // 512
    own = shard_at(0)
    acc = forward_mm([low, high], [2 * own, 2 * own + 1], dense, None, 0, total_blocks, F32, "forward_own")
    for s, (pieces, ids) in enumerate(arrivals):
        acc = forward_mm(pieces, ids, dense, acc, 0, total_blocks, F32, "forward_step")
    per_side = total_blocks // 2
    for_other = forward_mm(*last, dense, acc, (1 - side) * per_side, per_side, BF16, "forward_send")
    received = lax.ppermute(for_other, "col", swap)
    mine = forward_mm(*last, dense, acc, side * per_side, per_side, F32, "forward_keep")

    mean, node_out, grad_b, mean_grad, bias_part = middle(
        mine, received, divisor, node_features, out_grad, weight_self, weight_neigh,
        bias_term.reshape(1, width),
    )
    other_grad = lax.ppermute(mean_grad, "col", swap)

    terms = backward_mm([2 * opposite, 2 * opposite + 1], dense, mean_grad, other_grad, side, half, "backward_far")
    fl = lax.ppermute(terms[:half].astype(BF16), "row", clockwise)
    bh = lax.ppermute(terms[half:].astype(BF16), "row", counter)
    fh = bl = None
    for s in range(far - 1, 0, -1):
        ahead, behind = shard_at(s), shard_at(-s)
        terms = backward_mm(
            [2 * ahead, 2 * behind + 1, 2 * ahead + 1, 2 * behind],
            dense, mean_grad, other_grad, side, half, "backward_step",
        )
        sums = []
        for k, got in enumerate((fl, bh, fh, bl)):
            part = terms[k * half : (k + 1) * half]
            sums.append((part if got is None else part + got.astype(F32)).astype(BF16))
        fl = lax.ppermute(sums[0], "row", clockwise)
        bh = lax.ppermute(sums[1], "row", counter)
        fh = lax.ppermute(sums[2], "row", clockwise)
        bl = lax.ppermute(sums[3], "row", counter)
    terms = backward_mm([2 * own, 2 * own + 1], dense, mean_grad, other_grad, side, half, "backward_own")
    self_term = lax.dot_general(
        grad_b, weight_self, (((1,), (1,)), ((), ())), preferred_element_type=F32
    )
    rest = terms + self_term
    feature_grad = jnp.concatenate(
        [
            (rest[:half] + fl.astype(F32) + bl.astype(F32)).astype(BF16),
            (rest[half:] + fh.astype(F32) + bh.astype(F32)).astype(BF16),
        ],
        axis=0,
    )

    grad_scale = (node_rows * n * grid_cols) ** (-0.5)
    contract = (((0,), (0,)), ((), ()))
    both = jnp.stack(
        [
            lax.dot_general(node_features, grad_b, contract, preferred_element_type=F32),
            lax.dot_general(mean, grad_b, contract, preferred_element_type=F32),
        ]
    )
    bias_rows = bias_part

    def exchange(send, bias_now, axis, perm):
        got = lax.ppermute(jnp.concatenate([send, bias_now], axis=0), axis, perm)
        return got[: send.shape[0]], bias_now + got[send.shape[0] :]

    got, bias_rows = exchange(
        lax.dynamic_index_in_dim(both, 1 - side, 0, False), bias_rows, "col", swap
    )
    matrix = lax.dynamic_index_in_dim(both, side, 0, False) + got
    bits = int(math.log2(n))
    for b in range(bits):
        perm = [(r, r ^ (1 << b)) for r in range(n)]
        flag = (row_id >> b) & 1
        parts = matrix.reshape(2, matrix.shape[0] // 2, width)
        got, bias_rows = exchange(
            lax.dynamic_index_in_dim(parts, 1 - flag, 0, False), bias_rows, "row", perm
        )
        matrix = lax.dynamic_index_in_dim(parts, flag, 0, False) + got
    for b in reversed(range(bits)):
        perm = [(r, r ^ (1 << b)) for r in range(n)]
        flag = (row_id >> b) & 1
        got = lax.ppermute(matrix, "row", perm)
        matrix = jnp.concatenate(
            [jnp.where(flag == 0, matrix, got), jnp.where(flag == 0, got, matrix)], axis=0
        )
    matrix = matrix * grad_scale
    got = lax.ppermute(matrix, "col", swap)
    grad_self = jnp.where(side == 0, matrix, got)
    grad_neigh = jnp.where(side == 0, got, matrix)
    grad_bias = jnp.sum(bias_rows, axis=0) * grad_scale
    return node_out, feature_grad, grad_self, grad_neigh, grad_bias


def solution(mesh):
    in_specs = (
        P(("groups", "row", "col"), None),
        P(("groups", "row"), "col", None),
        P(("groups", "row"), "col", None),
        P(("groups", "row"), "col", None, None, None),
        P(("groups", "row"), "col"),
        P(),
        P(),
        P(),
        P(("groups", "row", "col"), None),
    )
    out_specs = (
        P(("groups", "row", "col"), None),
        P(("groups", "row", "col"), None),
        P("groups", None),
        P("groups", None),
        P("groups"),
    )
    return jax.shard_map(local, mesh=mesh, in_specs=in_specs, out_specs=out_specs, check_vma=False)
```

time: 502 us -> 196 us (0.39)
  waiting for transfers between devices: 200 us -> 27.1 us
  matrix products: 153 us -> 1.14 us
  Pallas kernels: 0 us -> 91.9 us
  local copies, waits for them, and re-layouts: 58.5 us -> 6.05 us
  starting transfers between devices: 0.2 us -> 44.1 us
  blocking collectives: 38.4 us -> 0 us
  other arithmetic: 35 us -> 7.49 us
    dot_general x60 -> x4, matrix products: 153 us -> 1.14 us  [the longest x1 0.35 us: local(): lax.dot_general(node_features, grad_b, contract, preferred_element_type=F32)]
    reduce_scatter x2 -> x0, waiting for transfers between devices: 115 us -> none  [the longest x1 111 us: local(): lax.psum_scatter(column_totals.reshape(block_cols * 128, width), 'row', s...]
    pallas_call x0 -> x13, Pallas kernels: none -> 91.9 us  [the longest x1 32.1 us: unpack(): pl.pallas_call(partial(unpack_kernel, block_rows), grid_spec=pltpu.Prefet...]
    all_gather x2 -> x0, waiting for transfers between devices: 85 us -> none  [the longest x1 76.9 us: local(): gathered = lax.all_gather(node_features, 'row', axis=0, tiled=True)]
    ppermute x0 -> x39, starting transfers between devices: none -> 44.1 us  [the longest x4 9.1 us: local(): fl = lax.ppermute(fl, 'row', clockwise)]
    psum x1 -> x0, blocking collectives: 35.9 us -> none  [local(): lax.psum((local_self, local_neigh, local_bias), ('row', 'col'))]
    while x38 -> x0, local copies, waits for them, and re-layouts: 33.4 us -> none
    ppermute x0 -> x39, waiting for transfers between devices: none -> 27.1 us  [the longest x4 9.29 us: exchange(): got = lax.ppermute(jnp.concatenate([send, bias_now], axis=0), axis, perm)]
  transfers between devices with their start and end apart: 5 -> 39, of which waited for: 4 -> 11; matrix products, arithmetic and copies ran while one was open for 23% -> 5% of each run, Pallas kernels for 0% -> 43%
where the time goes in v1:
time: 196 us; the launch traced here: 195 us
  Pallas kernels  91.9 us (47%)
  starting transfers between devices  44.1 us (22%)
  waiting for transfers between devices  27.1 us (14%)
  between operations  17.4 us (9%)
  other arithmetic  7.49 us (4%)
  local copies, waits for them, and re-layouts  6.05 us (3%)
    pallas_call x1, Pallas kernels, unpack(): pl.pallas_call(partial(unpack_kernel, block_rows), grid_spec=pltpu.Prefet...  32.1 us
    pallas_call x6, Pallas kernels, forward_mm(): pl.pallas_call(partial(forward_kernel, count, acc is not None), grid_spec...  30.1 us
    pallas_call x5, Pallas kernels, backward_mm(): pl.pallas_call(backward_kernel, grid_spec=pltpu.PrefetchScalarGridSpec(nu...  25.2 us
    ppermute x4, waiting for transfers between devices, exchange(): got = lax.ppermute(jnp.concatenate([send, bias_now], axis=0), axis, perm)  9.29 us
    ppermute x4, starting transfers between devices, local(): fl = lax.ppermute(fl, 'row', clockwise)  9.1 us
    ppermute x3, waiting for transfers between devices, local(): fl = lax.ppermute(sums[0], 'row', clockwise)  7.58 us
    ppermute x4, starting transfers between devices, exchange(): got = lax.ppermute(jnp.concatenate([send, bias_now], axis=0), axis, perm)  6.94 us
    ppermute x3, starting transfers between devices, local(): got = lax.ppermute(matrix, 'row', perm)  6.18 us
  transfers between devices with their start and end apart: 39, of which 11 were waited for; matrix products, arithmetic and copies ran while one was open for 5% of the time, Pallas kernels for 43%

profile of v1, /device:TPU:0, one launch (start us, length us, event | category | flops | bytes accessed | tf_op | source)
XLA Modules:
  0.0 195.2 jit_solution(13392392885886342228)
XLA Ops:
  1.7 3.1 %collective-permute-start = (bf16[512,256]{1,0:T(8,128)(2,1)S(1)}, bf16[512,256]{1,0:T(8,128)(2,1)S(1)}, u32[]{:S(2)}, u32[]{:S(2)}) collective-permute-start(bf16[512,256]{1,0:T(8,128)(2,1)S(1)} %get-tuple-element.34.refs_0_), channel_id=1, source_target_pairs={{0,4},{4,8},{8,12},{12,14},{14,10},{10,6},{6,2},{2,0},{1,5},{5,9},... | collective-permute-start | bytes 786440 | tf_op jit(solution)/shard_map/ppermute | solution.py:234
  29.1 32.1 %unpack_tiles.1.refs_2_.refs_3_.refs_4_.refs_5_.refs_6_.refs_7_.b_mine.b_other = bf16[8192,2048]{1,0:T(8,128)(2,1)} custom-call(s32[1024]{0:T(1024)S(1)} %select_reduce_fusion.table_ref, s32[384,8,128]{2,1,0:T(8,128)S(1)} %bitcast.67), custom_call_target="tpu_custom_call" | custom-call | bytes 35127296 | tf_op jit(solution)/shard_map/unpack_tiles/pallas_call | solution.py:35
  67.3 3.9 %collective-permute-done.1.refs_0_ = bf16[512,256]{1,0:T(8,128)(2,1)S(1)} collective-permute-done((bf16[512,256]{1,0:T(8,128)(2,1)S(1)}, bf16[512,256]{1,0:T(8,128)(2,1)S(1)}, u32[]{:S(2)}, u32[]{:S(2)}) %collective-permute-start.1) | collective-permute-done | bytes 262176 | tf_op jit(solution)/shard_map/ppermute | solution.py:234
  73.2 4.7 %forward_own.1.refs_8_ = f32[256,2048]{1,0:T(8,128)S(1)} custom-call(s32[3]{0:T(128)S(1)} %pad_add_fusion.2.ids_ref, bf16[512,256]{1,0:T(8,128)(2,1)S(1)} %get-tuple-element.34.refs_0_, bf16[512,256]{1,0:T(8,128)(2,1)S(1)} %get-tuple-element.33.refs_1_, bf16[8192,2048]{1,0:T(8,128)(2,1)} %unpack_tiles.1.refs_2_.refs_3_.refs_4_.refs_5_.refs_6_.refs_7_.b_mine.b_other, ...), custom_call_target="tpu_custom_call" | custom-call | flops 1073741824 | bytes 8388608 | tf_op jit(solution)/shard_map/forward_own/pallas_call | solution.py:89
  80.0 6.5 %forward_step.3.refs_8_ = f32[256,2048]{1,0:T(8,128)S(1)} custom-call(s32[5]{0:T(128)S(1)} %stack.40.ids_ref, bf16[512,256]{1,0:T(8,128)(2,1)S(1)} %collective-permute-done.refs_0_, bf16[512,256]{1,0:T(8,128)(2,1)S(1)} %collective-permute-done.4.refs_1_, bf16[512,256]{1,0:T(8,128)(2,1)S(1)} %collective-permute-done.8.refs_2_, ...), custom_call_target="tpu_custom_call" | custom-call | flops 2147483648 | bytes 12582912 | tf_op jit(solution)/shard_map/forward_step/pallas_call | solution.py:89
  88.6 6.5 %forward_step.4.refs_8_ = f32[256,2048]{1,0:T(8,128)S(1)} custom-call(s32[5]{0:T(128)S(1)} %stack.39.ids_ref, bf16[512,256]{1,0:T(8,128)(2,1)S(1)} %collective-permute-done.1.refs_0_, bf16[512,256]{1,0:T(8,128)(2,1)S(1)} %collective-permute-done.5.refs_1_, bf16[512,256]{1,0:T(8,128)(2,1)S(1)} %collective-permute-done.9.refs_2_, ...), custom_call_target="tpu_custom_call" | custom-call | flops 2147483648 | bytes 12582912 | tf_op jit(solution)/shard_map/forward_step/pallas_call | solution.py:89
  95.2 6.5 %forward_step.5.refs_4_ = f32[256,2048]{1,0:T(8,128)S(1)} custom-call(s32[5]{0:T(128)S(1)} %stack.38.ids_ref, bf16[512,256]{1,0:T(8,128)(2,1)S(1)} %collective-permute-done.2.refs_0_, bf16[512,256]{1,0:T(8,128)(2,1)S(1)} %collective-permute-done.6.refs_1_, bf16[512,256]{1,0:T(8,128)(2,1)S(1)} %collective-permute-done.10.refs_2_, ...), custom_call_target="tpu_custom_call" | custom-call | flops 2147483648 | bytes 12582912 | tf_op jit(solution)/shard_map/forward_step/pallas_call | solution.py:89
  101.7 2.9 %forward_send.1 = bf16[256,1024]{1,0:T(8,128)(2,1)S(1)} custom-call(s32[3]{0:T(128)S(1)} %pad_add_fusion.3.ids_ref, bf16[512,256]{1,0:T(8,128)(2,1)S(1)} %collective-permute-done.3.refs_0_, bf16[512,256]{1,0:T(8,128)(2,1)S(1)} %collective-permute-done.7.refs_1_, bf16[8192,2048]{1,0:T(8,128)(2,1)} %unpack_tiles.1.refs_2_.refs_3_.refs_4_.refs_5_.refs_6_.refs_7_.b_mine.b_other, ...), custom_call_target="tpu_custom_call" | custom-call | flops 536870912 | bytes 4194304 | tf_op jit(solution)/shard_map/forward_send/pallas_call | solution.py:89
  106.7 3.0 %forward_keep.1.agg_ref = f32[256,1024]{1,0:T(8,128)S(1)} custom-call(s32[3]{0:T(128)S(1)} %pad_add_fusion.ids_ref, bf16[512,256]{1,0:T(8,128)(2,1)S(1)} %collective-permute-done.3.refs_0_, bf16[512,256]{1,0:T(8,128)(2,1)S(1)} %collective-permute-done.7.refs_1_, bf16[8192,2048]{1,0:T(8,128)(2,1)} %unpack_tiles.1.refs_2_.refs_3_.refs_4_.refs_5_.refs_6_.refs_7_.b_mine.b_other, ...), custom_call_target="tpu_custom_call" | custom-call | flops 536870912 | bytes 4194304 | tf_op jit(solution)/shard_map/forward_keep/pallas_call | solution.py:89
  109.8 4.4 %layer.1 = (bf16[1024,256]{1,0:T(8,128)(2,1)S(1)}, bf16[1024,256]{1,0:T(8,128)(2,1)}, bf16[1024,256]{1,0:T(8,128)(2,1)S(1)}, bf16[1024,256]{1,0:T(8,128)(2,1)S(1)}, f32[8,256]{1,0:T(8,128)S(1)}) custom-call(f32[256,1024]{1,0:T(8,128)S(1)} %forward_keep.1.agg_ref, bf16[256,1024]{1,0:T(8,128)(2,1)} %collective-permute-done.14.other_ref, ...), custom_call_target="tpu_custom_call" | custom-call | flops 402653184 | bytes 4718592 | tf_op jit(solution)/shard_map/layer/pallas_call | solution.py:153
  119.0 3.7 %collective-permute-done.32 = f32[136,256]{1,0:T(8,128)S(1)} collective-permute-done((f32[136,256]{1,0:T(8,128)S(1)}, f32[136,256]{1,0:T(8,128)S(1)}, u32[]{:S(2)}, u32[]{:S(2)}) %collective-permute-start.32) | collective-permute-done | bytes 139296 | tf_op jit(solution)/shard_map/ppermute | solution.py:319
  124.7 2.5 %collective-permute-done.33 = f32[72,256]{1,0:T(8,128)S(1)} collective-permute-done((f32[72,256]{1,0:T(8,128)S(1)}, f32[72,256]{1,0:T(8,128)S(1)}, u32[]{:S(2)}, u32[]{:S(2)}) %collective-permute-start.33) | collective-permute-done | bytes 73760 | tf_op jit(solution)/shard_map/ppermute | solution.py:319
  127.2 2.9 %collective-permute-start.34 = (f32[40,256]{1,0:T(8,128)S(1)}, f32[40,256]{1,0:T(8,128)S(1)}, u32[]{:S(2)}, u32[]{:S(2)}) collective-permute-start(f32[40,256]{1,0:T(8,128)S(1)} %pad_maximum_fusion.6), channel_id=1, source_target_pairs={{0,8},{2,10},{4,12},{6,14},{8,0},{10,2},{12,4},{14,6},{1,9},{3,11}... | collective-permute-start | bytes 122888 | tf_op jit(solution)/shard_map/ppermute | solution.py:319
  132.2 2.8 %collective-permute-start.35 = (f32[32,256]{1,0:T(8,128)S(1)}, f32[32,256]{1,0:T(8,128)S(1)}, u32[]{:S(2)}, u32[]{:S(2)}) collective-permute-start(f32[32,256]{1,0:T(8,128)S(1)} %slice_add_fusion.14), channel_id=1, source_target_pairs={{0,8},{2,10},{4,12},{6,14},{8,0},{10,2},{12,4},{14,6},{1,9},{3,11}... | collective-permute-start | bytes 98312 | tf_op jit(solution)/shard_map/ppermute | solution.py:338
  135.7 3.6 %backward_far.1 = f32[1024,256]{1,0:T(8,128)S(1)} custom-call(s32[4]{0:T(128)S(1)} %get-tuple-element.50.ids_ref, bf16[1024,256]{1,0:T(8,128)(2,1)S(1)} %get-tuple-element.11.mine_ref, bf16[1024,256]{1,0:T(8,128)(2,1)S(1)} %collective-permute-done.16.other_ref, bf16[8192,2048]{1,0:T(8,128)(2,1)} %unpack_tiles.1.refs_2_.refs_3_.refs_4_.refs_5_.refs_6_.refs_7_.b_mine.b_other, ...), custom_call_target="tpu_custom_call" | custom-call | flops 1073741824 | bytes 5242880 | tf_op jit(solution)/shard_map/backward_far/pallas_call | solution.py:180
  141.4 6.0 %backward_step.5 = f32[2048,256]{1,0:T(8,128)S(1)} custom-call(s32[6]{0:T(128)S(1)} %stack.49.ids_ref, bf16[1024,256]{1,0:T(8,128)(2,1)S(1)} %get-tuple-element.11.mine_ref, bf16[1024,256]{1,0:T(8,128)(2,1)S(1)} %collective-permute-done.16.other_ref, bf16[8192,2048]{1,0:T(8,128)(2,1)} %unpack_tiles.1.refs_2_.refs_3_.refs_4_.refs_5_.refs_6_.refs_7_.b_mine.b_other, ...), custom_call_target="tpu_custom_call" | custom-call | flops 2147483648 | bytes 10485760 | tf_op jit(solution)/shard_map/backward_step/pallas_call | solution.py:180
  149.8 6.0 %backward_step.4 = f32[2048,256]{1,0:T(8,128)S(1)} custom-call(s32[6]{0:T(128)S(1)} %stack.48.ids_ref, bf16[1024,256]{1,0:T(8,128)(2,1)S(1)} %get-tuple-element.11.mine_ref, bf16[1024,256]{1,0:T(8,128)(2,1)S(1)} %collective-permute-done.16.other_ref, bf16[8192,2048]{1,0:T(8,128)(2,1)} %unpack_tiles.1.refs_2_.refs_3_.refs_4_.refs_5_.refs_6_.refs_7_.b_mine.b_other, ...), custom_call_target="tpu_custom_call" | custom-call | flops 2147483648 | bytes 10485760 | tf_op jit(solution)/shard_map/backward_step/pallas_call | solution.py:180
  155.8 6.0 %backward_step.3 = f32[2048,256]{1,0:T(8,128)S(1)} custom-call(s32[6]{0:T(128)S(1)} %stack.47.ids_ref, bf16[1024,256]{1,0:T(8,128)(2,1)S(1)} %get-tuple-element.11.mine_ref, bf16[1024,256]{1,0:T(8,128)(2,1)S(1)} %collective-permute-done.16.other_ref, bf16[8192,2048]{1,0:T(8,128)(2,1)} %unpack_tiles.1.refs_2_.refs_3_.refs_4_.refs_5_.refs_6_.refs_7_.b_mine.b_other, ...), custom_call_target="tpu_custom_call" | custom-call | flops 2147483648 | bytes 10485760 | tf_op jit(solution)/shard_map/backward_step/pallas_call | solution.py:180
  167.7 5.2 %collective-permute-done.18 = bf16[512,256]{1,0:T(8,128)(2,1)S(1)} collective-permute-done((bf16[512,256]{1,0:T(8,128)(2,1)S(1)}, bf16[512,256]{1,0:T(8,128)(2,1)S(1)}, u32[]{:S(2)}, u32[]{:S(2)}) %collective-permute-start.18) | collective-permute-done | bytes 262176 | tf_op jit(solution)/shard_map/ppermute | solution.py:291
  173.3 2.3 %collective-permute-start.22 = (bf16[512,256]{1,0:T(8,128)(2,1)S(1)}, bf16[512,256]{1,0:T(8,128)(2,1)S(1)}, u32[]{:S(2)}, u32[]{:S(2)}) collective-permute-start(bf16[512,256]{1,0:T(8,128)(2,1)S(1)} %get-tuple-element.22), channel_id=1, source_target_pairs={{4,0},{8,4},{12,8},{14,12},{10,14},{6,10},{2,6},{0,2},{5,1},{9,5},... | collective-permute-start | bytes 786440 | tf_op jit(solution)/shard_map/ppermute | solution.py:294
  177.7 2.4 %collective-permute-done.19 = bf16[512,256]{1,0:T(8,128)(2,1)S(1)} collective-permute-done((bf16[512,256]{1,0:T(8,128)(2,1)S(1)}, bf16[512,256]{1,0:T(8,128)(2,1)S(1)}, u32[]{:S(2)}, u32[]{:S(2)}) %collective-permute-start.19) | collective-permute-done | bytes 262176 | tf_op jit(solution)/shard_map/ppermute | solution.py:291
  180.1 4.3 %collective-permute-done.25 = bf16[512,256]{1,0:T(8,128)(2,1)S(1)} collective-permute-done((bf16[512,256]{1,0:T(8,128)(2,1)S(1)}, bf16[512,256]{1,0:T(8,128)(2,1)S(1)}, u32[]{:S(2)}, u32[]{:S(2)}) %collective-permute-start.25) | collective-permute-done | bytes 262176 | tf_op jit(solution)/shard_map/ppermute | solution.py:293
  184.7 2.1 %collective-permute-start.23 = (bf16[512,256]{1,0:T(8,128)(2,1)S(1)}, bf16[512,256]{1,0:T(8,128)(2,1)S(1)}, u32[]{:S(2)}, u32[]{:S(2)}) collective-permute-start(bf16[512,256]{1,0:T(8,128)(2,1)S(1)} %get-tuple-element.18), channel_id=1, source_target_pairs={{4,0},{8,4},{12,8},{14,12},{10,14},{6,10},{2,6},{0,2},{5,1},{9,5},... | collective-permute-start | bytes 786440 | tf_op jit(solution)/shard_map/ppermute | solution.py:294
  188.9 3.6 %backward_own.1 = f32[1024,256]{1,0:T(8,128)S(1)} custom-call(s32[4]{0:T(128)S(1)} %get-tuple-element.49.ids_ref, bf16[1024,256]{1,0:T(8,128)(2,1)S(1)} %get-tuple-element.11.mine_ref, bf16[1024,256]{1,0:T(8,128)(2,1)S(1)} %collective-permute-done.16.other_ref, bf16[8192,2048]{1,0:T(8,128)(2,1)} %unpack_tiles.1.refs_2_.refs_3_.refs_4_.refs_5_.refs_6_.refs_7_.b_mine.b_other, ...), custom_call_target="tpu_custom_call" | custom-call | flops 1073741824 | bytes 5242880 | tf_op jit(solution)/shard_map/backward_own/pallas_call | solution.py:180
  (149 shorter events, 50.8 us)
Async XLA Ops:
  1.7 60.2 %collective-permute-start = (bf16[512,256]{1,0:T(8,128)(2,1)S(1)}, bf16[512,256]{1,0:T(8,128)(2,1)S(1)}, u32[]{:S(2)}, u32[]{:S(2)}) collective-permute-start(bf16[512,256]{1,0:T(8,128)(2,1)S(1)} %get-tuple-element.34.refs_0_), channel_id=1, source_target_pairs={{0,4},{4,8},{8,12},{12,14},{14,10},{10,6},{6,2},{2,0},{1,5},{5,9},... | collective-permute-start | bytes 786440 | tf_op jit(solution)/shard_map/ppermute | solution.py:234
  4.8 59.3 %collective-permute-start.11 = (bf16[512,256]{1,0:T(8,128)(2,1)S(1)}, bf16[512,256]{1,0:T(8,128)(2,1)S(1)}, u32[]{:S(2)}, u32[]{:S(2)}) collective-permute-start(bf16[512,256]{1,0:T(8,128)(2,1)S(1)} %get-tuple-element.34.refs_0_), channel_id=1, source_target_pairs={{4,0},{8,4},{12,8},{14,12},{10,14},{6,10},{2,6},{0,2},{5,1},{9,5},... | collective-permute-start | bytes 786440 | tf_op jit(solution)/shard_map/ppermute | solution.py:237
  4.8 59.1 %collective-permute-start.4 = (bf16[512,256]{1,0:T(8,128)(2,1)S(1)}, bf16[512,256]{1,0:T(8,128)(2,1)S(1)}, u32[]{:S(2)}, u32[]{:S(2)}) collective-permute-start(bf16[512,256]{1,0:T(8,128)(2,1)S(1)} %get-tuple-element.33.refs_1_), channel_id=1, source_target_pairs={{4,0},{8,4},{12,8},{14,12},{10,14},{6,10},{2,6},{0,2},{5,1},{9,5},... | collective-permute-start | bytes 786440 | tf_op jit(solution)/shard_map/ppermute | solution.py:235
  6.7 59.2 %collective-permute-start.8 = (bf16[512,256]{1,0:T(8,128)(2,1)S(1)}, bf16[512,256]{1,0:T(8,128)(2,1)S(1)}, u32[]{:S(2)}, u32[]{:S(2)}) collective-permute-start(bf16[512,256]{1,0:T(8,128)(2,1)S(1)} %get-tuple-element.33.refs_1_), channel_id=1, source_target_pairs={{0,4},{4,8},{8,12},{12,14},{14,10},{10,6},{6,2},{2,0},{1,5},{5,9},... | collective-permute-start | bytes 786440 | tf_op jit(solution)/shard_map/ppermute | solution.py:236
  61.9 9.2 %collective-permute-start.1 = (bf16[512,256]{1,0:T(8,128)(2,1)S(1)}, bf16[512,256]{1,0:T(8,128)(2,1)S(1)}, u32[]{:S(2)}, u32[]{:S(2)}) collective-permute-start(bf16[512,256]{1,0:T(8,128)(2,1)S(1)} %collective-permute-done.refs_0_), channel_id=1, source_target_pairs={{0,4},{4,8},{8,12},{12,14},{14,10},{10,6},{6,2},{2,0},{1,5},{5,9},... | collective-permute-start | bytes 786440 | tf_op jit(solution)/shard_map/ppermute | solution.py:234
  63.9 9.2 %collective-permute-start.5 = (bf16[512,256]{1,0:T(8,128)(2,1)S(1)}, bf16[512,256]{1,0:T(8,128)(2,1)S(1)}, u32[]{:S(2)}, u32[]{:S(2)}) collective-permute-start(bf16[512,256]{1,0:T(8,128)(2,1)S(1)} %collective-permute-done.4.refs_1_), channel_id=1, source_target_pairs={{4,0},{8,4},{12,8},{14,12},{10,14},{6,10},{2,6},{0,2},{5,1},{9,5},... | collective-permute-start | bytes 786440 | tf_op jit(solution)/shard_map/ppermute | solution.py:235
  64.0 15.9 %collective-permute-start.12 = (bf16[512,256]{1,0:T(8,128)(2,1)S(1)}, bf16[512,256]{1,0:T(8,128)(2,1)S(1)}, u32[]{:S(2)}, u32[]{:S(2)}) collective-permute-start(bf16[512,256]{1,0:T(8,128)(2,1)S(1)} %collective-permute-done.11.refs_3_), channel_id=1, source_target_pairs={{4,0},{8,4},{12,8},{14,12},{10,14},{6,10},{2,6},{0,2},{5,1},{9,5},... | collective-permute-start | bytes 786440 | tf_op jit(solution)/shard_map/ppermute | solution.py:237
  66.0 11.9 %collective-permute-start.9 = (bf16[512,256]{1,0:T(8,128)(2,1)S(1)}, bf16[512,256]{1,0:T(8,128)(2,1)S(1)}, u32[]{:S(2)}, u32[]{:S(2)}) collective-permute-start(bf16[512,256]{1,0:T(8,128)(2,1)S(1)} %collective-permute-done.8.refs_2_), channel_id=1, source_target_pairs={{0,4},{4,8},{8,12},{12,14},{14,10},{10,6},{6,2},{2,0},{1,5},{5,9},... | collective-permute-start | bytes 786440 | tf_op jit(solution)/shard_map/ppermute | solution.py:236
  71.2 15.4 %collective-permute-start.2 = (bf16[512,256]{1,0:T(8,128)(2,1)S(1)}, bf16[512,256]{1,0:T(8,128)(2,1)S(1)}, u32[]{:S(2)}, u32[]{:S(2)}) collective-permute-start(bf16[512,256]{1,0:T(8,128)(2,1)S(1)} %collective-permute-done.1.refs_0_), channel_id=1, source_target_pairs={{0,4},{4,8},{8,12},{12,14},{14,10},{10,6},{6,2},{2,0},{1,5},{5,9},... | collective-permute-start | bytes 786440 | tf_op jit(solution)/shard_map/ppermute | solution.py:234
  73.2 15.4 %collective-permute-start.6 = (bf16[512,256]{1,0:T(8,128)(2,1)S(1)}, bf16[512,256]{1,0:T(8,128)(2,1)S(1)}, u32[]{:S(2)}, u32[]{:S(2)}) collective-permute-start(bf16[512,256]{1,0:T(8,128)(2,1)S(1)} %collective-permute-done.5.refs_1_), channel_id=1, source_target_pairs={{4,0},{8,4},{12,8},{14,12},{10,14},{6,10},{2,6},{0,2},{5,1},{9,5},... | collective-permute-start | bytes 786440 | tf_op jit(solution)/shard_map/ppermute | solution.py:235
  77.9 17.2 %collective-permute-start.10 = (bf16[512,256]{1,0:T(8,128)(2,1)S(1)}, bf16[512,256]{1,0:T(8,128)(2,1)S(1)}, u32[]{:S(2)}, u32[]{:S(2)}) collective-permute-start(bf16[512,256]{1,0:T(8,128)(2,1)S(1)} %collective-permute-done.9.refs_2_), channel_id=1, source_target_pairs={{0,4},{4,8},{8,12},{12,14},{14,10},{10,6},{6,2},{2,0},{1,5},{5,9},... | collective-permute-start | bytes 786440 | tf_op jit(solution)/shard_map/ppermute | solution.py:236
  80.0 15.2 %collective-permute-start.13 = (bf16[512,256]{1,0:T(8,128)(2,1)S(1)}, bf16[512,256]{1,0:T(8,128)(2,1)S(1)}, u32[]{:S(2)}, u32[]{:S(2)}) collective-permute-start(bf16[512,256]{1,0:T(8,128)(2,1)S(1)} %collective-permute-done.12.refs_3_), channel_id=1, source_target_pairs={{4,0},{8,4},{12,8},{14,12},{10,14},{6,10},{2,6},{0,2},{5,1},{9,5},... | collective-permute-start | bytes 786440 | tf_op jit(solution)/shard_map/ppermute | solution.py:237
  86.5 15.2 %collective-permute-start.3 = (bf16[512,256]{1,0:T(8,128)(2,1)S(1)}, bf16[512,256]{1,0:T(8,128)(2,1)S(1)}, u32[]{:S(2)}, u32[]{:S(2)}) collective-permute-start(bf16[512,256]{1,0:T(8,128)(2,1)S(1)} %collective-permute-done.2.refs_0_), channel_id=1, source_target_pairs={{0,4},{4,8},{8,12},{12,14},{14,10},{10,6},{6,2},{2,0},{1,5},{5,9},... | collective-permute-start | bytes 786440 | tf_op jit(solution)/shard_map/ppermute | solution.py:240
  88.6 13.1 %collective-permute-start.7 = (bf16[512,256]{1,0:T(8,128)(2,1)S(1)}, bf16[512,256]{1,0:T(8,128)(2,1)S(1)}, u32[]{:S(2)}, u32[]{:S(2)}) collective-permute-start(bf16[512,256]{1,0:T(8,128)(2,1)S(1)} %collective-permute-done.6.refs_1_), channel_id=1, source_target_pairs={{4,0},{8,4},{12,8},{14,12},{10,14},{6,10},{2,6},{0,2},{5,1},{9,5},... | collective-permute-start | bytes 786440 | tf_op jit(solution)/shard_map/ppermute | solution.py:241
  132.2 29.6 %collective-permute-start.35 = (f32[32,256]{1,0:T(8,128)S(1)}, f32[32,256]{1,0:T(8,128)S(1)}, u32[]{:S(2)}, u32[]{:S(2)}) collective-permute-start(f32[32,256]{1,0:T(8,128)S(1)} %slice_add_fusion.14), channel_id=1, source_target_pairs={{0,8},{2,10},{4,12},{6,14},{8,0},{10,2},{12,4},{14,6},{1,9},{3,11}... | collective-permute-start | bytes 98312 | tf_op jit(solution)/shard_map/ppermute | solution.py:338
  139.4 24.3 %collective-permute-start.17 = (bf16[512,256]{1,0:T(8,128)(2,1)S(1)}, bf16[512,256]{1,0:T(8,128)(2,1)S(1)}, u32[]{:S(2)}, u32[]{:S(2)}) collective-permute-start(bf16[512,256]{1,0:T(8,128)(2,1)S(1)} %get-tuple-element.31), channel_id=1, source_target_pairs={{0,4},{4,8},{8,12},{12,14},{14,10},{10,6},{6,2},{2,0},{1,5},{5,9},... | collective-permute-start | bytes 786440 | tf_op jit(solution)/shard_map/ppermute | solution.py:278
  141.3 22.4 %collective-permute-start.27 = (bf16[512,256]{1,0:T(8,128)(2,1)S(1)}, bf16[512,256]{1,0:T(8,128)(2,1)S(1)}, u32[]{:S(2)}, u32[]{:S(2)}) collective-permute-start(bf16[512,256]{1,0:T(8,128)(2,1)S(1)} %get-tuple-element.32), channel_id=1, source_target_pairs={{4,0},{8,4},{12,8},{14,12},{10,14},{6,10},{2,6},{0,2},{5,1},{9,5},... | collective-permute-start | bytes 786440 | tf_op jit(solution)/shard_map/ppermute | solution.py:279
  147.6 20.1 %collective-permute-start.21 = (bf16[512,256]{1,0:T(8,128)(2,1)S(1)}, bf16[512,256]{1,0:T(8,128)(2,1)S(1)}, u32[]{:S(2)}, u32[]{:S(2)}) collective-permute-start(bf16[512,256]{1,0:T(8,128)(2,1)S(1)} %get-tuple-element.27), channel_id=1, source_target_pairs={{4,0},{8,4},{12,8},{14,12},{10,14},{6,10},{2,6},{0,2},{5,1},{9,5},... | collective-permute-start | bytes 786440 | tf_op jit(solution)/shard_map/ppermute | solution.py:294
  149.2 18.5 %collective-permute-start.24 = (bf16[512,256]{1,0:T(8,128)(2,1)S(1)}, bf16[512,256]{1,0:T(8,128)(2,1)S(1)}, u32[]{:S(2)}, u32[]{:S(2)}) collective-permute-start(bf16[512,256]{1,0:T(8,128)(2,1)S(1)} %get-tuple-element.28), channel_id=1, source_target_pairs={{0,4},{4,8},{8,12},{12,14},{14,10},{10,6},{6,2},{2,0},{1,5},{5,9},... | collective-permute-start | bytes 786440 | tf_op jit(solution)/shard_map/ppermute | solution.py:293
  163.8 9.0 %collective-permute-start.18 = (bf16[512,256]{1,0:T(8,128)(2,1)S(1)}, bf16[512,256]{1,0:T(8,128)(2,1)S(1)}, u32[]{:S(2)}, u32[]{:S(2)}) collective-permute-start(bf16[512,256]{1,0:T(8,128)(2,1)S(1)} %get-tuple-element.23), channel_id=1, source_target_pairs={{0,4},{4,8},{8,12},{12,14},{14,10},{10,6},{6,2},{2,0},{1,5},{5,9},... | collective-permute-start | bytes 786440 | tf_op jit(solution)/shard_map/ppermute | solution.py:291
  166.2 11.3 %collective-permute-start.37 = (f32[128,256]{1,0:T(8,128)S(1)}, f32[128,256]{1,0:T(8,128)S(1)}, u32[]{:S(2)}, u32[]{:S(2)}) collective-permute-start(f32[128,256]{1,0:T(8,128)S(1)} %pad_maximum_fusion.3), channel_id=1, source_target_pairs={{0,2},{2,0},{4,6},{6,4},{8,10},{10,8},{12,14},{14,12},{1,3},{3,1},... | collective-permute-start | bytes 393224 | tf_op jit(solution)/shard_map/ppermute | solution.py:338
  175.5 8.9 %collective-permute-start.25 = (bf16[512,256]{1,0:T(8,128)(2,1)S(1)}, bf16[512,256]{1,0:T(8,128)(2,1)S(1)}, u32[]{:S(2)}, u32[]{:S(2)}) collective-permute-start(bf16[512,256]{1,0:T(8,128)(2,1)S(1)} %get-tuple-element.21), channel_id=1, source_target_pairs={{0,4},{4,8},{8,12},{12,14},{14,10},{10,6},{6,2},{2,0},{1,5},{5,9},... | collective-permute-start | bytes 786440 | tf_op jit(solution)/shard_map/ppermute | solution.py:293
  175.5 8.9 %collective-permute-start.29 = (bf16[512,256]{1,0:T(8,128)(2,1)S(1)}, bf16[512,256]{1,0:T(8,128)(2,1)S(1)}, u32[]{:S(2)}, u32[]{:S(2)}) collective-permute-start(bf16[512,256]{1,0:T(8,128)(2,1)S(1)} %get-tuple-element.20), channel_id=1, source_target_pairs={{4,0},{8,4},{12,8},{14,12},{10,14},{6,10},{2,6},{0,2},{5,1},{9,5},... | collective-permute-start | bytes 786440 | tf_op jit(solution)/shard_map/ppermute | solution.py:292
  177.6 15.0 %collective-permute-start.38 = (f32[256,256]{1,0:T(8,128)S(1)}, f32[256,256]{1,0:T(8,128)S(1)}, u32[]{:S(2)}, u32[]{:S(2)}) collective-permute-start(f32[256,256]{1,0:T(8,128)S(1)} %maximum_multiply_fusion), channel_id=1, source_target_pairs={{0,1},{1,0},{2,3},{3,2},{4,5},{5,4},{6,7},{7,6},{8,9},{9,8},{10,11... | collective-permute-start | bytes 786440 | tf_op jit(solution)/shard_map/ppermute | solution.py:343
  (26 other events, 169.5 us)

commit v2 on v0

v2 whole, which is shorter than its diff:
```python
from functools import partial
import math

import jax
import jax.numpy as jnp
from jax import lax
from jax.experimental import pallas as pl
from jax.experimental.pallas import tpu as pltpu
from jax.sharding import PartitionSpec as P

VMEM_LIMIT = 14 * 1024 * 1024
BRIEF = pl.CostEstimate(flops=1024, bytes_accessed=1024, transcendentals=0)
GELU_C = math.sqrt(2.0 / math.pi)
F32 = jnp.float32
BF16 = jnp.bfloat16


def ring_order(n):
    return list(range(0, n, 2)) + list(range(n - 1, 0, -2))


def unpack_tile(masks_ref, slot, test):
    words = masks_ref[jnp.maximum(slot, 0)]
    words = jnp.where(slot >= 0, words, 0)
    one, zero = jnp.ones((), BF16), jnp.zeros((), BF16)
    parts = []
    for k in range(8):
        row = jnp.broadcast_to(words[k : k + 1, :], (16, 128)).astype(jnp.int16)
        parts.append(jnp.where(jnp.bitwise_and(row, test) != 0, one, zero))
    return jnp.concatenate(parts, axis=0)


def bit_tests():
    return jnp.left_shift(jnp.ones((), jnp.int16), lax.broadcasted_iota(jnp.int16, (16, 128), 0))


def fill_tiles(table_ref, masks_ref, block_rows, first_col, cols, row_of, tiles, dst):
    test = bit_tests()

    def one_column(c, carry):
        base = (first_col + c) * block_rows
        start = pl.multiple_of(c * 128, 128)
        for r in range(tiles):
            tile = unpack_tile(masks_ref, table_ref[base + row_of(r)], test)
            dst[pl.ds(start, 128), 128 * r : 128 * r + 128] = tile
        return carry

    lax.fori_loop(0, cols, one_column, 0)


def vmem_spec():
    return pl.BlockSpec(memory_space=pltpu.VMEM)


def smem_spec():
    return pl.BlockSpec(memory_space=pltpu.SMEM)


def forward_kernel(cols, side_at, block_rows, tblk, has_acc, ids_ref, table_ref, masks_ref, *refs):
    count = len(cols)
    xs = refs[:count]
    acc_ref = refs[count] if has_acc else None
    out_ref, turned, tiles = refs[count + int(has_acc) :]
    rows = xs[0].shape[0]
    for k in range(count):
        turned[:, k * rows : (k + 1) * rows] = xs[k][...].T
    first = ids_ref[side_at] * out_ref.shape[1] if side_at is not None else 0

    def block(q, carry):
        start = pl.multiple_of(q * tblk, tblk)
        begin = first + start
        first_row = begin // 128
        for k in range(count):
            at, extra = cols[k]
            fill_tiles(
                table_ref, masks_ref, block_rows, ids_ref[at] + extra, rows // 128,
                lambda r: first_row + r, tblk // 128, tiles.at[pl.ds(k * rows, rows)],
            )
        total = jnp.dot(turned[...], tiles[...], preferred_element_type=F32)
        if has_acc:
            total = total + acc_ref[:, pl.ds(pl.multiple_of(begin, tblk), tblk)]
        out_ref[:, pl.ds(start, tblk)] = total.astype(out_ref.dtype)
        return carry

    lax.fori_loop(0, out_ref.shape[1] // tblk, block, 0)


def forward_mm(pieces, cols, side_at, ids, table, masks, acc, out_rows, tblk, block_rows, out_dtype, name):
    rows, width = pieces[0].shape
    count = len(pieces)
    args = [ids, table, masks] + list(pieces) + ([] if acc is None else [acc])
    return pl.pallas_call(
        partial(forward_kernel, tuple(cols), side_at, block_rows, tblk, acc is not None),
        in_specs=[smem_spec(), smem_spec()] + [vmem_spec()] * (len(args) - 2),
        out_specs=vmem_spec(),
        scratch_shapes=[
            pltpu.VMEM((width, count * rows), BF16),
            pltpu.VMEM((count * rows, tblk), BF16),
        ],
        out_shape=jax.ShapeDtypeStruct((width, out_rows), out_dtype),
        compiler_params=pltpu.CompilerParams(vmem_limit_bytes=VMEM_LIMIT),
        cost_estimate=BRIEF,
        name=name,
    )(*args)


def shard_kernel(at, block_rows, ids_ref, table_ref, masks_ref, out_ref):
    fill_tiles(
        table_ref, masks_ref, block_rows, ids_ref[at], out_ref.shape[0] // 128,
        lambda r: r, block_rows, out_ref,
    )


def shard_tiles(at, node_rows, ids, table, masks, block_rows):
    return pl.pallas_call(
        partial(shard_kernel, at, block_rows),
        in_specs=[smem_spec(), smem_spec(), vmem_spec()],
        out_specs=vmem_spec(),
        out_shape=jax.ShapeDtypeStruct((node_rows, block_rows * 128), BF16),
        compiler_params=pltpu.CompilerParams(vmem_limit_bytes=VMEM_LIMIT),
        cost_estimate=BRIEF,
        name="far_tiles",
    )(ids, table, masks)


def last_kernel(at, ids_ref, tiles_ref, low_ref, high_ref, acc_ref, out_ref, turned):
    half = low_ref.shape[0]
    turned[:, :half] = low_ref[...].T
    turned[:, half:] = high_ref[...].T
    rows = out_ref.shape[1]
    columns = pl.ds(pl.multiple_of(ids_ref[at] * rows, rows), rows)
    total = jnp.dot(turned[...], tiles_ref[:, columns], preferred_element_type=F32)
    out_ref[...] = (total + acc_ref[:, columns]).astype(out_ref.dtype)


def last_forward(pieces, at, ids, tiles, acc, out_dtype, name):
    half, width = pieces[0].shape
    rows = acc.shape[1] // 2
    return pl.pallas_call(
        partial(last_kernel, at),
        in_specs=[smem_spec()] + [vmem_spec()] * 4,
        out_specs=vmem_spec(),
        out_shape=jax.ShapeDtypeStruct((width, rows), out_dtype),
        scratch_shapes=[pltpu.VMEM((width, 2 * half), BF16)],
        compiler_params=pltpu.CompilerParams(vmem_limit_bytes=VMEM_LIMIT),
        cost_estimate=BRIEF,
        name=name,
    )(ids, tiles, *pieces, acc)


def first_kernel(at, has_acc, ids_ref, tiles_ref, grad_ref, *refs):
    out_ref = refs[-1]
    rows = grad_ref.shape[0]
    columns = pl.ds(pl.multiple_of(ids_ref[at] * rows, rows), rows)
    total = jnp.dot(tiles_ref[:, columns], grad_ref[...], preferred_element_type=F32)
    if has_acc:
        total = total + refs[0][...]
    out_ref[...] = total.astype(out_ref.dtype)


def first_backward(grad, at, ids, tiles, acc, out_dtype, name):
    rows, width = grad.shape
    args = [ids, tiles, grad] + ([] if acc is None else [acc])
    return pl.pallas_call(
        partial(first_kernel, at, acc is not None),
        in_specs=[smem_spec()] + [vmem_spec()] * (len(args) - 1),
        out_specs=vmem_spec(),
        out_shape=jax.ShapeDtypeStruct((tiles.shape[0], width), out_dtype),
        compiler_params=pltpu.CompilerParams(vmem_limit_bytes=VMEM_LIMIT),
        cost_estimate=BRIEF,
        name=name,
    )(*args)


def middle_kernel(
    agg_ref, other_ref, div_ref, own_ref, og_ref, wn_ref,
    mean_ref, out_ref, gb_ref, mg_ref, bias_ref,
):
    div = div_ref[...]
    rows = div.shape[1]
    width = own_ref.shape[1]
    mean = ((agg_ref[...] + other_ref[...].astype(F32)) / div).T.astype(BF16)
    mean_ref[...] = mean
    pre = own_ref[...] + jnp.dot(mean, wn_ref[...], preferred_element_type=F32)
    square = pre * pre
    bent = jnp.tanh(GELU_C * (pre + 0.044715 * (square * pre)))
    half = 0.5 * (1.0 + bent)
    out_ref[...] = (pre * half).astype(BF16)
    slope = half + 0.5 * pre * (1.0 - bent * bent) * (GELU_C * (1.0 + 3.0 * 0.044715 * square))
    pre_grad = og_ref[...] * slope
    grad_b = pre_grad.astype(BF16)
    gb_ref[...] = grad_b
    div_column = jnp.broadcast_to(div, (128, rows)).T
    div_full = jnp.concatenate([div_column] * (width // 128), axis=1)
    mean_grad = lax.dot_general(
        grad_b, wn_ref[...], (((1,), (1,)), ((), ())), preferred_element_type=F32
    )
    mg_ref[...] = (mean_grad / div_full).astype(BF16)
    part = jnp.sum(pre_grad.reshape(rows // 32, 32, width), axis=0)

    @pl.when(pl.program_id(0) == 0)
    def _():
        bias_ref[...] = part

    @pl.when(pl.program_id(0) != 0)
    def _():
        bias_ref[...] += part


def middle(agg, other, divisor, own, og, wn):
    rows, width = own.shape
    blk = 256
    turned = pl.BlockSpec((width, blk), lambda i: (0, i))
    plain = pl.BlockSpec((blk, width), lambda i: (i, 0))
    weight = pl.BlockSpec((width, width), lambda i: (0, 0))
    act = jax.ShapeDtypeStruct((rows, width), BF16)
    return pl.pallas_call(
        middle_kernel,
        grid=(rows // blk,),
        in_specs=[
            turned, turned, pl.BlockSpec((1, blk), lambda i: (0, i)), plain, plain, weight,
        ],
        out_specs=[plain] * 4 + [pl.BlockSpec((32, width), lambda i: (0, 0))],
        out_shape=[act] * 4 + [jax.ShapeDtypeStruct((32, width), F32)],
        compiler_params=pltpu.CompilerParams(vmem_limit_bytes=VMEM_LIMIT),
        cost_estimate=BRIEF,
        name="layer",
    )(agg, other, divisor, own, og, wn)


def backward_kernel(cols, sides, block_rows, has_acc, ids_ref, table_ref, masks_ref, after_ref, *refs):
    del after_ref
    grads = refs[: len(sides)]
    acc_ref = refs[len(sides)] if has_acc else None
    out_ref, tiles = refs[len(sides) + int(has_acc) :]
    piece_rows = out_ref.shape[0]
    rows = grads[0].shape[0]
    per_side = rows // 128
    first_col = ids_ref[cols[0]]
    for p in range(1, len(cols)):
        first_col = jnp.where(pl.program_id(0) == p, ids_ref[cols[p]], first_col)
    for k, side_at in enumerate(sides):
        base = ids_ref[side_at] * per_side
        fill_tiles(
            table_ref, masks_ref, block_rows, first_col, piece_rows // 128,
            lambda r: base + r, per_side, tiles.at[:, pl.ds(k * rows, rows)],
        )
    total = None
    for k in range(len(sides)):
        term = jnp.dot(
            tiles[:, k * rows : (k + 1) * rows], grads[k][...], preferred_element_type=F32
        )
        total = term if total is None else total + term
    if has_acc:
        total = total + acc_ref[...].astype(F32)
    out_ref[...] = total.astype(out_ref.dtype)


def backward_mm(cols, grads, sides, after, ids, table, masks, acc, piece_rows, block_rows, out_dtype, name):
    rows, width = grads[0].shape
    args = [ids, table, masks, after] + list(grads) + ([] if acc is None else [acc])
    piece = pl.BlockSpec((piece_rows, width), lambda p: (p, 0))
    return pl.pallas_call(
        partial(backward_kernel, tuple(cols), tuple(sides), block_rows, acc is not None),
        grid=(len(cols),),
        in_specs=[smem_spec(), smem_spec(), vmem_spec(), pl.BlockSpec(memory_space=pl.ANY)]
        + [vmem_spec()] * len(grads)
        + ([] if acc is None else [piece]),
        out_specs=piece,
        scratch_shapes=[pltpu.VMEM((piece_rows, len(grads) * rows), BF16)],
        out_shape=jax.ShapeDtypeStruct((len(cols) * piece_rows, width), out_dtype),
        compiler_params=pltpu.CompilerParams(vmem_limit_bytes=VMEM_LIMIT),
        cost_estimate=BRIEF,
        name=name,
    )(*args)


def small_call(kernel, name, out_shape, args):
    return pl.pallas_call(
        kernel,
        in_specs=[smem_spec()] + [vmem_spec()] * (len(args) - 1),
        out_specs=jax.tree.map(lambda _: vmem_spec(), out_shape),
        out_shape=out_shape,
        compiler_params=pltpu.CompilerParams(vmem_limit_bytes=VMEM_LIMIT),
        cost_estimate=BRIEF,
        name=name,
    )(*args)


def weight_kernel(at, ids_ref, x_ref, mean_ref, gb_ref, bias_ref, keep_ref, send_ref):
    width = gb_ref.shape[1]
    grad = gb_ref[...]
    own = jnp.dot(x_ref[...].T, grad, preferred_element_type=F32)
    neigh = jnp.dot(mean_ref[...].T, grad, preferred_element_type=F32)
    first = ids_ref[at] == 0
    keep_ref[:width] = jnp.where(first, own, neigh)
    send_ref[:width] = jnp.where(first, neigh, own)
    keep_ref[width:] = bias_ref[...]
    send_ref[width:] = bias_ref[...]


def split_kernel(at, ids_ref, keep_ref, got_ref, *outs):
    chunk = outs[0].shape[0]
    for x, out in enumerate(outs):
        rows = pl.ds(pl.multiple_of(ids_ref[at + x], 8), chunk)
        out[...] = keep_ref[rows] + got_ref[rows]


def join_kernel(at, scale, ids_ref, *refs):
    out = refs[-1]
    for x, part in enumerate(refs[:-1]):
        rows = pl.ds(pl.multiple_of(ids_ref[at + x], 8), part.shape[0])
        out[rows] = part[...] * scale


def local(
    node_features, tile_rows, tile_cols, tile_masks, tile_count,
    weight_self, weight_neigh, bias_term, out_grad,
):
    node_rows, width = node_features.shape
    n = lax.axis_size("row")
    grid_cols = lax.axis_size("col")
    slots = tile_masks.shape[2]
    block_rows = grid_cols * node_rows // 128
    block_cols = n * node_rows // 128
    half = node_rows // 2
    far = n // 2

    order = ring_order(n)
    clockwise = [(order[k], order[(k + 1) % n]) for k in range(n)]
    counter = [(b, a) for a, b in clockwise]
    swap = [(0, 1), (1, 0)]
    row_id = lax.axis_index("row")
    side = lax.axis_index("col").astype(jnp.int32)
    shard_cols = node_rows // 128
    at_side, at_other, at_quad = n, n + 1, n + 2
    bias_rows = 32
    chunk = (width + bias_rows) // 4
    known = [
        [order[(order.index(r) + k) % n] * shard_cols for k in range(n)]
        + [c, 1 - c]
        + [((r & 3) ^ x) * chunk for x in range(4)]
        for r in range(n)
        for c in range(grid_cols)
    ]
    ids = lax.dynamic_index_in_dim(
        jnp.array(known, jnp.int32), row_id * grid_cols + side, 0, keepdims=False
    )

    row_index = tile_rows.reshape(slots)
    col_index = tile_cols.reshape(slots)
    masks = jnp.transpose(tile_masks.reshape(slots, 128, 8), (0, 2, 1))
    slot_ids = jnp.arange(slots, dtype=jnp.int32)
    live = slot_ids < tile_count.reshape(())
    keys = jnp.where(live, col_index * block_rows + row_index, -1)
    spots = jnp.arange(block_rows * block_cols, dtype=jnp.int32)
    table = jnp.max(jnp.where(keys[None, :] == spots[:, None], slot_ids[None, :], -1), axis=1)
    counts = jnp.sum(lax.population_count(masks), axis=1).astype(BF16)
    pick = ((jnp.arange(block_rows, dtype=jnp.int32)[:, None] == row_index[None, :]) & live[None, :])
    degree = jnp.dot(pick.astype(BF16), counts, preferred_element_type=F32).reshape(2, 1, node_rows)
    sent_degree = lax.ppermute(lax.dynamic_index_in_dim(degree, 1 - side, 0, False), "col", swap)
    degree = lax.dynamic_index_in_dim(degree, side, 0, False) + sent_degree
    divisor = jnp.maximum(degree, 1.0)

    forward = partial(forward_mm, ids=ids, table=table, masks=masks, block_rows=block_rows, tblk=1024)
    row_total = block_rows * 128
    from_left = from_right = node_features
    pieces, cols, acc = [node_features], [(0, 0)], None
    early = (node_features, weight_self, bias_term, out_grad, ids, divisor)
    for s in range(1, far + 1):
        if s < far:
            next_left = lax.ppermute(from_left, "row", clockwise)
            next_right = lax.ppermute(from_right, "row", counter)
            next_cols = [(n - s, 0), (s, 0)]
        else:
            next_left = lax.ppermute(from_left[:half], "row", clockwise)
            next_right = lax.ppermute(from_right[half:], "row", counter)
        acc = forward(
            pieces, cols, None, acc=acc, out_rows=row_total, out_dtype=F32, name="forward_step"
        )
        if s == 2:
            x_now, ws_now, b_now, og_now, ids_now, div_now = early
            own_part = jnp.dot(x_now, ws_now, preferred_element_type=F32) + b_now
            far_tiles = shard_tiles(far, node_rows, ids_now, table, masks, block_rows)
            early = (own_part, og_now.astype(F32), far_tiles, div_now)
        acc, from_left, from_right, early = lax.optimization_barrier((acc, next_left, next_right, early))
        pieces, cols = [from_left, from_right], next_cols
    own_part, wide_out_grad, far_tiles, divisor = early
    for_other = last_forward(pieces, at_other, ids, far_tiles, acc, BF16, "forward_send")
    received = lax.ppermute(for_other, "col", swap)
    mine = last_forward(pieces, at_side, ids, far_tiles, acc, F32, "forward_keep")
    mine, received = lax.optimization_barrier((mine, received))

    mean, node_out, grad_b, mean_grad, bias_part = middle(
        mine, received, divisor, own_part, wide_out_grad, weight_neigh
    )
    other_grad = lax.ppermute(mean_grad, "col", swap)

    backward = partial(
        backward_mm, ids=ids, table=table, masks=masks, piece_rows=node_rows, block_rows=block_rows
    )
    far_terms = first_backward(mean_grad, at_side, ids, far_tiles, None, F32, "backward_far_own")
    far_terms = first_backward(other_grad, at_other, ids, far_tiles, far_terms, BF16, "backward_far")
    both_grads, both_sides = [mean_grad, other_grad], [at_side, at_other]

    grad_scale = (node_rows * n * grid_cols) ** (-0.5)
    bits = int(math.log2(n))

    matrix_shape = jax.ShapeDtypeStruct((4 * chunk, width), F32)

    def quad_perm(x):
        return [(r, r ^ x) for r in range(n)]

    def to_core(parts):
        keep, send = small_call(
            partial(weight_kernel, at_side), "weight_grads", [matrix_shape] * 2, (ids,) + parts
        )
        return keep, lax.ppermute(send, "col", swap)

    def to_quad(parts):
        quarter = jax.ShapeDtypeStruct((chunk, width), F32)
        parts = small_call(partial(split_kernel, at_quad), "split_grads", [quarter] * 4, (ids,) + parts)
        return [parts[0]] + [lax.ppermute(parts[x], "row", quad_perm(x)) for x in (1, 2, 3)]

    def add_all(b, parts):
        quarter = sum(parts[1:], parts[0])
        return [quarter, lax.ppermute(quarter, "row", [(r, r ^ (1 << b)) for r in range(n)])]

    def from_quad(parts):
        quarter = sum(parts[1:], parts[0])
        return [quarter] + [lax.ppermute(quarter, "row", quad_perm(x)) for x in (1, 2, 3)]

    spread = [[] for _ in range(far)]
    spread[0].append(to_core)
    spread[1].append(to_quad)
    for b in range(2, bits):
        spread[b].append(partial(add_all, b))
    spread[far - 1].append(from_quad)

    weights = (node_features, mean, grad_b, bias_part)
    right, left = far_terms[:half], far_terms[half:]
    for s in range(far - 1, -1, -1):
        right, left, grads = lax.optimization_barrier((right, left, both_grads))
        right = lax.ppermute(right, "row", clockwise)
        left = lax.ppermute(left, "row", counter)
        if s > 0:
            terms = backward(
                [s, n - s], grads, both_sides, grads[0], acc=None, out_dtype=BF16, name="backward_step"
            )
        else:
            terms = backward(
                [0], grads, both_sides, grads[0], acc=None, out_dtype=F32, name="backward_own"
            )
            self_term = lax.dot_general(
                grad_b, weight_self, (((1,), (1,)), ((), ())), preferred_element_type=F32
            )
            terms = terms + self_term
        terms, weights = lax.optimization_barrier((terms, weights))
        for one in spread[far - 1 - s]:
            weights = one(weights)
        terms, right, left, both_grads = lax.optimization_barrier((terms, right, left, grads))
        if s > 0:
            if s == far - 1:
                gap = jnp.zeros((half, width), BF16)
                right = jnp.concatenate([right, gap], axis=0)
                left = jnp.concatenate([gap, left], axis=0)
            right = (terms[:node_rows].astype(F32) + right.astype(F32)).astype(BF16)
            left = (terms[node_rows:].astype(F32) + left.astype(F32)).astype(BF16)
        else:
            feature_grad = (terms + right.astype(F32) + left.astype(F32)).astype(BF16)

    matrix = small_call(
        partial(join_kernel, at_quad, grad_scale), "join_grads", matrix_shape, (ids,) + tuple(weights)
    )
    got = lax.ppermute(matrix[:width], "col", swap)
    grad_self = jnp.where(side == 0, matrix[:width], got)
    grad_neigh = jnp.where(side == 0, got, matrix[:width])
    grad_bias = jnp.sum(matrix[width:], axis=0)
    return node_out, feature_grad, grad_self, grad_neigh, grad_bias


def solution(mesh):
    in_specs = (
        P(("groups", "row", "col"), None),
        P(("groups", "row"), "col", None),
        P(("groups", "row"), "col", None),
        P(("groups", "row"), "col", None, None, None),
        P(("groups", "row"), "col"),
        P(),
        P(),
        P(),
        P(("groups", "row", "col"), None),
    )
    out_specs = (
        P(("groups", "row", "col"), None),
        P(("groups", "row", "col"), None),
        P("groups", None),
        P("groups", None),
        P("groups"),
    )
    return jax.shard_map(local, mesh=mesh, in_specs=in_specs, out_specs=out_specs, check_vma=False)
```

time: 502 us -> 122 us (0.24)
  waiting for transfers between devices: 200 us -> 26.9 us
  matrix products: 153 us -> 0.77 us
  local copies, waits for them, and re-layouts: 58.5 us -> 5.76 us
  Pallas kernels: 0 us -> 51.8 us
  blocking collectives: 38.4 us -> 0 us
  other arithmetic: 35 us -> 7.99 us
  starting transfers between devices: 0.2 us -> 27.2 us
  between operations: 14.6 us -> 1.68 us
    dot_general x60 -> x3, matrix products: 153 us -> 0.77 us  [the longest x1 0.33 us: local(): lax.dot_general(grad_b, weight_self, (((1,), (1,)), ((), ())), preferred_...]
    reduce_scatter x2 -> x0, waiting for transfers between devices: 115 us -> none  [the longest x1 111 us: local(): lax.psum_scatter(column_totals.reshape(block_cols * 128, width), 'row', s...]
    all_gather x2 -> x0, waiting for transfers between devices: 85 us -> none  [the longest x1 76.9 us: local(): gathered = lax.all_gather(node_features, 'row', axis=0, tiled=True)]
    pallas_call x0 -> x17, Pallas kernels: none -> 51.8 us  [the longest x4 20.6 us: forward_mm(): pl.pallas_call(partial(forward_kernel, tuple(cols), side_at, block_rows,...]
    psum x1 -> x0, blocking collectives: 35.9 us -> none  [local(): lax.psum((local_self, local_neigh, local_bias), ('row', 'col'))]
    while x38 -> x0, local copies, waits for them, and re-layouts: 33.4 us -> none
    ppermute x0 -> x28, starting transfers between devices: none -> 27.2 us  [the longest x3 5.09 us: local(): next_right = lax.ppermute(from_right, 'row', counter)]
    ppermute x0 -> x28, waiting for transfers between devices: none -> 26.9 us  [the longest x4 6.9 us: local(): right = lax.ppermute(right, 'row', clockwise)]
  transfers between devices with their start and end apart: 5 -> 28, of which waited for: 4 -> 19; matrix products, arithmetic and copies ran while one was open for 23% -> 7% of each run, Pallas kernels for 0% -> 38%
where the time goes in v2:
time: 122 us
  Pallas kernels  51.8 us (42%)
  starting transfers between devices  27.2 us (22%)
  waiting for transfers between devices  26.9 us (22%)
  other arithmetic  7.99 us (7%)
  local copies, waits for them, and re-layouts  5.76 us (5%)
  between operations  1.68 us (1%)
    pallas_call x4, Pallas kernels, forward_mm(): pl.pallas_call(partial(forward_kernel, tuple(cols), side_at, block_rows,...  20.6 us
    pallas_call x4, Pallas kernels, backward_mm(): pl.pallas_call(partial(backward_kernel, tuple(cols), tuple(sides), block_...  19.3 us
    ppermute x4, waiting for transfers between devices, local(): right = lax.ppermute(right, 'row', clockwise)  6.9 us
    ppermute x3, waiting for transfers between devices, local(): next_left = lax.ppermute(from_left, 'row', clockwise)  5.31 us
    ppermute x3, starting transfers between devices, local(): next_right = lax.ppermute(from_right, 'row', counter)  5.09 us
    unnamed x20, local copies, waits for them, and re-layouts  4.95 us
    ppermute x4, starting transfers between devices, local(): right = lax.ppermute(right, 'row', clockwise)  4.74 us
    ppermute x3, starting transfers between devices, from_quad(): lax.ppermute(quarter, 'row', quad_perm(x))  4.49 us
  transfers between devices with their start and end apart: 28, of which 19 were waited for; matrix products, arithmetic and copies ran while one was open for 7% of the time, Pallas kernels for 38%

profile of v2, /device:TPU:0, one launch (start us, length us, event | category | flops | bytes accessed | tf_op | source)
XLA Modules:
  0.0 122.1 jit_solution(165295744486749444)
XLA Ops:
  0.7 3.0 %collective-permute-start.1 = (bf16[1024,256]{1,0:T(8,128)(2,1)}, bf16[1024,256]{1,0:T(8,128)(2,1)S(1)}, u32[]{:S(2)}, u32[]{:S(2)}) collective-permute-start(bf16[1024,256]{1,0:T(8,128)(2,1)} %x_ref), channel_id=1, source_target_pairs={{4,0},{8,4},{12,8},{14,12},{10,14},{6,10},{2,6},{0,2},{5,1},{9,5},... | collective-permute-start | bytes 1572872 | tf_op jit(solution)/shard_map/ppermute | solution.py:373
  5.2 2.0 %popcnt_reduce_fusion = s32[384,128]{1,0:T(8,128)S(1)} fusion(s32[1,1,384,128,8]{3,4,2,1,0:T(8,128)} %param.13), kind=kLoop, calls=%fused_computation | loop fusion | flops 737280 | bytes 1769472 | tf_op jit(solution)/shard_map/reduce_sum | solution.py:358
  9.5 3.3 %forward_step.4.refs_2_ = f32[256,2048]{1,0:T(8,128)S(1)} custom-call(s32[14]{0:T(128)S(1)} %fusion.7.ids_ref, s32[1024]{0:T(1024)S(1)} %select_reduce_fusion.table_ref, s32[384,8,128]{2,1,0:T(8,128)S(1)} %bitcast.19, bf16[1024,256]{1,0:T(8,128)(2,1)S(1)} %copy-done.4), custom_call_target="tpu_custom_call" | custom-call | flops 1024 | bytes 1024 | tf_op jit(solution)/shard_map/forward_step/pallas_call | solution.py:92
  14.2 1.7 %collective-permute-done.1.refs_1_ = bf16[1024,256]{1,0:T(8,128)(2,1)S(1)} collective-permute-done((bf16[1024,256]{1,0:T(8,128)(2,1)}, bf16[1024,256]{1,0:T(8,128)(2,1)S(1)}, u32[]{:S(2)}, u32[]{:S(2)}) %collective-permute-start.1) | collective-permute-done | bytes 524320 | tf_op jit(solution)/shard_map/ppermute | solution.py:373
  20.9 5.7 %forward_step.5.refs_2_ = f32[256,2048]{1,0:T(8,128)S(1)} custom-call(s32[14]{0:T(128)S(1)} %fusion.7.ids_ref, s32[1024]{0:T(1024)S(1)} %select_reduce_fusion.table_ref, s32[384,8,128]{2,1,0:T(8,128)S(1)} %bitcast.20, bf16[1024,256]{1,0:T(8,128)(2,1)S(1)} %collective-permute-done.refs_0_, bf16[1024,256]{1,0:T(8,128)(2,1)S(1)} %collective-permute-done.1.refs_1_, ...), custom_call_target="tpu_custom_call" | custom-call | flops 1024 | bytes 1024 | tf_op jit(solution)/shard_map/forward_step/pallas_call | solution.py:92
  26.7 1.7 %far_tiles.1.tiles_ref = bf16[1024,2048]{1,0:T(8,128)(2,1)S(1)} custom-call(s32[14]{0:T(128)S(1)} %fusion.7.ids_ref, s32[1024]{0:T(1024)S(1)} %select_reduce_fusion.table_ref, s32[384,8,128]{2,1,0:T(8,128)S(1)} %bitcast.21), custom_call_target="tpu_custom_call" | custom-call | flops 1024 | bytes 1024 | tf_op jit(solution)/shard_map/far_tiles/pallas_call | solution.py:115
  32.3 5.7 %forward_step.6.refs_2_ = f32[256,2048]{1,0:T(8,128)S(1)} custom-call(s32[14]{0:T(128)S(1)} %fusion.7.ids_ref, s32[1024]{0:T(1024)S(1)} %select_reduce_fusion.table_ref, s32[384,8,128]{2,1,0:T(8,128)S(1)} %bitcast.22, bf16[1024,256]{1,0:T(8,128)(2,1)S(1)} %collective-permute-done.3.refs_0_, bf16[1024,256]{1,0:T(8,128)(2,1)S(1)} %collective-permute-done.4.refs_1_, ...), custom_call_target="tpu_custom_call" | custom-call | flops 1024 | bytes 1024 | tf_op jit(solution)/shard_map/forward_step/pallas_call | solution.py:92
  38.0 3.9 %collective-permute-done.5.refs_0_ = bf16[1024,256]{1,0:T(8,128)(2,1)S(1)} collective-permute-done((bf16[1024,256]{1,0:T(8,128)(2,1)S(1)}, bf16[1024,256]{1,0:T(8,128)(2,1)S(1)}, u32[]{:S(2)}, u32[]{:S(2)}) %collective-permute-start.5) | collective-permute-done | bytes 524320 | tf_op jit(solution)/shard_map/ppermute | solution.py:372
  43.2 1.6 %collective-permute-start.7 = (bf16[512,256]{1,0:T(8,128)(2,1)S(1)}, bf16[512,256]{1,0:T(8,128)(2,1)S(1)}, u32[]{:S(2)}, u32[]{:S(2)}) collective-permute-start(bf16[512,256]{1,0:T(8,128)(2,1)S(1)} %slice.38), channel_id=1, source_target_pairs={{0,4},{4,8},{8,12},{12,14},{14,10},{10,6},{6,2},{2,0},{1,5},{5,9},... | collective-permute-start | bytes 786440 | tf_op jit(solution)/shard_map/ppermute | solution.py:376
  45.3 5.7 %forward_step.7.acc_ref = f32[256,2048]{1,0:T(8,128)S(1)} custom-call(s32[14]{0:T(128)S(1)} %fusion.7.ids_ref, s32[1024]{0:T(1024)S(1)} %select_reduce_fusion.table_ref, s32[384,8,128]{2,1,0:T(8,128)S(1)} %bitcast.23, bf16[1024,256]{1,0:T(8,128)(2,1)S(1)} %collective-permute-done.5.refs_0_, bf16[1024,256]{1,0:T(8,128)(2,1)S(1)} %collective-permute-done.6.refs_1_, ...), custom_call_target="tpu_custom_call" | custom-call | flops 1024 | bytes 1024 | tf_op jit(solution)/shard_map/forward_step/pallas_call | solution.py:92
  54.5 3.1 %layer.1 = (bf16[1024,256]{1,0:T(8,128)(2,1)S(1)}, bf16[1024,256]{1,0:T(8,128)(2,1)}, bf16[1024,256]{1,0:T(8,128)(2,1)S(1)}, bf16[1024,256]{1,0:T(8,128)(2,1)S(1)}, f32[32,256]{1,0:T(8,128)S(1)}) custom-call(f32[256,1024]{1,0:T(8,128)S(1)} %forward_keep.1.agg_ref, bf16[256,1024]{1,0:T(8,128)(2,1)S(1)} %collective-permute-done.9.other_ref, ...), custom_call_target="tpu_custom_call" | custom-call | flops 1024 | bytes 1024 | tf_op jit(solution)/shard_map/layer/pallas_call | solution.py:217
  60.7 1.7 %collective-permute-start.11 = (bf16[512,256]{1,0:T(8,128)(2,1)S(1)}, bf16[512,256]{1,0:T(8,128)(2,1)S(1)}, u32[]{:S(2)}, u32[]{:S(2)}) collective-permute-start(bf16[512,256]{1,0:T(8,128)(2,1)S(1)} %get-tuple-element.138), channel_id=1, source_target_pairs={{0,4},{4,8},{8,12},{12,14},{14,10},{10,6},{6,2},{2,0},{1,5},{5,9},... | collective-permute-start | bytes 786440 | tf_op jit(solution)/shard_map/ppermute | solution.py:444
  62.8 5.4 %backward_step.3 = bf16[2048,256]{1,0:T(8,128)(2,1)S(1)} custom-call(s32[14]{0:T(128)S(1)} %fusion.7.ids_ref, s32[1024]{0:T(1024)S(1)} %select_reduce_fusion.table_ref, s32[384,8,128]{2,1,0:T(8,128)S(1)} %bitcast.24, bf16[1024,256]{1,0:T(8,128)(2,1)S(1)} %get-tuple-element.177.grad_ref.after_ref.refs_0_, ...), custom_call_target="tpu_custom_call" | custom-call | flops 1024 | bytes 1024 | tf_op jit(solution)/shard_map/backward_step/pallas_call | solution.py:263
  73.9 5.4 %backward_step.4 = bf16[2048,256]{1,0:T(8,128)(2,1)S(1)} custom-call(s32[14]{0:T(128)S(1)} %fusion.7.ids_ref, s32[1024]{0:T(1024)S(1)} %select_reduce_fusion.table_ref, s32[384,8,128]{2,1,0:T(8,128)S(1)} %bitcast.25, bf16[1024,256]{1,0:T(8,128)(2,1)S(1)} %get-tuple-element.177.grad_ref.after_ref.refs_0_, ...), custom_call_target="tpu_custom_call" | custom-call | flops 1024 | bytes 1024 | tf_op jit(solution)/shard_map/backward_step/pallas_call | solution.py:263
  79.4 4.2 %collective-permute-done.14 = bf16[1024,256]{1,0:T(8,128)(2,1)S(1)} collective-permute-done((bf16[1024,256]{1,0:T(8,128)(2,1)S(1)}, bf16[1024,256]{1,0:T(8,128)(2,1)S(1)}, u32[]{:S(2)}, u32[]{:S(2)}) %collective-permute-start.14) | collective-permute-done | bytes 524320 | tf_op jit(solution)/shard_map/ppermute | solution.py:444
  88.7 2.5 %collective-permute-start.18 = (f32[72,256]{1,0:T(8,128)S(1)}, f32[72,256]{1,0:T(8,128)S(1)}, u32[]{:S(2)}, u32[]{:S(2)}) collective-permute-start(f32[72,256]{1,0:T(8,128)S(1)} %get-tuple-element.168), channel_id=1, source_target_pairs={{0,6},{2,4},{4,2},{6,0},{8,14},{10,12},{12,10},{14,8},{1,7},{3,5},... | collective-permute-start | bytes 221192 | tf_op jit(solution)/shard_map/ppermute | solution.py:423
  91.3 5.4 %backward_step.5 = bf16[2048,256]{1,0:T(8,128)(2,1)S(1)} custom-call(s32[14]{0:T(128)S(1)} %fusion.7.ids_ref, s32[1024]{0:T(1024)S(1)} %select_reduce_fusion.table_ref, s32[384,8,128]{2,1,0:T(8,128)S(1)} %bitcast.26, bf16[1024,256]{1,0:T(8,128)(2,1)S(1)} %get-tuple-element.177.grad_ref.after_ref.refs_0_, ...), custom_call_target="tpu_custom_call" | custom-call | flops 1024 | bytes 1024 | tf_op jit(solution)/shard_map/backward_step/pallas_call | solution.py:263
  96.7 2.4 %collective-permute-done.16 = f32[72,256]{1,0:T(8,128)S(1)} collective-permute-done((f32[72,256]{1,0:T(8,128)S(1)}, f32[72,256]{1,0:T(8,128)S(1)}, u32[]{:S(2)}, u32[]{:S(2)}) %collective-permute-start.16) | collective-permute-done | bytes 73760 | tf_op jit(solution)/shard_map/ppermute | solution.py:423
  102.2 3.0 %backward_own.1 = f32[1024,256]{1,0:T(8,128)S(1)} custom-call(s32[14]{0:T(128)S(1)} %fusion.7.ids_ref, s32[1024]{0:T(1024)S(1)} %select_reduce_fusion.table_ref, s32[384,8,128]{2,1,0:T(8,128)S(1)} %bitcast.27, bf16[1024,256]{1,0:T(8,128)(2,1)S(1)} %get-tuple-element.177.grad_ref.after_ref.refs_0_, ...), custom_call_target="tpu_custom_call" | custom-call | flops 1024 | bytes 1024 | tf_op jit(solution)/shard_map/backward_own/pallas_call | solution.py:263
  105.5 2.7 %collective-permute-start.26 = (f32[72,256]{1,0:T(8,128)S(1)}, f32[72,256]{1,0:T(8,128)S(1)}, u32[]{:S(2)}, u32[]{:S(2)}) collective-permute-start(f32[72,256]{1,0:T(8,128)S(1)} %add.96.refs_0_), channel_id=1, source_target_pairs={{0,6},{2,4},{4,2},{6,0},{8,14},{10,12},{12,10},{14,8},{1,7},{3,5},... | collective-permute-start | bytes 221192 | tf_op jit(solution)/shard_map/ppermute | solution.py:431
  108.2 1.8 %collective-permute-start.25 = (f32[72,256]{1,0:T(8,128)S(1)}, f32[72,256]{1,0:T(8,128)S(1)}, u32[]{:S(2)}, u32[]{:S(2)}) collective-permute-start(f32[72,256]{1,0:T(8,128)S(1)} %add.96.refs_0_), channel_id=1, source_target_pairs={{0,4},{2,6},{4,0},{6,2},{8,12},{10,14},{12,8},{14,10},{1,5},{3,7},... | collective-permute-start | bytes 221192 | tf_op jit(solution)/shard_map/ppermute | solution.py:431
  112.1 2.7 %collective-permute-done.25.refs_2_ = f32[72,256]{1,0:T(8,128)S(1)} collective-permute-done((f32[72,256]{1,0:T(8,128)S(1)}, f32[72,256]{1,0:T(8,128)S(1)}, u32[]{:S(2)}, u32[]{:S(2)}) %collective-permute-start.25) | collective-permute-done | bytes 73760 | tf_op jit(solution)/shard_map/ppermute | solution.py:431
  117.6 1.8 %broadcast_select_fusion = (f32[256,256]{1,0:T(8,128)}, f32[256,256]{1,0:T(8,128)}) fusion(f32[256,256]{1,0:T(8,128)} %collective-permute-done.27, pred[]{:T(512)S(6)} %eq.36, f32[288,256]{1,0:T(8,128)S(1)} %join_grads.1), kind=kLoop, calls=%fused_computation.12 | loop fusion | flops 131072 | bytes 1048577 | tf_op jit(solution)/shard_map/jit(_where)/select_n | solution.py:477
  119.3 1.8 %collective-permute-done.22 = bf16[1024,256]{1,0:T(8,128)(2,1)S(1)} collective-permute-done((bf16[1024,256]{1,0:T(8,128)(2,1)}, bf16[1024,256]{1,0:T(8,128)(2,1)S(1)}, u32[]{:S(2)}, u32[]{:S(2)}) %collective-permute-start.22) | collective-permute-done | bytes 524320 | tf_op jit(solution)/shard_map/ppermute | solution.py:444
  (95 shorter events, 42.0 us)
Async XLA Ops:
  0.7 15.2 %collective-permute-start.1 = (bf16[1024,256]{1,0:T(8,128)(2,1)}, bf16[1024,256]{1,0:T(8,128)(2,1)S(1)}, u32[]{:S(2)}, u32[]{:S(2)}) collective-permute-start(bf16[1024,256]{1,0:T(8,128)(2,1)} %x_ref), channel_id=1, source_target_pairs={{4,0},{8,4},{12,8},{14,12},{10,14},{6,10},{2,6},{0,2},{5,1},{9,5},... | collective-permute-start | bytes 1572872 | tf_op jit(solution)/shard_map/ppermute | solution.py:373
  3.7 13.6 %collective-permute-start = (bf16[1024,256]{1,0:T(8,128)(2,1)}, bf16[1024,256]{1,0:T(8,128)(2,1)S(1)}, u32[]{:S(2)}, u32[]{:S(2)}) collective-permute-start(bf16[1024,256]{1,0:T(8,128)(2,1)} %x_ref), channel_id=1, source_target_pairs={{0,4},{4,8},{8,12},{12,14},{14,10},{10,6},{6,2},{2,0},{1,5},{5,9},... | collective-permute-start | bytes 1572872 | tf_op jit(solution)/shard_map/ppermute | solution.py:372
  7.3 6.9 %collective-permute-start.2 = (f32[1,1024]{1,0:T(1,128)S(1)}, f32[1,1024]{1,0:T(1,128)S(1)}, u32[]{:S(2)}, u32[]{:S(2)}) collective-permute-start(f32[1,1024]{1,0:T(1,128)S(1)} %dynamic-slice_bitcast_fusion), channel_id=1, source_target_pairs={{0,1},{1,0},{2,3},{3,2},{4,5},{5,4},{6,7},{7,6},{8,9},{9,8},{10,11... | collective-permute-start | bytes 12296 | tf_op jit(solution)/shard_map/ppermute | solution.py:361
  17.3 12.5 %collective-permute-start.3 = (bf16[1024,256]{1,0:T(8,128)(2,1)S(1)}, bf16[1024,256]{1,0:T(8,128)(2,1)S(1)}, u32[]{:S(2)}, u32[]{:S(2)}) collective-permute-start(bf16[1024,256]{1,0:T(8,128)(2,1)S(1)} %collective-permute-done.refs_0_), channel_id=1, source_target_pairs={{0,4},{4,8},{8,12},{12,14},{14,10},{10,6},{6,2},{2,0},{1,5},{5,9},... | collective-permute-start | bytes 1572872 | tf_op jit(solution)/shard_map/ppermute | solution.py:372
  17.7 12.6 %collective-permute-start.4 = (bf16[1024,256]{1,0:T(8,128)(2,1)S(1)}, bf16[1024,256]{1,0:T(8,128)(2,1)S(1)}, u32[]{:S(2)}, u32[]{:S(2)}) collective-permute-start(bf16[1024,256]{1,0:T(8,128)(2,1)S(1)} %collective-permute-done.1.refs_1_), channel_id=1, source_target_pairs={{4,0},{8,4},{12,8},{14,12},{10,14},{6,10},{2,6},{0,2},{5,1},{9,5},... | collective-permute-start | bytes 1572872 | tf_op jit(solution)/shard_map/ppermute | solution.py:373
  30.3 11.7 %collective-permute-start.5 = (bf16[1024,256]{1,0:T(8,128)(2,1)S(1)}, bf16[1024,256]{1,0:T(8,128)(2,1)S(1)}, u32[]{:S(2)}, u32[]{:S(2)}) collective-permute-start(bf16[1024,256]{1,0:T(8,128)(2,1)S(1)} %collective-permute-done.3.refs_0_), channel_id=1, source_target_pairs={{0,4},{4,8},{8,12},{12,14},{14,10},{10,6},{6,2},{2,0},{1,5},{5,9},... | collective-permute-start | bytes 1572872 | tf_op jit(solution)/shard_map/ppermute | solution.py:372
  31.9 11.3 %collective-permute-start.6 = (bf16[1024,256]{1,0:T(8,128)(2,1)S(1)}, bf16[1024,256]{1,0:T(8,128)(2,1)S(1)}, u32[]{:S(2)}, u32[]{:S(2)}) collective-permute-start(bf16[1024,256]{1,0:T(8,128)(2,1)S(1)} %collective-permute-done.4.refs_1_), channel_id=1, source_target_pairs={{4,0},{8,4},{12,8},{14,12},{10,14},{6,10},{2,6},{0,2},{5,1},{9,5},... | collective-permute-start | bytes 1572872 | tf_op jit(solution)/shard_map/ppermute | solution.py:373
  43.2 7.8 %collective-permute-start.7 = (bf16[512,256]{1,0:T(8,128)(2,1)S(1)}, bf16[512,256]{1,0:T(8,128)(2,1)S(1)}, u32[]{:S(2)}, u32[]{:S(2)}) collective-permute-start(bf16[512,256]{1,0:T(8,128)(2,1)S(1)} %slice.38), channel_id=1, source_target_pairs={{0,4},{4,8},{8,12},{12,14},{14,10},{10,6},{6,2},{2,0},{1,5},{5,9},... | collective-permute-start | bytes 786440 | tf_op jit(solution)/shard_map/ppermute | solution.py:376
  44.8 6.4 %collective-permute-start.8 = (bf16[512,256]{1,0:T(8,128)(2,1)S(1)}, bf16[512,256]{1,0:T(8,128)(2,1)S(1)}, u32[]{:S(2)}, u32[]{:S(2)}) collective-permute-start(bf16[512,256]{1,0:T(8,128)(2,1)S(1)} %slice.39), channel_id=1, source_target_pairs={{4,0},{8,4},{12,8},{14,12},{10,14},{6,10},{2,6},{0,2},{5,1},{9,5},... | collective-permute-start | bytes 786440 | tf_op jit(solution)/shard_map/ppermute | solution.py:377
  60.7 8.4 %collective-permute-start.11 = (bf16[512,256]{1,0:T(8,128)(2,1)S(1)}, bf16[512,256]{1,0:T(8,128)(2,1)S(1)}, u32[]{:S(2)}, u32[]{:S(2)}) collective-permute-start(bf16[512,256]{1,0:T(8,128)(2,1)S(1)} %get-tuple-element.138), channel_id=1, source_target_pairs={{0,4},{4,8},{8,12},{12,14},{14,10},{10,6},{6,2},{2,0},{1,5},{5,9},... | collective-permute-start | bytes 786440 | tf_op jit(solution)/shard_map/ppermute | solution.py:444
  62.5 8.1 %collective-permute-start.12 = (bf16[512,256]{1,0:T(8,128)(2,1)S(1)}, bf16[512,256]{1,0:T(8,128)(2,1)S(1)}, u32[]{:S(2)}, u32[]{:S(2)}) collective-permute-start(bf16[512,256]{1,0:T(8,128)(2,1)S(1)} %get-tuple-element.139), channel_id=1, source_target_pairs={{4,0},{8,4},{12,8},{14,12},{10,14},{6,10},{2,6},{0,2},{5,1},{9,5},... | collective-permute-start | bytes 786440 | tf_op jit(solution)/shard_map/ppermute | solution.py:445
  70.7 12.9 %collective-permute-start.14 = (bf16[1024,256]{1,0:T(8,128)(2,1)S(1)}, bf16[1024,256]{1,0:T(8,128)(2,1)S(1)}, u32[]{:S(2)}, u32[]{:S(2)}) collective-permute-start(bf16[1024,256]{1,0:T(8,128)(2,1)S(1)} %get-tuple-element.154), channel_id=1, source_target_pairs={{0,4},{4,8},{8,12},{12,14},{14,10},{10,6},{6,2},{2,0},{1,5},{5,9},... | collective-permute-start | bytes 1572872 | tf_op jit(solution)/shard_map/ppermute | solution.py:444
  72.2 12.5 %collective-permute-start.15 = (bf16[1024,256]{1,0:T(8,128)(2,1)S(1)}, bf16[1024,256]{1,0:T(8,128)(2,1)S(1)}, u32[]{:S(2)}, u32[]{:S(2)}) collective-permute-start(bf16[1024,256]{1,0:T(8,128)(2,1)S(1)} %get-tuple-element.155), channel_id=1, source_target_pairs={{4,0},{8,4},{12,8},{14,12},{10,14},{6,10},{2,6},{0,2},{5,1},{9,5},... | collective-permute-start | bytes 1572872 | tf_op jit(solution)/shard_map/ppermute | solution.py:445
  73.8 5.5 %collective-permute-start.13 = (f32[288,256]{1,0:T(8,128)S(1)}, f32[288,256]{1,0:T(8,128)S(1)}, u32[]{:S(2)}, u32[]{:S(2)}) collective-permute-start(f32[288,256]{1,0:T(8,128)S(1)} %get-tuple-element.152), channel_id=1, source_target_pairs={{0,1},{1,0},{2,3},{3,2},{4,5},{5,4},{6,7},{7,6},{8,9},{9,8},{10,11... | collective-permute-start | bytes 884744 | tf_op jit(solution)/shard_map/ppermute | solution.py:418
  85.0 16.0 %collective-permute-start.19 = (bf16[1024,256]{1,0:T(8,128)(2,1)S(1)}, bf16[1024,256]{1,0:T(8,128)(2,1)S(1)}, u32[]{:S(2)}, u32[]{:S(2)}) collective-permute-start(bf16[1024,256]{1,0:T(8,128)(2,1)S(1)} %get-tuple-element.170), channel_id=1, source_target_pairs={{0,4},{4,8},{8,12},{12,14},{14,10},{10,6},{6,2},{2,0},{1,5},{5,9},... | collective-permute-start | bytes 1572872 | tf_op jit(solution)/shard_map/ppermute | solution.py:444
  85.9 15.1 %collective-permute-start.20 = (bf16[1024,256]{1,0:T(8,128)(2,1)S(1)}, bf16[1024,256]{1,0:T(8,128)(2,1)S(1)}, u32[]{:S(2)}, u32[]{:S(2)}) collective-permute-start(bf16[1024,256]{1,0:T(8,128)(2,1)S(1)} %get-tuple-element.171), channel_id=1, source_target_pairs={{4,0},{8,4},{12,8},{14,12},{10,14},{6,10},{2,6},{0,2},{5,1},{9,5},... | collective-permute-start | bytes 1572872 | tf_op jit(solution)/shard_map/ppermute | solution.py:445
  87.7 11.4 %collective-permute-start.16 = (f32[72,256]{1,0:T(8,128)S(1)}, f32[72,256]{1,0:T(8,128)S(1)}, u32[]{:S(2)}, u32[]{:S(2)}) collective-permute-start(f32[72,256]{1,0:T(8,128)S(1)} %get-tuple-element.166), channel_id=1, source_target_pairs={{0,2},{2,0},{4,6},{6,4},{8,10},{10,8},{12,14},{14,12},{1,3},{3,1},... | collective-permute-start | bytes 221192 | tf_op jit(solution)/shard_map/ppermute | solution.py:423
  88.4 11.3 %collective-permute-start.17 = (f32[72,256]{1,0:T(8,128)S(1)}, f32[72,256]{1,0:T(8,128)S(1)}, u32[]{:S(2)}, u32[]{:S(2)}) collective-permute-start(f32[72,256]{1,0:T(8,128)S(1)} %get-tuple-element.167), channel_id=1, source_target_pairs={{0,4},{2,6},{4,0},{6,2},{8,12},{10,14},{12,8},{14,10},{1,5},{3,7},... | collective-permute-start | bytes 221192 | tf_op jit(solution)/shard_map/ppermute | solution.py:423
  88.7 11.2 %collective-permute-start.18 = (f32[72,256]{1,0:T(8,128)S(1)}, f32[72,256]{1,0:T(8,128)S(1)}, u32[]{:S(2)}, u32[]{:S(2)}) collective-permute-start(f32[72,256]{1,0:T(8,128)S(1)} %get-tuple-element.168), channel_id=1, source_target_pairs={{0,6},{2,4},{4,2},{6,0},{8,14},{10,12},{12,10},{14,8},{1,7},{3,5},... | collective-permute-start | bytes 221192 | tf_op jit(solution)/shard_map/ppermute | solution.py:423
  99.9 5.6 %collective-permute-start.21 = (f32[72,256]{1,0:T(8,128)S(1)}, f32[72,256]{1,0:T(8,128)S(1)}, u32[]{:S(2)}, u32[]{:S(2)}) collective-permute-start(f32[72,256]{1,0:T(8,128)S(1)} %add_add_fusion), channel_id=1, source_target_pairs={{0,8},{2,10},{4,12},{6,14},{8,0},{10,2},{12,4},{14,6},{1,9},{3,11}... | collective-permute-start | bytes 221192 | tf_op jit(solution)/shard_map/ppermute | solution.py:427
  105.5 6.5 %collective-permute-start.26 = (f32[72,256]{1,0:T(8,128)S(1)}, f32[72,256]{1,0:T(8,128)S(1)}, u32[]{:S(2)}, u32[]{:S(2)}) collective-permute-start(f32[72,256]{1,0:T(8,128)S(1)} %add.96.refs_0_), channel_id=1, source_target_pairs={{0,6},{2,4},{4,2},{6,0},{8,14},{10,12},{12,10},{14,8},{1,7},{3,5},... | collective-permute-start | bytes 221192 | tf_op jit(solution)/shard_map/ppermute | solution.py:431
  108.2 6.6 %collective-permute-start.25 = (f32[72,256]{1,0:T(8,128)S(1)}, f32[72,256]{1,0:T(8,128)S(1)}, u32[]{:S(2)}, u32[]{:S(2)}) collective-permute-start(f32[72,256]{1,0:T(8,128)S(1)} %add.96.refs_0_), channel_id=1, source_target_pairs={{0,4},{2,6},{4,0},{6,2},{8,12},{10,14},{12,8},{14,10},{1,5},{3,7},... | collective-permute-start | bytes 221192 | tf_op jit(solution)/shard_map/ppermute | solution.py:431
  110.0 11.1 %collective-permute-start.22 = (bf16[1024,256]{1,0:T(8,128)(2,1)}, bf16[1024,256]{1,0:T(8,128)(2,1)S(1)}, u32[]{:S(2)}, u32[]{:S(2)}) collective-permute-start(bf16[1024,256]{1,0:T(8,128)(2,1)} %get-tuple-element.184), channel_id=1, source_target_pairs={{0,4},{4,8},{8,12},{12,14},{14,10},{10,6},{6,2},{2,0},{1,5},{5,9},... | collective-permute-start | bytes 1572872 | tf_op jit(solution)/shard_map/ppermute | solution.py:444
  110.7 10.4 %collective-permute-start.23 = (bf16[1024,256]{1,0:T(8,128)(2,1)S(1)}, bf16[1024,256]{1,0:T(8,128)(2,1)S(1)}, u32[]{:S(2)}, u32[]{:S(2)}) collective-permute-start(bf16[1024,256]{1,0:T(8,128)(2,1)S(1)} %get-tuple-element.185), channel_id=1, source_target_pairs={{4,0},{8,4},{12,8},{14,12},{10,14},{6,10},{2,6},{0,2},{5,1},{9,5},... | collective-permute-start | bytes 1572872 | tf_op jit(solution)/shard_map/ppermute | solution.py:445
  (14 other events, 63.0 us)

commit v3 on v2

--- a/solution.py
+++ b/solution.py
@@ -196,7 +196,7 @@
         grad_b, wn_ref[...], (((1,), (1,)), ((), ())), preferred_element_type=F32
     )
     mg_ref[...] = (mean_grad / div_full).astype(BF16)
-    part = jnp.sum(pre_grad.reshape(rows // 32, 32, width), axis=0)
+    part = jnp.sum(pre_grad.reshape(rows // 64, 64, width), axis=0)
 
     @pl.when(pl.program_id(0) == 0)
     def _():
@@ -220,8 +220,8 @@
         in_specs=[
             turned, turned, pl.BlockSpec((1, blk), lambda i: (0, i)), plain, plain, weight,
         ],
-        out_specs=[plain] * 4 + [pl.BlockSpec((32, width), lambda i: (0, 0))],
-        out_shape=[act] * 4 + [jax.ShapeDtypeStruct((32, width), F32)],
+        out_specs=[plain] * 4 + [pl.BlockSpec((64, width), lambda i: (0, 0))],
+        out_shape=[act] * 4 + [jax.ShapeDtypeStruct((64, width), F32)],
         compiler_params=pltpu.CompilerParams(vmem_limit_bytes=VMEM_LIMIT),
         cost_estimate=BRIEF,
         name="layer",
@@ -270,47 +270,70 @@
         scratch_shapes=[pltpu.VMEM((piece_rows, len(grads) * rows), BF16)],
         out_shape=jax.ShapeDtypeStruct((len(cols) * piece_rows, width), out_dtype),
         compiler_params=pltpu.CompilerParams(vmem_limit_bytes=VMEM_LIMIT),
+        cost_estimate=pl.CostEstimate(
+            flops=8 * len(cols) * piece_rows * rows * len(grads) * width,
+            bytes_accessed=masks.size * 4 + 4 * len(cols) * piece_rows * width,
+            transcendentals=0,
+        ),
+        name=name,
+    )(*args)
+
+
+def small_call(kernel, name, out_shape, args, scratch=()):
+    return pl.pallas_call(
+        kernel,
+        in_specs=[smem_spec()] + [vmem_spec()] * (len(args) - 1),
+        out_specs=[vmem_spec()] * len(out_shape),
+        out_shape=out_shape,
+        scratch_shapes=list(scratch),
+        compiler_params=pltpu.CompilerParams(vmem_limit_bytes=VMEM_LIMIT),
         cost_estimate=BRIEF,
         name=name,
     )(*args)
 
 
-def small_call(kernel, name, out_shape, args):
-    return pl.pallas_call(
-        kernel,
-        in_specs=[smem_spec()] + [vmem_spec()] * (len(args) - 1),
-        out_specs=jax.tree.map(lambda _: vmem_spec(), out_shape),
-        out_shape=out_shape,
-        compiler_params=pltpu.CompilerParams(vmem_limit_bytes=VMEM_LIMIT),
-        cost_estimate=BRIEF,
-        name=name,
-    )(*args)
-
-
-def weight_kernel(at, ids_ref, x_ref, mean_ref, gb_ref, bias_ref, keep_ref, send_ref):
+def weight_kernel(at, ids_ref, x_ref, mean_ref, gb_ref, bias_ref, own_ref, *rest):
+    sends, sums = rest[:3], rest[3]
     width = gb_ref.shape[1]
     grad = gb_ref[...]
-    own = jnp.dot(x_ref[...].T, grad, preferred_element_type=F32)
-    neigh = jnp.dot(mean_ref[...].T, grad, preferred_element_type=F32)
+    sums[:width] = jnp.dot(x_ref[...].T, grad, preferred_element_type=F32)
+    sums[width : 2 * width] = jnp.dot(mean_ref[...].T, grad, preferred_element_type=F32)
+    sums[2 * width :] = bias_ref[...]
+    rows, extra = width // 4, bias_ref.shape[0] // 4
+    for x, out in enumerate((own_ref,) + sends):
+        quarter = ids_ref[at + x]
+        for base, count, to in ((0, rows, 0), (width, rows, rows), (2 * width, extra, 2 * rows)):
+            start = pl.multiple_of(base + quarter * count, 16)
+            out[to : to + count] = sums[pl.ds(start, count)].astype(out.dtype)
+
+
+def quad_sum_kernel(at, ids_ref, own_ref, one_ref, two_ref, three_ref, keep_ref, send_ref):
+    total = own_ref[...] + one_ref[...].astype(F32)
+    total = total + (two_ref[...].astype(F32) + three_ref[...].astype(F32))
+    extra = keep_ref.shape[0] * 2 - own_ref.shape[0]
+    rows = keep_ref.shape[0] - extra
     first = ids_ref[at] == 0
-    keep_ref[:width] = jnp.where(first, own, neigh)
-    send_ref[:width] = jnp.where(first, neigh, own)
-    keep_ref[width:] = bias_ref[...]
-    send_ref[width:] = bias_ref[...]
-
-
-def split_kernel(at, ids_ref, keep_ref, got_ref, *outs):
-    chunk = outs[0].shape[0]
-    for x, out in enumerate(outs):
-        rows = pl.ds(pl.multiple_of(ids_ref[at + x], 8), chunk)
-        out[...] = keep_ref[rows] + got_ref[rows]
-
-
-def join_kernel(at, scale, ids_ref, *refs):
-    out = refs[-1]
-    for x, part in enumerate(refs[:-1]):
-        rows = pl.ds(pl.multiple_of(ids_ref[at + x], 8), part.shape[0])
-        out[rows] = part[...] * scale
+    keep_ref[:rows] = jnp.where(first, total[:rows], total[rows : 2 * rows])
+    send_ref[:rows] = jnp.where(first, total[rows : 2 * rows], total[:rows])
+    keep_ref[rows:] = total[2 * rows :]
+    send_ref[rows:] = total[2 * rows :]
+
+
+def join_kernel(at, ids_ref, *refs):
+    parts, (matrix_ref, bias_ref) = refs[:-2], refs[-2:]
+    rows, extra = matrix_ref.shape[0] // 4, bias_ref.shape[0] // 4
+    for x, part in enumerate(parts):
+        quarter = ids_ref[at + x]
+        matrix_ref[pl.ds(pl.multiple_of(quarter * rows, 16), rows)] = part[:rows]
+        bias_ref[pl.ds(pl.multiple_of(quarter * extra, 16), extra)] = part[rows:]
+
+
+def scale_kernel(at, scale, ids_ref, own_ref, got_ref, bias_ref, self_ref, neigh_ref, sum_ref):
+    first = ids_ref[at] == 0
+    own, got = own_ref[...].astype(F32) * scale, got_ref[...].astype(F32) * scale
+    self_ref[...] = jnp.where(first, own, got)
+    neigh_ref[...] = jnp.where(first, got, own)
+    sum_ref[...] = jnp.sum(bias_ref[...].astype(F32), axis=0, keepdims=True) * scale
 
 
 def local(
@@ -334,12 +357,10 @@
     side = lax.axis_index("col").astype(jnp.int32)
     shard_cols = node_rows // 128
     at_side, at_other, at_quad = n, n + 1, n + 2
-    bias_rows = 32
-    chunk = (width + bias_rows) // 4
     known = [
         [order[(order.index(r) + k) % n] * shard_cols for k in range(n)]
         + [c, 1 - c]
-        + [((r & 3) ^ x) * chunk for x in range(4)]
+        + [(r & 3) ^ x for x in range(4)]
         for r in range(n)
         for c in range(grid_cols)
     ]
@@ -383,7 +404,8 @@
             own_part = jnp.dot(x_now, ws_now, preferred_element_type=F32) + b_now
             far_tiles = shard_tiles(far, node_rows, ids_now, table, masks, block_rows)
             early = (own_part, og_now.astype(F32), far_tiles, div_now)
-        acc, from_left, from_right, early = lax.optimization_barrier((acc, next_left, next_right, early))
+        acc, from_left, early = lax.optimization_barrier((acc, next_left, early))
+        acc, from_right = lax.optimization_barrier((acc, next_right))
         pieces, cols = [from_left, from_right], next_cols
     own_part, wide_out_grad, far_tiles, divisor = early
     for_other = last_forward(pieces, at_other, ids, far_tiles, acc, BF16, "forward_send")
@@ -406,41 +428,50 @@
     grad_scale = (node_rows * n * grid_cols) ** (-0.5)
     bits = int(math.log2(n))
 
-    matrix_shape = jax.ShapeDtypeStruct((4 * chunk, width), F32)
-
-    def quad_perm(x):
-        return [(r, r ^ x) for r in range(n)]
+    def array(rows, dtype):
+        return jax.ShapeDtypeStruct((rows, width), dtype)
+
+    def to_quad(parts, axis="row"):
+        return [lax.ppermute(part, axis, [(r, r ^ x) for r in range(n)]) for x, part in parts]
+
+    def start_quad(parts):
+        quarter = 2 * (width // 4) + 16
+        own, *sends = small_call(
+            partial(weight_kernel, at_quad), "weight_grads",
+            [array(quarter, F32)] + [array(quarter, BF16)] * 3, (ids,) + parts,
+            scratch=[pltpu.VMEM((2 * width + 64, width), F32)],
+        )
+        return [own] + to_quad(list(enumerate(sends, 1)))
 
     def to_core(parts):
         keep, send = small_call(
-            partial(weight_kernel, at_side), "weight_grads", [matrix_shape] * 2, (ids,) + parts
+            partial(quad_sum_kernel, at_side), "quad_sums", [array(width // 4 + 16, F32)] * 2,
+            (ids,) + tuple(parts),
         )
-        return keep, lax.ppermute(send, "col", swap)
-
-    def to_quad(parts):
-        quarter = jax.ShapeDtypeStruct((chunk, width), F32)
-        parts = small_call(partial(split_kernel, at_quad), "split_grads", [quarter] * 4, (ids,) + parts)
-        return [parts[0]] + [lax.ppermute(parts[x], "row", quad_perm(x)) for x in (1, 2, 3)]
+        return [keep, lax.ppermute(send, "col", swap)]
 
     def add_all(b, parts):
-        quarter = sum(parts[1:], parts[0])
+        quarter = parts[0] + parts[1]
         return [quarter, lax.ppermute(quarter, "row", [(r, r ^ (1 << b)) for r in range(n)])]
 
     def from_quad(parts):
-        quarter = sum(parts[1:], parts[0])
-        return [quarter] + [lax.ppermute(quarter, "row", quad_perm(x)) for x in (1, 2, 3)]
+        quarter = (parts[0] + parts[1]).astype(BF16)
+        return [quarter] + to_quad([(x, quarter) for x in (1, 2, 3)])
 
     spread = [[] for _ in range(far)]
-    spread[0].append(to_core)
-    spread[1].append(to_quad)
+    spread[0].append(start_quad)
+    spread[1].append(to_core)
     for b in range(2, bits):
-        spread[b].append(partial(add_all, b))
-    spread[far - 1].append(from_quad)
+        spread[b - 1].append(partial(add_all, b))
+    spread[bits - 1].append(from_quad)
 
     weights = (node_features, mean, grad_b, bias_part)
     right, left = far_terms[:half], far_terms[half:]
     for s in range(far - 1, -1, -1):
-        right, left, grads = lax.optimization_barrier((right, left, both_grads))
+        mean_grad, other_grad = both_grads
+        right, mean_grad = lax.optimization_barrier((right, mean_grad))
+        left, other_grad = lax.optimization_barrier((left, other_grad))
+        grads = [mean_grad, other_grad]
         right = lax.ppermute(right, "row", clockwise)
         left = lax.ppermute(left, "row", counter)
         if s > 0:
@@ -458,7 +489,7 @@
         terms, weights = lax.optimization_barrier((terms, weights))
         for one in spread[far - 1 - s]:
             weights = one(weights)
-        terms, right, left, both_grads = lax.optimization_barrier((terms, right, left, grads))
+        terms, both_grads = lax.optimization_barrier((terms, grads))
         if s > 0:
             if s == far - 1:
                 gap = jnp.zeros((half, width), BF16)
@@ -469,13 +500,16 @@
         else:
             feature_grad = (terms + right.astype(F32) + left.astype(F32)).astype(BF16)
 
-    matrix = small_call(
-        partial(join_kernel, at_quad, grad_scale), "join_grads", matrix_shape, (ids,) + tuple(weights)
-    )
-    got = lax.ppermute(matrix[:width], "col", swap)
-    grad_self = jnp.where(side == 0, matrix[:width], got)
-    grad_neigh = jnp.where(side == 0, got, matrix[:width])
-    grad_bias = jnp.sum(matrix[width:], axis=0)
+    matrix, bias_sums = small_call(
+        partial(join_kernel, at_quad), "join_grads", [array(width, BF16), array(64, BF16)],
+        (ids,) + tuple(weights),
+    )
+    got = lax.ppermute(matrix, "col", swap)
+    grad_self, grad_neigh, grad_bias = small_call(
+        partial(scale_kernel, at_side, grad_scale), "scale_grads",
+        [array(width, F32)] * 2 + [array(1, F32)], (ids, matrix, got, bias_sums),
+    )
+    grad_bias = grad_bias.reshape(width)
     return node_out, feature_grad, grad_self, grad_neigh, grad_bias
 
 

time: 122 us -> 114 us (0.934)
  waiting for transfers between devices: 26.9 us -> 19.3 us
  other arithmetic: 7.99 us -> 4.84 us
  Pallas kernels: 51.8 us -> 53.2 us
    ppermute x4, waiting for transfers between devices: 6.9 us -> 0.99 us  [local(): right = lax.ppermute(right, 'row', clockwise)]
    ppermute x4, waiting for transfers between devices: 2.55 us -> 7.82 us  [local(): left = lax.ppermute(left, 'row', counter)]
    ppermute x8, waiting for transfers between devices: 7.44 us -> 2.61 us  [the longest x1 1.33 us: local(): got = lax.ppermute(matrix, 'col', swap)]
    ppermute x3, starting transfers between devices: 5.09 us -> 0.66 us  [local(): next_right = lax.ppermute(from_right, 'row', counter)]
    ppermute x3, starting transfers between devices: 2.11 us -> 6.48 us  [local(): next_left = lax.ppermute(from_left, 'row', clockwise)]
    ppermute x3, waiting for transfers between devices: 3.39 us -> 0.01 us  [local(): next_right = lax.ppermute(from_right, 'row', counter)]
    ppermute x4, starting transfers between devices: 3.55 us -> 5.44 us  [local(): left = lax.ppermute(left, 'row', counter)]
    ppermute x4, starting transfers between devices: 4.74 us -> 2.87 us  [local(): right = lax.ppermute(right, 'row', clockwise)]
  transfers between devices with their start and end apart: 28 -> 28, of which waited for: 19 -> 12; matrix products, arithmetic and copies ran while one was open for 7% -> 5% of each run, Pallas kernels for 38% -> 42%
where the time goes in v3:
time: 114 us; the launch traced here: 113 us
  Pallas kernels  53.2 us (47%)
  starting transfers between devices  27.8 us (24%)
  waiting for transfers between devices  19.3 us (17%)
  local copies, waits for them, and re-layouts  5.74 us (5%)
  other arithmetic  4.84 us (4%)
  between operations  1.71 us (2%)
    pallas_call x4, Pallas kernels, forward_mm(): pl.pallas_call(partial(forward_kernel, tuple(cols), side_at, block_rows,...  20.6 us
    pallas_call x4, Pallas kernels, backward_mm(): pl.pallas_call(partial(backward_kernel, tuple(cols), tuple(sides), block_...  19.2 us
    ppermute x4, waiting for transfers between devices, local(): left = lax.ppermute(left, 'row', counter)  7.82 us
    ppermute x6, starting transfers between devices, to_quad(): lax.ppermute(part, axis, [(r, r ^ x) for r in range(n)])  7.11 us
    ppermute x3, waiting for transfers between devices, local(): next_left = lax.ppermute(from_left, 'row', clockwise)  6.74 us
    ppermute x3, starting transfers between devices, local(): next_left = lax.ppermute(from_left, 'row', clockwise)  6.48 us
    ppermute x4, starting transfers between devices, local(): left = lax.ppermute(left, 'row', counter)  5.44 us
    unnamed x20, local copies, waits for them, and re-layouts  4.94 us
  transfers between devices with their start and end apart: 28, of which 12 were waited for; matrix products, arithmetic and copies ran while one was open for 5% of the time, Pallas kernels for 42%

profile of v3, /device:TPU:0, one launch (start us, length us, event | category | flops | bytes accessed | tf_op | source)
XLA Modules:
  0.0 113.4 jit_solution(11477480776649569743)
XLA Ops:
  0.7 3.1 %collective-permute-start = (bf16[1024,256]{1,0:T(8,128)(2,1)}, bf16[1024,256]{1,0:T(8,128)(2,1)S(1)}, u32[]{:S(2)}, u32[]{:S(2)}) collective-permute-start(bf16[1024,256]{1,0:T(8,128)(2,1)} %x_ref), channel_id=1, source_target_pairs={{0,4},{4,8},{8,12},{12,14},{14,10},{10,6},{6,2},{2,0},{1,5},{5,9},... | collective-permute-start | bytes 1572872 | tf_op jit(solution)/shard_map/ppermute | solution.py:393
  5.1 2.0 %popcnt_reduce_fusion = s32[384,128]{1,0:T(8,128)S(1)} fusion(s32[1,1,384,128,8]{3,4,2,1,0:T(8,128)} %param.13), kind=kLoop, calls=%fused_computation | loop fusion | flops 737280 | bytes 1769472 | tf_op jit(solution)/shard_map/reduce_sum | solution.py:379
  9.4 3.3 %forward_step.4.refs_2_ = f32[256,2048]{1,0:T(8,128)S(1)} custom-call(s32[14]{0:T(128)S(1)} %fusion.7.ids_ref, s32[1024]{0:T(1024)S(1)} %select_reduce_fusion.table_ref, s32[384,8,128]{2,1,0:T(8,128)S(1)} %bitcast.20, bf16[1024,256]{1,0:T(8,128)(2,1)S(1)} %copy-done.4), custom_call_target="tpu_custom_call" | custom-call | flops 1024 | bytes 1024 | tf_op jit(solution)/shard_map/forward_step/pallas_call | solution.py:92
  14.2 1.7 %collective-permute-done.refs_0_ = bf16[1024,256]{1,0:T(8,128)(2,1)S(1)} collective-permute-done((bf16[1024,256]{1,0:T(8,128)(2,1)}, bf16[1024,256]{1,0:T(8,128)(2,1)S(1)}, u32[]{:S(2)}, u32[]{:S(2)}) %collective-permute-start) | collective-permute-done | bytes 524320 | tf_op jit(solution)/shard_map/ppermute | solution.py:393
  15.8 1.8 %collective-permute-start.3 = (bf16[1024,256]{1,0:T(8,128)(2,1)S(1)}, bf16[1024,256]{1,0:T(8,128)(2,1)S(1)}, u32[]{:S(2)}, u32[]{:S(2)}) collective-permute-start(bf16[1024,256]{1,0:T(8,128)(2,1)S(1)} %collective-permute-done.refs_0_), channel_id=1, source_target_pairs={{0,4},{4,8},{8,12},{12,14},{14,10},{10,6},{6,2},{2,0},{1,5},{5,9},... | collective-permute-start | bytes 1572872 | tf_op jit(solution)/shard_map/ppermute | solution.py:393
  17.9 1.6 %copy-done.3 = f32[256,2048]{1,0:T(8,128)S(1)} copy-done((f32[256,2048]{1,0:T(8,128)S(1)}, f32[256,2048]{1,0:T(8,128)}, u32[]{:S(2)}) %copy-start.3) | copy-done | bytes 2097176
  19.4 5.8 %forward_step.5.refs_2_ = f32[256,2048]{1,0:T(8,128)S(1)} custom-call(s32[14]{0:T(128)S(1)} %fusion.7.ids_ref, s32[1024]{0:T(1024)S(1)} %select_reduce_fusion.table_ref, s32[384,8,128]{2,1,0:T(8,128)S(1)} %bitcast.21, bf16[1024,256]{1,0:T(8,128)(2,1)S(1)} %collective-permute-done.refs_0_, bf16[1024,256]{1,0:T(8,128)(2,1)S(1)} %collective-permute-done.2.refs_1_, ...), custom_call_target="tpu_custom_call" | custom-call | flops 1024 | bytes 1024 | tf_op jit(solution)/shard_map/forward_step/pallas_call | solution.py:92
  25.2 1.7 %far_tiles.1.tiles_ref = bf16[1024,2048]{1,0:T(8,128)(2,1)S(1)} custom-call(s32[14]{0:T(128)S(1)} %fusion.7.ids_ref, s32[1024]{0:T(1024)S(1)} %select_reduce_fusion.table_ref, s32[384,8,128]{2,1,0:T(8,128)S(1)} %bitcast.22), custom_call_target="tpu_custom_call" | custom-call | flops 1024 | bytes 1024 | tf_op jit(solution)/shard_map/far_tiles/pallas_call | solution.py:115
  28.9 1.6 %collective-permute-start.5 = (bf16[1024,256]{1,0:T(8,128)(2,1)S(1)}, bf16[1024,256]{1,0:T(8,128)(2,1)S(1)}, u32[]{:S(2)}, u32[]{:S(2)}) collective-permute-start(bf16[1024,256]{1,0:T(8,128)(2,1)S(1)} %collective-permute-done.3.refs_0_), channel_id=1, source_target_pairs={{0,4},{4,8},{8,12},{12,14},{14,10},{10,6},{6,2},{2,0},{1,5},{5,9},... | collective-permute-start | bytes 1572872 | tf_op jit(solution)/shard_map/ppermute | solution.py:393
  31.0 5.7 %forward_step.6.refs_2_ = f32[256,2048]{1,0:T(8,128)S(1)} custom-call(s32[14]{0:T(128)S(1)} %fusion.7.ids_ref, s32[1024]{0:T(1024)S(1)} %select_reduce_fusion.table_ref, s32[384,8,128]{2,1,0:T(8,128)S(1)} %bitcast.23, bf16[1024,256]{1,0:T(8,128)(2,1)S(1)} %collective-permute-done.3.refs_0_, bf16[1024,256]{1,0:T(8,128)(2,1)S(1)} %collective-permute-done.4.refs_1_, ...), custom_call_target="tpu_custom_call" | custom-call | flops 1024 | bytes 1024 | tf_op jit(solution)/shard_map/forward_step/pallas_call | solution.py:92
  36.7 4.4 %collective-permute-done.5.refs_0_ = bf16[1024,256]{1,0:T(8,128)(2,1)S(1)} collective-permute-done((bf16[1024,256]{1,0:T(8,128)(2,1)S(1)}, bf16[1024,256]{1,0:T(8,128)(2,1)S(1)}, u32[]{:S(2)}, u32[]{:S(2)}) %collective-permute-start.5) | collective-permute-done | bytes 524320 | tf_op jit(solution)/shard_map/ppermute | solution.py:393
  41.1 1.5 %collective-permute-start.7 = (bf16[512,256]{1,0:T(8,128)(2,1)S(1)}, bf16[512,256]{1,0:T(8,128)(2,1)S(1)}, u32[]{:S(2)}, u32[]{:S(2)}) collective-permute-start(bf16[512,256]{1,0:T(8,128)(2,1)S(1)} %slice.30), channel_id=1, source_target_pairs={{0,4},{4,8},{8,12},{12,14},{14,10},{10,6},{6,2},{2,0},{1,5},{5,9},... | collective-permute-start | bytes 786440 | tf_op jit(solution)/shard_map/ppermute | solution.py:397
  43.3 5.7 %forward_step.7.acc_ref = f32[256,2048]{1,0:T(8,128)S(1)} custom-call(s32[14]{0:T(128)S(1)} %fusion.7.ids_ref, s32[1024]{0:T(1024)S(1)} %select_reduce_fusion.table_ref, s32[384,8,128]{2,1,0:T(8,128)S(1)} %bitcast.24, bf16[1024,256]{1,0:T(8,128)(2,1)S(1)} %collective-permute-done.5.refs_0_, bf16[1024,256]{1,0:T(8,128)(2,1)S(1)} %collective-permute-done.6.refs_1_, ...), custom_call_target="tpu_custom_call" | custom-call | flops 1024 | bytes 1024 | tf_op jit(solution)/shard_map/forward_step/pallas_call | solution.py:92
  52.4 3.1 %layer.1 = (bf16[1024,256]{1,0:T(8,128)(2,1)S(1)}, bf16[1024,256]{1,0:T(8,128)(2,1)}, bf16[1024,256]{1,0:T(8,128)(2,1)S(1)}, bf16[1024,256]{1,0:T(8,128)(2,1)S(1)}, f32[64,256]{1,0:T(8,128)S(1)}) custom-call(f32[256,1024]{1,0:T(8,128)S(1)} %forward_keep.1.agg_ref, bf16[256,1024]{1,0:T(8,128)(2,1)S(1)} %collective-permute-done.9.other_ref, ...), custom_call_target="tpu_custom_call" | custom-call | flops 1024 | bytes 1024 | tf_op jit(solution)/shard_map/layer/pallas_call | solution.py:217
  60.7 5.4 %backward_step.3 = bf16[2048,256]{1,0:T(8,128)(2,1)S(1)} custom-call(s32[14]{0:T(128)S(1)} %fusion.7.ids_ref, s32[1024]{0:T(1024)S(1)} %select_reduce_fusion.table_ref, s32[384,8,128]{2,1,0:T(8,128)S(1)} %bitcast.25, bf16[1024,256]{1,0:T(8,128)(2,1)S(1)} %get-tuple-element.178.grad_ref.after_ref.refs_0_, ...), custom_call_target="tpu_custom_call" | custom-call | flops 8589934592 | bytes 3670016 | tf_op jit(solution)/shard_map/backward_step/pallas_call | solution.py:263
  68.6 1.6 %collective-permute-start.14 = (bf16[144,256]{1,0:T(8,128)(2,1)S(1)}, bf16[144,256]{1,0:T(8,128)(2,1)S(1)}, u32[]{:S(2)}, u32[]{:S(2)}) collective-permute-start(bf16[144,256]{1,0:T(8,128)(2,1)S(1)} %get-tuple-element.158), channel_id=1, source_target_pairs={{0,4},{2,6},{4,0},{6,2},{8,12},{10,14},{12,8},{14,10},{1,5},{3,7},... | collective-permute-start | bytes 221192 | tf_op jit(solution)/shard_map/ppermute | solution.py:435
  73.0 5.4 %backward_step.4 = bf16[2048,256]{1,0:T(8,128)(2,1)S(1)} custom-call(s32[14]{0:T(128)S(1)} %fusion.7.ids_ref, s32[1024]{0:T(1024)S(1)} %select_reduce_fusion.table_ref, s32[384,8,128]{2,1,0:T(8,128)S(1)} %bitcast.26, bf16[1024,256]{1,0:T(8,128)(2,1)S(1)} %get-tuple-element.178.grad_ref.after_ref.refs_0_, ...), custom_call_target="tpu_custom_call" | custom-call | flops 8589934592 | bytes 3670016 | tf_op jit(solution)/shard_map/backward_step/pallas_call | solution.py:263
  80.4 2.7 %collective-permute-start.19 = (f32[80,256]{1,0:T(8,128)S(1)}, f32[80,256]{1,0:T(8,128)S(1)}, u32[]{:S(2)}, u32[]{:S(2)}) collective-permute-start(f32[80,256]{1,0:T(8,128)S(1)} %add.82), channel_id=1, source_target_pairs={{0,8},{2,10},{4,12},{6,14},{8,0},{10,2},{12,4},{14,6},{1,9},{3,11}... | collective-permute-start | bytes 245768 | tf_op jit(solution)/shard_map/ppermute | solution.py:455
  83.1 4.2 %collective-permute-done.17 = bf16[1024,256]{1,0:T(8,128)(2,1)S(1)} collective-permute-done((bf16[1024,256]{1,0:T(8,128)(2,1)S(1)}, bf16[1024,256]{1,0:T(8,128)(2,1)S(1)}, u32[]{:S(2)}, u32[]{:S(2)}) %collective-permute-start.17) | collective-permute-done | bytes 524320 | tf_op jit(solution)/shard_map/ppermute | solution.py:476
  89.7 5.4 %backward_step.5 = bf16[2048,256]{1,0:T(8,128)(2,1)S(1)} custom-call(s32[14]{0:T(128)S(1)} %fusion.7.ids_ref, s32[1024]{0:T(1024)S(1)} %select_reduce_fusion.table_ref, s32[384,8,128]{2,1,0:T(8,128)S(1)} %bitcast.27, bf16[1024,256]{1,0:T(8,128)(2,1)S(1)} %get-tuple-element.178.grad_ref.after_ref.refs_0_, ...), custom_call_target="tpu_custom_call" | custom-call | flops 8589934592 | bytes 3670016 | tf_op jit(solution)/shard_map/backward_step/pallas_call | solution.py:263
  95.1 1.8 %collective-permute-start.24 = (bf16[80,256]{1,0:T(8,128)(2,1)S(1)}, bf16[80,256]{1,0:T(8,128)(2,1)S(1)}, u32[]{:S(2)}, u32[]{:S(2)}) collective-permute-start(bf16[80,256]{1,0:T(8,128)(2,1)S(1)} %add_convert_fusion.7.refs_0_), channel_id=1, source_target_pairs={{0,6},{2,4},{4,2},{6,0},{8,14},{10,12},{12,10},{14,8},{1,7},{3,5},... | collective-permute-start | bytes 122888 | tf_op jit(solution)/shard_map/ppermute | solution.py:435
  100.4 1.9 %collective-permute-start.26 = (bf16[1024,256]{1,0:T(8,128)(2,1)S(1)}, bf16[1024,256]{1,0:T(8,128)(2,1)S(1)}, u32[]{:S(2)}, u32[]{:S(2)}) collective-permute-start(bf16[1024,256]{1,0:T(8,128)(2,1)S(1)} %get-tuple-element.187), channel_id=1, source_target_pairs={{4,0},{8,4},{12,8},{14,12},{10,14},{6,10},{2,6},{0,2},{5,1},{9,5},... | collective-permute-start | bytes 1572872 | tf_op jit(solution)/shard_map/ppermute | solution.py:476
  102.5 3.0 %backward_own.1 = f32[1024,256]{1,0:T(8,128)S(1)} custom-call(s32[14]{0:T(128)S(1)} %fusion.7.ids_ref, s32[1024]{0:T(1024)S(1)} %select_reduce_fusion.table_ref, s32[384,8,128]{2,1,0:T(8,128)S(1)} %bitcast.28, bf16[1024,256]{1,0:T(8,128)(2,1)S(1)} %get-tuple-element.178.grad_ref.after_ref.refs_0_, ...), custom_call_target="tpu_custom_call" | custom-call | flops 4294967296 | bytes 2621440 | tf_op jit(solution)/shard_map/backward_own/pallas_call | solution.py:263
  109.2 2.7 %collective-permute-done.26 = bf16[1024,256]{1,0:T(8,128)(2,1)S(1)} collective-permute-done((bf16[1024,256]{1,0:T(8,128)(2,1)S(1)}, bf16[1024,256]{1,0:T(8,128)(2,1)S(1)}, u32[]{:S(2)}, u32[]{:S(2)}) %collective-permute-start.26) | collective-permute-done | bytes 524320 | tf_op jit(solution)/shard_map/ppermute | solution.py:476
  (93 shorter events, 34.6 us)
Async XLA Ops:
  0.7 15.2 %collective-permute-start = (bf16[1024,256]{1,0:T(8,128)(2,1)}, bf16[1024,256]{1,0:T(8,128)(2,1)S(1)}, u32[]{:S(2)}, u32[]{:S(2)}) collective-permute-start(bf16[1024,256]{1,0:T(8,128)(2,1)} %x_ref), channel_id=1, source_target_pairs={{0,4},{4,8},{8,12},{12,14},{14,10},{10,6},{6,2},{2,0},{1,5},{5,9},... | collective-permute-start | bytes 1572872 | tf_op jit(solution)/shard_map/ppermute | solution.py:393
  3.7 13.9 %collective-permute-start.2 = (bf16[1024,256]{1,0:T(8,128)(2,1)}, bf16[1024,256]{1,0:T(8,128)(2,1)S(1)}, u32[]{:S(2)}, u32[]{:S(2)}) collective-permute-start(bf16[1024,256]{1,0:T(8,128)(2,1)} %x_ref), channel_id=1, source_target_pairs={{4,0},{8,4},{12,8},{14,12},{10,14},{6,10},{2,6},{0,2},{5,1},{9,5},... | collective-permute-start | bytes 1572872 | tf_op jit(solution)/shard_map/ppermute | solution.py:394
  7.3 6.9 %collective-permute-start.1 = (f32[1,1024]{1,0:T(1,128)S(1)}, f32[1,1024]{1,0:T(1,128)S(1)}, u32[]{:S(2)}, u32[]{:S(2)}) collective-permute-start(f32[1,1024]{1,0:T(1,128)S(1)} %dynamic-slice_bitcast_fusion), channel_id=1, source_target_pairs={{0,1},{1,0},{2,3},{3,2},{4,5},{5,4},{6,7},{7,6},{8,9},{9,8},{10,11... | collective-permute-start | bytes 12296 | tf_op jit(solution)/shard_map/ppermute | solution.py:382
  15.8 13.1 %collective-permute-start.3 = (bf16[1024,256]{1,0:T(8,128)(2,1)S(1)}, bf16[1024,256]{1,0:T(8,128)(2,1)S(1)}, u32[]{:S(2)}, u32[]{:S(2)}) collective-permute-start(bf16[1024,256]{1,0:T(8,128)(2,1)S(1)} %collective-permute-done.refs_0_), channel_id=1, source_target_pairs={{0,4},{4,8},{8,12},{12,14},{14,10},{10,6},{6,2},{2,0},{1,5},{5,9},... | collective-permute-start | bytes 1572872 | tf_op jit(solution)/shard_map/ppermute | solution.py:393
  17.6 12.9 %collective-permute-start.4 = (bf16[1024,256]{1,0:T(8,128)(2,1)S(1)}, bf16[1024,256]{1,0:T(8,128)(2,1)S(1)}, u32[]{:S(2)}, u32[]{:S(2)}) collective-permute-start(bf16[1024,256]{1,0:T(8,128)(2,1)S(1)} %collective-permute-done.2.refs_1_), channel_id=1, source_target_pairs={{4,0},{8,4},{12,8},{14,12},{10,14},{6,10},{2,6},{0,2},{5,1},{9,5},... | collective-permute-start | bytes 1572872 | tf_op jit(solution)/shard_map/ppermute | solution.py:394
  28.9 12.2 %collective-permute-start.5 = (bf16[1024,256]{1,0:T(8,128)(2,1)S(1)}, bf16[1024,256]{1,0:T(8,128)(2,1)S(1)}, u32[]{:S(2)}, u32[]{:S(2)}) collective-permute-start(bf16[1024,256]{1,0:T(8,128)(2,1)S(1)} %collective-permute-done.3.refs_0_), channel_id=1, source_target_pairs={{0,4},{4,8},{8,12},{12,14},{14,10},{10,6},{6,2},{2,0},{1,5},{5,9},... | collective-permute-start | bytes 1572872 | tf_op jit(solution)/shard_map/ppermute | solution.py:393
  30.5 12.1 %collective-permute-start.6 = (bf16[1024,256]{1,0:T(8,128)(2,1)S(1)}, bf16[1024,256]{1,0:T(8,128)(2,1)S(1)}, u32[]{:S(2)}, u32[]{:S(2)}) collective-permute-start(bf16[1024,256]{1,0:T(8,128)(2,1)S(1)} %collective-permute-done.4.refs_1_), channel_id=1, source_target_pairs={{4,0},{8,4},{12,8},{14,12},{10,14},{6,10},{2,6},{0,2},{5,1},{9,5},... | collective-permute-start | bytes 1572872 | tf_op jit(solution)/shard_map/ppermute | solution.py:394
  41.1 7.9 %collective-permute-start.7 = (bf16[512,256]{1,0:T(8,128)(2,1)S(1)}, bf16[512,256]{1,0:T(8,128)(2,1)S(1)}, u32[]{:S(2)}, u32[]{:S(2)}) collective-permute-start(bf16[512,256]{1,0:T(8,128)(2,1)S(1)} %slice.30), channel_id=1, source_target_pairs={{0,4},{4,8},{8,12},{12,14},{14,10},{10,6},{6,2},{2,0},{1,5},{5,9},... | collective-permute-start | bytes 786440 | tf_op jit(solution)/shard_map/ppermute | solution.py:397
  42.7 6.4 %collective-permute-start.8 = (bf16[512,256]{1,0:T(8,128)(2,1)S(1)}, bf16[512,256]{1,0:T(8,128)(2,1)S(1)}, u32[]{:S(2)}, u32[]{:S(2)}) collective-permute-start(bf16[512,256]{1,0:T(8,128)(2,1)S(1)} %slice.31), channel_id=1, source_target_pairs={{4,0},{8,4},{12,8},{14,12},{10,14},{6,10},{2,6},{0,2},{5,1},{9,5},... | collective-permute-start | bytes 786440 | tf_op jit(solution)/shard_map/ppermute | solution.py:398
  58.6 12.1 %collective-permute-start.12 = (bf16[512,256]{1,0:T(8,128)(2,1)S(1)}, bf16[512,256]{1,0:T(8,128)(2,1)S(1)}, u32[]{:S(2)}, u32[]{:S(2)}) collective-permute-start(bf16[512,256]{1,0:T(8,128)(2,1)S(1)} %get-tuple-element.149), channel_id=1, source_target_pairs={{4,0},{8,4},{12,8},{14,12},{10,14},{6,10},{2,6},{0,2},{5,1},{9,5},... | collective-permute-start | bytes 786440 | tf_op jit(solution)/shard_map/ppermute | solution.py:476
  60.1 10.7 %collective-permute-start.11 = (bf16[512,256]{1,0:T(8,128)(2,1)S(1)}, bf16[512,256]{1,0:T(8,128)(2,1)S(1)}, u32[]{:S(2)}, u32[]{:S(2)}) collective-permute-start(bf16[512,256]{1,0:T(8,128)(2,1)S(1)} %get-tuple-element.146), channel_id=1, source_target_pairs={{0,4},{4,8},{8,12},{12,14},{14,10},{10,6},{6,2},{2,0},{1,5},{5,9},... | collective-permute-start | bytes 786440 | tf_op jit(solution)/shard_map/ppermute | solution.py:475
  67.2 11.2 %collective-permute-start.13 = (bf16[144,256]{1,0:T(8,128)(2,1)S(1)}, bf16[144,256]{1,0:T(8,128)(2,1)S(1)}, u32[]{:S(2)}, u32[]{:S(2)}) collective-permute-start(bf16[144,256]{1,0:T(8,128)(2,1)S(1)} %get-tuple-element.157), channel_id=1, source_target_pairs={{0,2},{2,0},{4,6},{6,4},{8,10},{10,8},{12,14},{14,12},{1,3},{3,1},... | collective-permute-start | bytes 221192 | tf_op jit(solution)/shard_map/ppermute | solution.py:435
  68.6 9.8 %collective-permute-start.14 = (bf16[144,256]{1,0:T(8,128)(2,1)S(1)}, bf16[144,256]{1,0:T(8,128)(2,1)S(1)}, u32[]{:S(2)}, u32[]{:S(2)}) collective-permute-start(bf16[144,256]{1,0:T(8,128)(2,1)S(1)} %get-tuple-element.158), channel_id=1, source_target_pairs={{0,4},{2,6},{4,0},{6,2},{8,12},{10,14},{12,8},{14,10},{1,5},{3,7},... | collective-permute-start | bytes 221192 | tf_op jit(solution)/shard_map/ppermute | solution.py:435
  70.2 8.2 %collective-permute-start.15 = (bf16[144,256]{1,0:T(8,128)(2,1)S(1)}, bf16[144,256]{1,0:T(8,128)(2,1)S(1)}, u32[]{:S(2)}, u32[]{:S(2)}) collective-permute-start(bf16[144,256]{1,0:T(8,128)(2,1)S(1)} %get-tuple-element.159), channel_id=1, source_target_pairs={{0,6},{2,4},{4,2},{6,0},{8,14},{10,12},{12,10},{14,8},{1,7},{3,5},... | collective-permute-start | bytes 221192 | tf_op jit(solution)/shard_map/ppermute | solution.py:435
  70.9 16.4 %collective-permute-start.17 = (bf16[1024,256]{1,0:T(8,128)(2,1)S(1)}, bf16[1024,256]{1,0:T(8,128)(2,1)S(1)}, u32[]{:S(2)}, u32[]{:S(2)}) collective-permute-start(bf16[1024,256]{1,0:T(8,128)(2,1)S(1)} %get-tuple-element.165), channel_id=1, source_target_pairs={{4,0},{8,4},{12,8},{14,12},{10,14},{6,10},{2,6},{0,2},{5,1},{9,5},... | collective-permute-start | bytes 1572872 | tf_op jit(solution)/shard_map/ppermute | solution.py:476
  72.4 14.9 %collective-permute-start.16 = (bf16[1024,256]{1,0:T(8,128)(2,1)S(1)}, bf16[1024,256]{1,0:T(8,128)(2,1)S(1)}, u32[]{:S(2)}, u32[]{:S(2)}) collective-permute-start(bf16[1024,256]{1,0:T(8,128)(2,1)S(1)} %get-tuple-element.162), channel_id=1, source_target_pairs={{0,4},{4,8},{8,12},{12,14},{14,10},{10,6},{6,2},{2,0},{1,5},{5,9},... | collective-permute-start | bytes 1572872 | tf_op jit(solution)/shard_map/ppermute | solution.py:475
  80.4 14.7 %collective-permute-start.19 = (f32[80,256]{1,0:T(8,128)S(1)}, f32[80,256]{1,0:T(8,128)S(1)}, u32[]{:S(2)}, u32[]{:S(2)}) collective-permute-start(f32[80,256]{1,0:T(8,128)S(1)} %add.82), channel_id=1, source_target_pairs={{0,8},{2,10},{4,12},{6,14},{8,0},{10,2},{12,4},{14,6},{1,9},{3,11}... | collective-permute-start | bytes 245768 | tf_op jit(solution)/shard_map/ppermute | solution.py:455
  87.6 12.0 %collective-permute-start.21 = (bf16[1024,256]{1,0:T(8,128)(2,1)S(1)}, bf16[1024,256]{1,0:T(8,128)(2,1)S(1)}, u32[]{:S(2)}, u32[]{:S(2)}) collective-permute-start(bf16[1024,256]{1,0:T(8,128)(2,1)S(1)} %get-tuple-element.179), channel_id=1, source_target_pairs={{4,0},{8,4},{12,8},{14,12},{10,14},{6,10},{2,6},{0,2},{5,1},{9,5},... | collective-permute-start | bytes 1572872 | tf_op jit(solution)/shard_map/ppermute | solution.py:476
  88.2 11.9 %collective-permute-start.20 = (bf16[1024,256]{1,0:T(8,128)(2,1)S(1)}, bf16[1024,256]{1,0:T(8,128)(2,1)S(1)}, u32[]{:S(2)}, u32[]{:S(2)}) collective-permute-start(bf16[1024,256]{1,0:T(8,128)(2,1)S(1)} %get-tuple-element.176), channel_id=1, source_target_pairs={{0,4},{4,8},{8,12},{12,14},{14,10},{10,6},{6,2},{2,0},{1,5},{5,9},... | collective-permute-start | bytes 1572872 | tf_op jit(solution)/shard_map/ppermute | solution.py:475
  95.1 10.7 %collective-permute-start.24 = (bf16[80,256]{1,0:T(8,128)(2,1)S(1)}, bf16[80,256]{1,0:T(8,128)(2,1)S(1)}, u32[]{:S(2)}, u32[]{:S(2)}) collective-permute-start(bf16[80,256]{1,0:T(8,128)(2,1)S(1)} %add_convert_fusion.7.refs_0_), channel_id=1, source_target_pairs={{0,6},{2,4},{4,2},{6,0},{8,14},{10,12},{12,10},{14,8},{1,7},{3,5},... | collective-permute-start | bytes 122888 | tf_op jit(solution)/shard_map/ppermute | solution.py:435
  96.9 9.0 %collective-permute-start.23 = (bf16[80,256]{1,0:T(8,128)(2,1)S(1)}, bf16[80,256]{1,0:T(8,128)(2,1)S(1)}, u32[]{:S(2)}, u32[]{:S(2)}) collective-permute-start(bf16[80,256]{1,0:T(8,128)(2,1)S(1)} %add_convert_fusion.7.refs_0_), channel_id=1, source_target_pairs={{0,4},{2,6},{4,0},{6,2},{8,12},{10,14},{12,8},{14,10},{1,5},{3,7},... | collective-permute-start | bytes 122888 | tf_op jit(solution)/shard_map/ppermute | solution.py:435
  97.3 8.6 %collective-permute-start.22 = (bf16[80,256]{1,0:T(8,128)(2,1)S(1)}, bf16[80,256]{1,0:T(8,128)(2,1)S(1)}, u32[]{:S(2)}, u32[]{:S(2)}) collective-permute-start(bf16[80,256]{1,0:T(8,128)(2,1)S(1)} %add_convert_fusion.7.refs_0_), channel_id=1, source_target_pairs={{0,2},{2,0},{4,6},{6,4},{8,10},{10,8},{12,14},{14,12},{1,3},{3,1},... | collective-permute-start | bytes 122888 | tf_op jit(solution)/shard_map/ppermute | solution.py:435
  100.4 11.5 %collective-permute-start.26 = (bf16[1024,256]{1,0:T(8,128)(2,1)S(1)}, bf16[1024,256]{1,0:T(8,128)(2,1)S(1)}, u32[]{:S(2)}, u32[]{:S(2)}) collective-permute-start(bf16[1024,256]{1,0:T(8,128)(2,1)S(1)} %get-tuple-element.187), channel_id=1, source_target_pairs={{4,0},{8,4},{12,8},{14,12},{10,14},{6,10},{2,6},{0,2},{5,1},{9,5},... | collective-permute-start | bytes 1572872 | tf_op jit(solution)/shard_map/ppermute | solution.py:476
  102.4 10.0 %collective-permute-start.25 = (bf16[1024,256]{1,0:T(8,128)(2,1)S(1)}, bf16[1024,256]{1,0:T(8,128)(2,1)S(1)}, u32[]{:S(2)}, u32[]{:S(2)}) collective-permute-start(bf16[1024,256]{1,0:T(8,128)(2,1)S(1)} %get-tuple-element.186), channel_id=1, source_target_pairs={{0,4},{4,8},{8,12},{12,14},{14,10},{10,6},{6,2},{2,0},{1,5},{5,9},... | collective-permute-start | bytes 1572872 | tf_op jit(solution)/shard_map/ppermute | solution.py:475
  (14 other events, 57.3 us)

commit v4 on v3

--- a/solution.py
+++ b/solution.py
@@ -8,7 +8,8 @@
 from jax.experimental.pallas import tpu as pltpu
 from jax.sharding import PartitionSpec as P
 
-VMEM_LIMIT = 14 * 1024 * 1024
+VMEM_LIMIT = 20 * 1024 * 1024
+LAYER_BLOCK = 1024
 BRIEF = pl.CostEstimate(flops=1024, bytes_accessed=1024, transcendentals=0)
 GELU_C = math.sqrt(2.0 / math.pi)
 F32 = jnp.float32
@@ -37,15 +38,11 @@
 def fill_tiles(table_ref, masks_ref, block_rows, first_col, cols, row_of, tiles, dst):
     test = bit_tests()
 
-    def one_column(c, carry):
+    for c in range(cols):
         base = (first_col + c) * block_rows
-        start = pl.multiple_of(c * 128, 128)
         for r in range(tiles):
             tile = unpack_tile(masks_ref, table_ref[base + row_of(r)], test)
-            dst[pl.ds(start, 128), 128 * r : 128 * r + 128] = tile
-        return carry
-
-    lax.fori_loop(0, cols, one_column, 0)
+            dst[128 * c : 128 * c + 128, 128 * r : 128 * r + 128] = tile
 
 
 def vmem_spec():
@@ -173,54 +170,45 @@
 
 
 def middle_kernel(
-    agg_ref, other_ref, div_ref, own_ref, og_ref, wn_ref,
+    blk, agg_ref, other_ref, div_ref, own_ref, og_ref, wn_ref,
     mean_ref, out_ref, gb_ref, mg_ref, bias_ref,
 ):
-    div = div_ref[...]
-    rows = div.shape[1]
-    width = own_ref.shape[1]
-    mean = ((agg_ref[...] + other_ref[...].astype(F32)) / div).T.astype(BF16)
-    mean_ref[...] = mean
-    pre = own_ref[...] + jnp.dot(mean, wn_ref[...], preferred_element_type=F32)
-    square = pre * pre
-    bent = jnp.tanh(GELU_C * (pre + 0.044715 * (square * pre)))
-    half = 0.5 * (1.0 + bent)
-    out_ref[...] = (pre * half).astype(BF16)
-    slope = half + 0.5 * pre * (1.0 - bent * bent) * (GELU_C * (1.0 + 3.0 * 0.044715 * square))
-    pre_grad = og_ref[...] * slope
-    grad_b = pre_grad.astype(BF16)
-    gb_ref[...] = grad_b
-    div_column = jnp.broadcast_to(div, (128, rows)).T
-    div_full = jnp.concatenate([div_column] * (width // 128), axis=1)
-    mean_grad = lax.dot_general(
-        grad_b, wn_ref[...], (((1,), (1,)), ((), ())), preferred_element_type=F32
-    )
-    mg_ref[...] = (mean_grad / div_full).astype(BF16)
-    part = jnp.sum(pre_grad.reshape(rows // 64, 64, width), axis=0)
-
-    @pl.when(pl.program_id(0) == 0)
-    def _():
-        bias_ref[...] = part
-
-    @pl.when(pl.program_id(0) != 0)
-    def _():
-        bias_ref[...] += part
-
-
-def middle(agg, other, divisor, own, og, wn):
+    rows, width = own_ref.shape
+    bias_ref[...] = jnp.zeros_like(bias_ref)
+
+    def block(i, carry):
+        here = pl.ds(pl.multiple_of(i * blk, blk), blk)
+        div = div_ref[:, here]
+        mean = ((agg_ref[:, here] + other_ref[:, here].astype(F32)) / div).T.astype(BF16)
+        mean_ref[here] = mean
+        pre = own_ref[here] + jnp.dot(mean, wn_ref[...], preferred_element_type=F32)
+        square = pre * pre
+        bent = jnp.tanh(GELU_C * (pre + 0.044715 * (square * pre)))
+        half = 0.5 * (1.0 + bent)
+        out_ref[here] = (pre * half).astype(BF16)
+        slope = half + 0.5 * pre * (1.0 - bent * bent) * (GELU_C * (1.0 + 3.0 * 0.044715 * square))
+        pre_grad = og_ref[here] * slope
+        grad_b = pre_grad.astype(BF16)
+        gb_ref[here] = grad_b
+        div_column = jnp.broadcast_to(div, (128, blk)).T
+        div_full = jnp.concatenate([div_column] * (width // 128), axis=1)
+        mean_grad = lax.dot_general(
+            grad_b, wn_ref[...], (((1,), (1,)), ((), ())), preferred_element_type=F32
+        )
+        mg_ref[here] = (mean_grad / div_full).astype(BF16)
+        bias_ref[...] += jnp.sum(pre_grad.reshape(blk // 64, 64, width), axis=0)
+        return carry
+
+    lax.fori_loop(0, rows // blk, block, 0)
+
+
+def middle(agg, other, divisor, own, og, wn, blk=LAYER_BLOCK):
     rows, width = own.shape
-    blk = 256
-    turned = pl.BlockSpec((width, blk), lambda i: (0, i))
-    plain = pl.BlockSpec((blk, width), lambda i: (i, 0))
-    weight = pl.BlockSpec((width, width), lambda i: (0, 0))
     act = jax.ShapeDtypeStruct((rows, width), BF16)
     return pl.pallas_call(
-        middle_kernel,
-        grid=(rows // blk,),
-        in_specs=[
-            turned, turned, pl.BlockSpec((1, blk), lambda i: (0, i)), plain, plain, weight,
-        ],
-        out_specs=[plain] * 4 + [pl.BlockSpec((64, width), lambda i: (0, 0))],
+        partial(middle_kernel, blk),
+        in_specs=[vmem_spec()] * 6,
+        out_specs=[vmem_spec()] * 5,
         out_shape=[act] * 4 + [jax.ShapeDtypeStruct((64, width), F32)],
         compiler_params=pltpu.CompilerParams(vmem_limit_bytes=VMEM_LIMIT),
         cost_estimate=BRIEF,
@@ -383,8 +371,8 @@
     degree = lax.dynamic_index_in_dim(degree, side, 0, False) + sent_degree
     divisor = jnp.maximum(degree, 1.0)
 
-    forward = partial(forward_mm, ids=ids, table=table, masks=masks, block_rows=block_rows, tblk=1024)
     row_total = block_rows * 128
+    forward = partial(forward_mm, ids=ids, table=table, masks=masks, block_rows=block_rows, tblk=row_total)
     from_left = from_right = node_features
     pieces, cols, acc = [node_features], [(0, 0)], None
     early = (node_features, weight_self, bias_term, out_grad, ids, divisor)
@@ -451,11 +439,11 @@
         return [keep, lax.ppermute(send, "col", swap)]
 
     def add_all(b, parts):
-        quarter = parts[0] + parts[1]
+        quarter = (parts[0].astype(F32) + parts[1].astype(F32)).astype(BF16)
         return [quarter, lax.ppermute(quarter, "row", [(r, r ^ (1 << b)) for r in range(n)])]
 
     def from_quad(parts):
-        quarter = (parts[0] + parts[1]).astype(BF16)
+        quarter = (parts[0].astype(F32) + parts[1].astype(F32)).astype(BF16)
         return [quarter] + to_quad([(x, quarter) for x in (1, 2, 3)])
 
     spread = [[] for _ in range(far)]

time: 114 us -> 110 us (0.965)
  Pallas kernels: 53.2 us -> 40.9 us
  waiting for transfers between devices: 19.3 us -> 28.3 us
    pallas_call x4, Pallas kernels: 20.6 us -> 14.5 us  [forward_mm(): pl.pallas_call(partial(forward_kernel, tuple(cols), side_at, block_rows,...]
    pallas_call x4, Pallas kernels: 19.2 us -> 14.1 us  [backward_mm(): pl.pallas_call(partial(backward_kernel, tuple(cols), tuple(sides), block_...]
    ppermute x3, waiting for transfers between devices: 6.74 us -> 11.1 us  [local(): next_left = lax.ppermute(from_left, 'row', clockwise)]
    ppermute x4, waiting for transfers between devices: 7.82 us -> 11.1 us  [local(): left = lax.ppermute(left, 'row', counter)]
    ppermute x4, starting transfers between devices: 5.44 us -> 2.81 us  [local(): left = lax.ppermute(left, 'row', counter)]
    ppermute x4, starting transfers between devices: 2.87 us -> 5.5 us  [local(): right = lax.ppermute(right, 'row', clockwise)]
    ppermute x1, waiting for transfers between devices: 0.02 us -> 1.56 us  [local(): next_right = lax.ppermute(from_right[half:], 'row', counter)]
  transfers between devices with their start and end apart: 28 -> 28, of which waited for: 12 -> 13; matrix products, arithmetic and copies ran while one was open for 5% -> 5% of each run, Pallas kernels for 42% -> 33%
where the time goes in v4:
time: 110 us
  Pallas kernels  40.9 us (37%)
  waiting for transfers between devices  28.3 us (26%)
  starting transfers between devices  27.9 us (25%)
  local copies, waits for them, and re-layouts  5.74 us (5%)
  other arithmetic  4.9 us (4%)
  between operations  1.7 us (2%)
    pallas_call x4, Pallas kernels, forward_mm(): pl.pallas_call(partial(forward_kernel, tuple(cols), side_at, block_rows,...  14.5 us
    pallas_call x4, Pallas kernels, backward_mm(): pl.pallas_call(partial(backward_kernel, tuple(cols), tuple(sides), block_...  14.1 us
    ppermute x3, waiting for transfers between devices, local(): next_left = lax.ppermute(from_left, 'row', clockwise)  11.1 us
    ppermute x4, waiting for transfers between devices, local(): left = lax.ppermute(left, 'row', counter)  11.1 us
    ppermute x6, starting transfers between devices, to_quad(): lax.ppermute(part, axis, [(r, r ^ x) for r in range(n)])  7.11 us
    ppermute x3, starting transfers between devices, local(): next_left = lax.ppermute(from_left, 'row', clockwise)  6.35 us
    ppermute x4, starting transfers between devices, local(): right = lax.ppermute(right, 'row', clockwise)  5.5 us
    unnamed x20, local copies, waits for them, and re-layouts  4.94 us
  transfers between devices with their start and end apart: 28, of which 13 were waited for; matrix products, arithmetic and copies ran while one was open for 5% of the time, Pallas kernels for 33%

profile of v4, /device:TPU:0, one launch (start us, length us, event | category | flops | bytes accessed | tf_op | source)
XLA Modules:
  0.0 110.2 jit_solution(7656840964871218738)
XLA Ops:
  0.7 3.1 %collective-permute-start = (bf16[1024,256]{1,0:T(8,128)(2,1)}, bf16[1024,256]{1,0:T(8,128)(2,1)S(1)}, u32[]{:S(2)}, u32[]{:S(2)}) collective-permute-start(bf16[1024,256]{1,0:T(8,128)(2,1)} %x_ref), channel_id=1, source_target_pairs={{0,4},{4,8},{8,12},{12,14},{14,10},{10,6},{6,2},{2,0},{1,5},{5,9},... | collective-permute-start | bytes 1572872 | tf_op jit(solution)/shard_map/ppermute | solution.py:381
  5.1 2.0 %popcnt_reduce_fusion = s32[384,128]{1,0:T(8,128)S(1)} fusion(s32[1,1,384,128,8]{3,4,2,1,0:T(8,128)} %param.13), kind=kLoop, calls=%fused_computation | loop fusion | flops 737280 | bytes 1769472 | tf_op jit(solution)/shard_map/reduce_sum | solution.py:367
  9.4 2.4 %forward_step.4.refs_2_ = f32[256,2048]{1,0:T(8,128)S(1)} custom-call(s32[14]{0:T(128)S(1)} %fusion.7.ids_ref, s32[1024]{0:T(1024)S(1)} %select_reduce_fusion.table_ref, s32[384,8,128]{2,1,0:T(8,128)S(1)} %bitcast.20, bf16[1024,256]{1,0:T(8,128)(2,1)S(1)} %copy-done.4), custom_call_target="tpu_custom_call" | custom-call | flops 1024 | bytes 1024 | tf_op jit(solution)/shard_map/forward_step/pallas_call | solution.py:89
  13.2 2.6 %collective-permute-done.refs_0_ = bf16[1024,256]{1,0:T(8,128)(2,1)S(1)} collective-permute-done((bf16[1024,256]{1,0:T(8,128)(2,1)}, bf16[1024,256]{1,0:T(8,128)(2,1)S(1)}, u32[]{:S(2)}, u32[]{:S(2)}) %collective-permute-start) | collective-permute-done | bytes 524320 | tf_op jit(solution)/shard_map/ppermute | solution.py:381
  15.8 1.8 %collective-permute-start.3 = (bf16[1024,256]{1,0:T(8,128)(2,1)S(1)}, bf16[1024,256]{1,0:T(8,128)(2,1)S(1)}, u32[]{:S(2)}, u32[]{:S(2)}) collective-permute-start(bf16[1024,256]{1,0:T(8,128)(2,1)S(1)} %collective-permute-done.refs_0_), channel_id=1, source_target_pairs={{0,4},{4,8},{8,12},{12,14},{14,10},{10,6},{6,2},{2,0},{1,5},{5,9},... | collective-permute-start | bytes 1572872 | tf_op jit(solution)/shard_map/ppermute | solution.py:381
  17.9 1.6 %copy-done.3 = f32[256,2048]{1,0:T(8,128)S(1)} copy-done((f32[256,2048]{1,0:T(8,128)S(1)}, f32[256,2048]{1,0:T(8,128)}, u32[]{:S(2)}) %copy-start.3) | copy-done | bytes 2097176
  19.4 4.0 %forward_step.5.refs_2_ = f32[256,2048]{1,0:T(8,128)S(1)} custom-call(s32[14]{0:T(128)S(1)} %fusion.7.ids_ref, s32[1024]{0:T(1024)S(1)} %select_reduce_fusion.table_ref, s32[384,8,128]{2,1,0:T(8,128)S(1)} %bitcast.21, bf16[1024,256]{1,0:T(8,128)(2,1)S(1)} %collective-permute-done.refs_0_, bf16[1024,256]{1,0:T(8,128)(2,1)S(1)} %collective-permute-done.2.refs_1_, ...), custom_call_target="tpu_custom_call" | custom-call | flops 1024 | bytes 1024 | tf_op jit(solution)/shard_map/forward_step/pallas_call | solution.py:89
  23.5 1.7 %far_tiles.1.tiles_ref = bf16[1024,2048]{1,0:T(8,128)(2,1)S(1)} custom-call(s32[14]{0:T(128)S(1)} %fusion.7.ids_ref, s32[1024]{0:T(1024)S(1)} %select_reduce_fusion.table_ref, s32[384,8,128]{2,1,0:T(8,128)S(1)} %bitcast.22), custom_call_target="tpu_custom_call" | custom-call | flops 1024 | bytes 1024 | tf_op jit(solution)/shard_map/far_tiles/pallas_call | solution.py:112
  26.5 2.4 %collective-permute-done.3.refs_0_ = bf16[1024,256]{1,0:T(8,128)(2,1)S(1)} collective-permute-done((bf16[1024,256]{1,0:T(8,128)(2,1)S(1)}, bf16[1024,256]{1,0:T(8,128)(2,1)S(1)}, u32[]{:S(2)}, u32[]{:S(2)}) %collective-permute-start.3) | collective-permute-done | bytes 524320 | tf_op jit(solution)/shard_map/ppermute | solution.py:381
  31.0 4.0 %forward_step.6.refs_2_ = f32[256,2048]{1,0:T(8,128)S(1)} custom-call(s32[14]{0:T(128)S(1)} %fusion.7.ids_ref, s32[1024]{0:T(1024)S(1)} %select_reduce_fusion.table_ref, s32[384,8,128]{2,1,0:T(8,128)S(1)} %bitcast.23, bf16[1024,256]{1,0:T(8,128)(2,1)S(1)} %collective-permute-done.3.refs_0_, bf16[1024,256]{1,0:T(8,128)(2,1)S(1)} %collective-permute-done.4.refs_1_, ...), custom_call_target="tpu_custom_call" | custom-call | flops 1024 | bytes 1024 | tf_op jit(solution)/shard_map/forward_step/pallas_call | solution.py:89
  35.0 6.1 %collective-permute-done.5.refs_0_ = bf16[1024,256]{1,0:T(8,128)(2,1)S(1)} collective-permute-done((bf16[1024,256]{1,0:T(8,128)(2,1)S(1)}, bf16[1024,256]{1,0:T(8,128)(2,1)S(1)}, u32[]{:S(2)}, u32[]{:S(2)}) %collective-permute-start.5) | collective-permute-done | bytes 524320 | tf_op jit(solution)/shard_map/ppermute | solution.py:381
  43.5 4.0 %forward_step.7.acc_ref = f32[256,2048]{1,0:T(8,128)S(1)} custom-call(s32[14]{0:T(128)S(1)} %fusion.7.ids_ref, s32[1024]{0:T(1024)S(1)} %select_reduce_fusion.table_ref, s32[384,8,128]{2,1,0:T(8,128)S(1)} %bitcast.24, bf16[1024,256]{1,0:T(8,128)(2,1)S(1)} %collective-permute-done.5.refs_0_, bf16[1024,256]{1,0:T(8,128)(2,1)S(1)} %collective-permute-done.6.refs_1_, ...), custom_call_target="tpu_custom_call" | custom-call | flops 1024 | bytes 1024 | tf_op jit(solution)/shard_map/forward_step/pallas_call | solution.py:89
  47.6 1.6 %collective-permute-done.8.high_ref = bf16[512,256]{1,0:T(8,128)(2,1)S(1)} collective-permute-done((bf16[512,256]{1,0:T(8,128)(2,1)S(1)}, bf16[512,256]{1,0:T(8,128)(2,1)S(1)}, u32[]{:S(2)}, u32[]{:S(2)}) %collective-permute-start.8) | collective-permute-done | bytes 262176 | tf_op jit(solution)/shard_map/ppermute | solution.py:386
  52.4 1.9 %layer.1 = (bf16[1024,256]{1,0:T(8,128)(2,1)S(1)}, bf16[1024,256]{1,0:T(8,128)(2,1)}, bf16[1024,256]{1,0:T(8,128)(2,1)S(1)}, bf16[1024,256]{1,0:T(8,128)(2,1)S(1)}, f32[64,256]{1,0:T(8,128)S(1)}) custom-call(f32[256,1024]{1,0:T(8,128)S(1)} %forward_keep.1.agg_ref, bf16[256,1024]{1,0:T(8,128)(2,1)S(1)} %collective-permute-done.9.other_ref, ...), custom_call_target="tpu_custom_call" | custom-call | flops 1024 | bytes 1024 | tf_op jit(solution)/shard_map/layer/pallas_call | solution.py:208
  59.6 3.9 %backward_step.3 = bf16[2048,256]{1,0:T(8,128)(2,1)S(1)} custom-call(s32[14]{0:T(128)S(1)} %fusion.7.ids_ref, s32[1024]{0:T(1024)S(1)} %select_reduce_fusion.table_ref, s32[384,8,128]{2,1,0:T(8,128)S(1)} %bitcast.25, bf16[1024,256]{1,0:T(8,128)(2,1)S(1)} %get-tuple-element.178.grad_ref.after_ref.refs_0_, ...), custom_call_target="tpu_custom_call" | custom-call | flops 8589934592 | bytes 3670016 | tf_op jit(solution)/shard_map/backward_step/pallas_call | solution.py:251
  70.5 4.0 %backward_step.4 = bf16[2048,256]{1,0:T(8,128)(2,1)S(1)} custom-call(s32[14]{0:T(128)S(1)} %fusion.7.ids_ref, s32[1024]{0:T(1024)S(1)} %select_reduce_fusion.table_ref, s32[384,8,128]{2,1,0:T(8,128)S(1)} %bitcast.26, bf16[1024,256]{1,0:T(8,128)(2,1)S(1)} %get-tuple-element.178.grad_ref.after_ref.refs_0_, ...), custom_call_target="tpu_custom_call" | custom-call | flops 8589934592 | bytes 3670016 | tf_op jit(solution)/shard_map/backward_step/pallas_call | solution.py:251
  76.4 2.7 %collective-permute-start.19 = (bf16[80,256]{1,0:T(8,128)(2,1)S(1)}, bf16[80,256]{1,0:T(8,128)(2,1)S(1)}, u32[]{:S(2)}, u32[]{:S(2)}) collective-permute-start(bf16[80,256]{1,0:T(8,128)(2,1)S(1)} %add_convert_fusion.8), channel_id=1, source_target_pairs={{0,8},{2,10},{4,12},{6,14},{8,0},{10,2},{12,4},{14,6},{1,9},{3,11}... | collective-permute-start | bytes 122888 | tf_op jit(solution)/shard_map/ppermute | solution.py:443
  79.1 4.4 %collective-permute-done.17 = bf16[1024,256]{1,0:T(8,128)(2,1)S(1)} collective-permute-done((bf16[1024,256]{1,0:T(8,128)(2,1)S(1)}, bf16[1024,256]{1,0:T(8,128)(2,1)S(1)}, u32[]{:S(2)}, u32[]{:S(2)}) %collective-permute-start.17) | collective-permute-done | bytes 524320 | tf_op jit(solution)/shard_map/ppermute | solution.py:464
  84.3 1.6 %collective-permute-start.20 = (bf16[1024,256]{1,0:T(8,128)(2,1)S(1)}, bf16[1024,256]{1,0:T(8,128)(2,1)S(1)}, u32[]{:S(2)}, u32[]{:S(2)}) collective-permute-start(bf16[1024,256]{1,0:T(8,128)(2,1)S(1)} %get-tuple-element.176), channel_id=1, source_target_pairs={{0,4},{4,8},{8,12},{12,14},{14,10},{10,6},{6,2},{2,0},{1,5},{5,9},... | collective-permute-start | bytes 1572872 | tf_op jit(solution)/shard_map/ppermute | solution.py:463
  85.9 4.0 %backward_step.5 = bf16[2048,256]{1,0:T(8,128)(2,1)S(1)} custom-call(s32[14]{0:T(128)S(1)} %fusion.7.ids_ref, s32[1024]{0:T(1024)S(1)} %select_reduce_fusion.table_ref, s32[384,8,128]{2,1,0:T(8,128)S(1)} %bitcast.27, bf16[1024,256]{1,0:T(8,128)(2,1)S(1)} %get-tuple-element.178.grad_ref.after_ref.refs_0_, ...), custom_call_target="tpu_custom_call" | custom-call | flops 8589934592 | bytes 3670016 | tf_op jit(solution)/shard_map/backward_step/pallas_call | solution.py:251
  91.8 1.6 %collective-permute-start.22 = (bf16[80,256]{1,0:T(8,128)(2,1)S(1)}, bf16[80,256]{1,0:T(8,128)(2,1)S(1)}, u32[]{:S(2)}, u32[]{:S(2)}) collective-permute-start(bf16[80,256]{1,0:T(8,128)(2,1)S(1)} %add_convert_fusion.7.refs_0_), channel_id=1, source_target_pairs={{0,2},{2,0},{4,6},{6,4},{8,10},{10,8},{12,14},{14,12},{1,3},{3,1},... | collective-permute-start | bytes 122888 | tf_op jit(solution)/shard_map/ppermute | solution.py:423
  93.4 3.5 %collective-permute-done.21 = bf16[1024,256]{1,0:T(8,128)(2,1)S(1)} collective-permute-done((bf16[1024,256]{1,0:T(8,128)(2,1)S(1)}, bf16[1024,256]{1,0:T(8,128)(2,1)S(1)}, u32[]{:S(2)}, u32[]{:S(2)}) %collective-permute-start.21) | collective-permute-done | bytes 524320 | tf_op jit(solution)/shard_map/ppermute | solution.py:464
  99.7 2.2 %backward_own.1 = f32[1024,256]{1,0:T(8,128)S(1)} custom-call(s32[14]{0:T(128)S(1)} %fusion.7.ids_ref, s32[1024]{0:T(1024)S(1)} %select_reduce_fusion.table_ref, s32[384,8,128]{2,1,0:T(8,128)S(1)} %bitcast.28, bf16[1024,256]{1,0:T(8,128)(2,1)S(1)} %get-tuple-element.178.grad_ref.after_ref.refs_0_, ...), custom_call_target="tpu_custom_call" | custom-call | flops 4294967296 | bytes 2621440 | tf_op jit(solution)/shard_map/backward_own/pallas_call | solution.py:251
  105.7 3.1 %collective-permute-done.26 = bf16[1024,256]{1,0:T(8,128)(2,1)S(1)} collective-permute-done((bf16[1024,256]{1,0:T(8,128)(2,1)S(1)}, bf16[1024,256]{1,0:T(8,128)(2,1)S(1)}, u32[]{:S(2)}, u32[]{:S(2)}) %collective-permute-start.26) | collective-permute-done | bytes 524320 | tf_op jit(solution)/shard_map/ppermute | solution.py:464
  (93 shorter events, 38.2 us)
Async XLA Ops:
  0.7 15.2 %collective-permute-start = (bf16[1024,256]{1,0:T(8,128)(2,1)}, bf16[1024,256]{1,0:T(8,128)(2,1)S(1)}, u32[]{:S(2)}, u32[]{:S(2)}) collective-permute-start(bf16[1024,256]{1,0:T(8,128)(2,1)} %x_ref), channel_id=1, source_target_pairs={{0,4},{4,8},{8,12},{12,14},{14,10},{10,6},{6,2},{2,0},{1,5},{5,9},... | collective-permute-start | bytes 1572872 | tf_op jit(solution)/shard_map/ppermute | solution.py:381
  3.7 13.9 %collective-permute-start.2 = (bf16[1024,256]{1,0:T(8,128)(2,1)}, bf16[1024,256]{1,0:T(8,128)(2,1)S(1)}, u32[]{:S(2)}, u32[]{:S(2)}) collective-permute-start(bf16[1024,256]{1,0:T(8,128)(2,1)} %x_ref), channel_id=1, source_target_pairs={{4,0},{8,4},{12,8},{14,12},{10,14},{6,10},{2,6},{0,2},{5,1},{9,5},... | collective-permute-start | bytes 1572872 | tf_op jit(solution)/shard_map/ppermute | solution.py:382
  7.3 5.9 %collective-permute-start.1 = (f32[1,1024]{1,0:T(1,128)S(1)}, f32[1,1024]{1,0:T(1,128)S(1)}, u32[]{:S(2)}, u32[]{:S(2)}) collective-permute-start(f32[1,1024]{1,0:T(1,128)S(1)} %dynamic-slice_bitcast_fusion), channel_id=1, source_target_pairs={{0,1},{1,0},{2,3},{3,2},{4,5},{5,4},{6,7},{7,6},{8,9},{9,8},{10,11... | collective-permute-start | bytes 12296 | tf_op jit(solution)/shard_map/ppermute | solution.py:370
  15.8 13.1 %collective-permute-start.3 = (bf16[1024,256]{1,0:T(8,128)(2,1)S(1)}, bf16[1024,256]{1,0:T(8,128)(2,1)S(1)}, u32[]{:S(2)}, u32[]{:S(2)}) collective-permute-start(bf16[1024,256]{1,0:T(8,128)(2,1)S(1)} %collective-permute-done.refs_0_), channel_id=1, source_target_pairs={{0,4},{4,8},{8,12},{12,14},{14,10},{10,6},{6,2},{2,0},{1,5},{5,9},... | collective-permute-start | bytes 1572872 | tf_op jit(solution)/shard_map/ppermute | solution.py:381
  17.6 12.8 %collective-permute-start.4 = (bf16[1024,256]{1,0:T(8,128)(2,1)S(1)}, bf16[1024,256]{1,0:T(8,128)(2,1)S(1)}, u32[]{:S(2)}, u32[]{:S(2)}) collective-permute-start(bf16[1024,256]{1,0:T(8,128)(2,1)S(1)} %collective-permute-done.2.refs_1_), channel_id=1, source_target_pairs={{4,0},{8,4},{12,8},{14,12},{10,14},{6,10},{2,6},{0,2},{5,1},{9,5},... | collective-permute-start | bytes 1572872 | tf_op jit(solution)/shard_map/ppermute | solution.py:382
  28.9 12.2 %collective-permute-start.5 = (bf16[1024,256]{1,0:T(8,128)(2,1)S(1)}, bf16[1024,256]{1,0:T(8,128)(2,1)S(1)}, u32[]{:S(2)}, u32[]{:S(2)}) collective-permute-start(bf16[1024,256]{1,0:T(8,128)(2,1)S(1)} %collective-permute-done.3.refs_0_), channel_id=1, source_target_pairs={{0,4},{4,8},{8,12},{12,14},{14,10},{10,6},{6,2},{2,0},{1,5},{5,9},... | collective-permute-start | bytes 1572872 | tf_op jit(solution)/shard_map/ppermute | solution.py:381
  30.4 12.1 %collective-permute-start.6 = (bf16[1024,256]{1,0:T(8,128)(2,1)S(1)}, bf16[1024,256]{1,0:T(8,128)(2,1)S(1)}, u32[]{:S(2)}, u32[]{:S(2)}) collective-permute-start(bf16[1024,256]{1,0:T(8,128)(2,1)S(1)} %collective-permute-done.4.refs_1_), channel_id=1, source_target_pairs={{4,0},{8,4},{12,8},{14,12},{10,14},{6,10},{2,6},{0,2},{5,1},{9,5},... | collective-permute-start | bytes 1572872 | tf_op jit(solution)/shard_map/ppermute | solution.py:382
  41.1 6.4 %collective-permute-start.7 = (bf16[512,256]{1,0:T(8,128)(2,1)S(1)}, bf16[512,256]{1,0:T(8,128)(2,1)S(1)}, u32[]{:S(2)}, u32[]{:S(2)}) collective-permute-start(bf16[512,256]{1,0:T(8,128)(2,1)S(1)} %slice.30), channel_id=1, source_target_pairs={{0,4},{4,8},{8,12},{12,14},{14,10},{10,6},{6,2},{2,0},{1,5},{5,9},... | collective-permute-start | bytes 786440 | tf_op jit(solution)/shard_map/ppermute | solution.py:385
  42.5 6.6 %collective-permute-start.8 = (bf16[512,256]{1,0:T(8,128)(2,1)S(1)}, bf16[512,256]{1,0:T(8,128)(2,1)S(1)}, u32[]{:S(2)}, u32[]{:S(2)}) collective-permute-start(bf16[512,256]{1,0:T(8,128)(2,1)S(1)} %slice.31), channel_id=1, source_target_pairs={{4,0},{8,4},{12,8},{14,12},{10,14},{6,10},{2,6},{0,2},{5,1},{9,5},... | collective-permute-start | bytes 786440 | tf_op jit(solution)/shard_map/ppermute | solution.py:386
  57.6 10.7 %collective-permute-start.12 = (bf16[512,256]{1,0:T(8,128)(2,1)S(1)}, bf16[512,256]{1,0:T(8,128)(2,1)S(1)}, u32[]{:S(2)}, u32[]{:S(2)}) collective-permute-start(bf16[512,256]{1,0:T(8,128)(2,1)S(1)} %get-tuple-element.149), channel_id=1, source_target_pairs={{4,0},{8,4},{12,8},{14,12},{10,14},{6,10},{2,6},{0,2},{5,1},{9,5},... | collective-permute-start | bytes 786440 | tf_op jit(solution)/shard_map/ppermute | solution.py:464
  58.3 9.9 %collective-permute-start.11 = (bf16[512,256]{1,0:T(8,128)(2,1)S(1)}, bf16[512,256]{1,0:T(8,128)(2,1)S(1)}, u32[]{:S(2)}, u32[]{:S(2)}) collective-permute-start(bf16[512,256]{1,0:T(8,128)(2,1)S(1)} %get-tuple-element.146), channel_id=1, source_target_pairs={{0,4},{4,8},{8,12},{12,14},{14,10},{10,6},{6,2},{2,0},{1,5},{5,9},... | collective-permute-start | bytes 786440 | tf_op jit(solution)/shard_map/ppermute | solution.py:463
  64.7 9.8 %collective-permute-start.13 = (bf16[144,256]{1,0:T(8,128)(2,1)S(1)}, bf16[144,256]{1,0:T(8,128)(2,1)S(1)}, u32[]{:S(2)}, u32[]{:S(2)}) collective-permute-start(bf16[144,256]{1,0:T(8,128)(2,1)S(1)} %get-tuple-element.157), channel_id=1, source_target_pairs={{0,2},{2,0},{4,6},{6,4},{8,10},{10,8},{12,14},{14,12},{1,3},{3,1},... | collective-permute-start | bytes 221192 | tf_op jit(solution)/shard_map/ppermute | solution.py:423
  65.5 9.0 %collective-permute-start.14 = (bf16[144,256]{1,0:T(8,128)(2,1)S(1)}, bf16[144,256]{1,0:T(8,128)(2,1)S(1)}, u32[]{:S(2)}, u32[]{:S(2)}) collective-permute-start(bf16[144,256]{1,0:T(8,128)(2,1)S(1)} %get-tuple-element.158), channel_id=1, source_target_pairs={{0,4},{2,6},{4,0},{6,2},{8,12},{10,14},{12,8},{14,10},{1,5},{3,7},... | collective-permute-start | bytes 221192 | tf_op jit(solution)/shard_map/ppermute | solution.py:423
  66.7 7.7 %collective-permute-start.15 = (bf16[144,256]{1,0:T(8,128)(2,1)S(1)}, bf16[144,256]{1,0:T(8,128)(2,1)S(1)}, u32[]{:S(2)}, u32[]{:S(2)}) collective-permute-start(bf16[144,256]{1,0:T(8,128)(2,1)S(1)} %get-tuple-element.159), channel_id=1, source_target_pairs={{0,6},{2,4},{4,2},{6,0},{8,14},{10,12},{12,10},{14,8},{1,7},{3,5},... | collective-permute-start | bytes 221192 | tf_op jit(solution)/shard_map/ppermute | solution.py:423
  68.4 15.1 %collective-permute-start.17 = (bf16[1024,256]{1,0:T(8,128)(2,1)S(1)}, bf16[1024,256]{1,0:T(8,128)(2,1)S(1)}, u32[]{:S(2)}, u32[]{:S(2)}) collective-permute-start(bf16[1024,256]{1,0:T(8,128)(2,1)S(1)} %get-tuple-element.165), channel_id=1, source_target_pairs={{4,0},{8,4},{12,8},{14,12},{10,14},{6,10},{2,6},{0,2},{5,1},{9,5},... | collective-permute-start | bytes 1572872 | tf_op jit(solution)/shard_map/ppermute | solution.py:464
  69.2 14.3 %collective-permute-start.16 = (bf16[1024,256]{1,0:T(8,128)(2,1)S(1)}, bf16[1024,256]{1,0:T(8,128)(2,1)S(1)}, u32[]{:S(2)}, u32[]{:S(2)}) collective-permute-start(bf16[1024,256]{1,0:T(8,128)(2,1)S(1)} %get-tuple-element.162), channel_id=1, source_target_pairs={{0,4},{4,8},{8,12},{12,14},{14,10},{10,6},{6,2},{2,0},{1,5},{5,9},... | collective-permute-start | bytes 1572872 | tf_op jit(solution)/shard_map/ppermute | solution.py:463
  76.4 13.4 %collective-permute-start.19 = (bf16[80,256]{1,0:T(8,128)(2,1)S(1)}, bf16[80,256]{1,0:T(8,128)(2,1)S(1)}, u32[]{:S(2)}, u32[]{:S(2)}) collective-permute-start(bf16[80,256]{1,0:T(8,128)(2,1)S(1)} %add_convert_fusion.8), channel_id=1, source_target_pairs={{0,8},{2,10},{4,12},{6,14},{8,0},{10,2},{12,4},{14,6},{1,9},{3,11}... | collective-permute-start | bytes 122888 | tf_op jit(solution)/shard_map/ppermute | solution.py:443
  83.8 13.2 %collective-permute-start.21 = (bf16[1024,256]{1,0:T(8,128)(2,1)S(1)}, bf16[1024,256]{1,0:T(8,128)(2,1)S(1)}, u32[]{:S(2)}, u32[]{:S(2)}) collective-permute-start(bf16[1024,256]{1,0:T(8,128)(2,1)S(1)} %get-tuple-element.179), channel_id=1, source_target_pairs={{4,0},{8,4},{12,8},{14,12},{10,14},{6,10},{2,6},{0,2},{5,1},{9,5},... | collective-permute-start | bytes 1572872 | tf_op jit(solution)/shard_map/ppermute | solution.py:464
  84.3 13.0 %collective-permute-start.20 = (bf16[1024,256]{1,0:T(8,128)(2,1)S(1)}, bf16[1024,256]{1,0:T(8,128)(2,1)S(1)}, u32[]{:S(2)}, u32[]{:S(2)}) collective-permute-start(bf16[1024,256]{1,0:T(8,128)(2,1)S(1)} %get-tuple-element.176), channel_id=1, source_target_pairs={{0,4},{4,8},{8,12},{12,14},{14,10},{10,6},{6,2},{2,0},{1,5},{5,9},... | collective-permute-start | bytes 1572872 | tf_op jit(solution)/shard_map/ppermute | solution.py:463
  89.9 12.4 %collective-permute-start.24 = (bf16[80,256]{1,0:T(8,128)(2,1)S(1)}, bf16[80,256]{1,0:T(8,128)(2,1)S(1)}, u32[]{:S(2)}, u32[]{:S(2)}) collective-permute-start(bf16[80,256]{1,0:T(8,128)(2,1)S(1)} %add_convert_fusion.7.refs_0_), channel_id=1, source_target_pairs={{0,6},{2,4},{4,2},{6,0},{8,14},{10,12},{12,10},{14,8},{1,7},{3,5},... | collective-permute-start | bytes 122888 | tf_op jit(solution)/shard_map/ppermute | solution.py:423
  91.0 11.3 %collective-permute-start.23 = (bf16[80,256]{1,0:T(8,128)(2,1)S(1)}, bf16[80,256]{1,0:T(8,128)(2,1)S(1)}, u32[]{:S(2)}, u32[]{:S(2)}) collective-permute-start(bf16[80,256]{1,0:T(8,128)(2,1)S(1)} %add_convert_fusion.7.refs_0_), channel_id=1, source_target_pairs={{0,4},{2,6},{4,0},{6,2},{8,12},{10,14},{12,8},{14,10},{1,5},{3,7},... | collective-permute-start | bytes 122888 | tf_op jit(solution)/shard_map/ppermute | solution.py:423
  91.8 10.5 %collective-permute-start.22 = (bf16[80,256]{1,0:T(8,128)(2,1)S(1)}, bf16[80,256]{1,0:T(8,128)(2,1)S(1)}, u32[]{:S(2)}, u32[]{:S(2)}) collective-permute-start(bf16[80,256]{1,0:T(8,128)(2,1)S(1)} %add_convert_fusion.7.refs_0_), channel_id=1, source_target_pairs={{0,2},{2,0},{4,6},{6,4},{8,10},{10,8},{12,14},{14,12},{1,3},{3,1},... | collective-permute-start | bytes 122888 | tf_op jit(solution)/shard_map/ppermute | solution.py:423
  97.6 11.1 %collective-permute-start.26 = (bf16[1024,256]{1,0:T(8,128)(2,1)S(1)}, bf16[1024,256]{1,0:T(8,128)(2,1)S(1)}, u32[]{:S(2)}, u32[]{:S(2)}) collective-permute-start(bf16[1024,256]{1,0:T(8,128)(2,1)S(1)} %get-tuple-element.187), channel_id=1, source_target_pairs={{4,0},{8,4},{12,8},{14,12},{10,14},{6,10},{2,6},{0,2},{5,1},{9,5},... | collective-permute-start | bytes 1572872 | tf_op jit(solution)/shard_map/ppermute | solution.py:464
  98.4 10.8 %collective-permute-start.25 = (bf16[1024,256]{1,0:T(8,128)(2,1)S(1)}, bf16[1024,256]{1,0:T(8,128)(2,1)S(1)}, u32[]{:S(2)}, u32[]{:S(2)}) collective-permute-start(bf16[1024,256]{1,0:T(8,128)(2,1)S(1)} %get-tuple-element.186), channel_id=1, source_target_pairs={{0,4},{4,8},{8,12},{12,14},{14,10},{10,6},{6,2},{2,0},{1,5},{5,9},... | collective-permute-start | bytes 1572872 | tf_op jit(solution)/shard_map/ppermute | solution.py:463
  (14 other events, 55.5 us)

commit v5 on v3

--- a/solution.py
+++ b/solution.py
@@ -37,15 +37,11 @@
 def fill_tiles(table_ref, masks_ref, block_rows, first_col, cols, row_of, tiles, dst):
     test = bit_tests()
 
-    def one_column(c, carry):
+    for c in range(cols):
         base = (first_col + c) * block_rows
-        start = pl.multiple_of(c * 128, 128)
         for r in range(tiles):
             tile = unpack_tile(masks_ref, table_ref[base + row_of(r)], test)
-            dst[pl.ds(start, 128), 128 * r : 128 * r + 128] = tile
-        return carry
-
-    lax.fori_loop(0, cols, one_column, 0)
+            dst[128 * c : 128 * c + 128, 128 * r : 128 * r + 128] = tile
 
 
 def vmem_spec():
@@ -89,15 +85,19 @@
     rows, width = pieces[0].shape
     count = len(pieces)
     args = [ids, table, masks] + list(pieces) + ([] if acc is None else [acc])
+    turned = (width, count * rows)
+    out_shape = [jax.ShapeDtypeStruct((width, out_rows), out_dtype)]
+    scratch = [pltpu.VMEM((count * rows, tblk), BF16)]
+    if acc is None:
+        out_shape.append(jax.ShapeDtypeStruct(turned, BF16))
+    else:
+        scratch.insert(0, pltpu.VMEM(turned, BF16))
     return pl.pallas_call(
         partial(forward_kernel, tuple(cols), side_at, block_rows, tblk, acc is not None),
         in_specs=[smem_spec(), smem_spec()] + [vmem_spec()] * (len(args) - 2),
-        out_specs=vmem_spec(),
-        scratch_shapes=[
-            pltpu.VMEM((width, count * rows), BF16),
-            pltpu.VMEM((count * rows, tblk), BF16),
-        ],
-        out_shape=jax.ShapeDtypeStruct((width, out_rows), out_dtype),
+        out_specs=[vmem_spec()] * len(out_shape),
+        scratch_shapes=scratch,
+        out_shape=out_shape,
         compiler_params=pltpu.CompilerParams(vmem_limit_bytes=VMEM_LIMIT),
         cost_estimate=BRIEF,
         name=name,
@@ -173,14 +173,13 @@
 
 
 def middle_kernel(
-    agg_ref, other_ref, div_ref, own_ref, og_ref, wn_ref,
-    mean_ref, out_ref, gb_ref, mg_ref, bias_ref,
+    at, ids_ref, agg_ref, other_ref, div_ref, own_ref, og_ref, wn_ref, xt_ref,
+    out_ref, gb_ref, mg_ref, keep_ref, send_ref,
 ):
+    rows, width = own_ref.shape
     div = div_ref[...]
-    rows = div.shape[1]
-    width = own_ref.shape[1]
-    mean = ((agg_ref[...] + other_ref[...].astype(F32)) / div).T.astype(BF16)
-    mean_ref[...] = mean
+    mean_turned = (agg_ref[...] + other_ref[...].astype(F32)) / div
+    mean = mean_turned.T.astype(BF16)
     pre = own_ref[...] + jnp.dot(mean, wn_ref[...], preferred_element_type=F32)
     square = pre * pre
     bent = jnp.tanh(GELU_C * (pre + 0.044715 * (square * pre)))
@@ -196,36 +195,28 @@
         grad_b, wn_ref[...], (((1,), (1,)), ((), ())), preferred_element_type=F32
     )
     mg_ref[...] = (mean_grad / div_full).astype(BF16)
-    part = jnp.sum(pre_grad.reshape(rows // 64, 64, width), axis=0)
-
-    @pl.when(pl.program_id(0) == 0)
-    def _():
-        bias_ref[...] = part
-
-    @pl.when(pl.program_id(0) != 0)
-    def _():
-        bias_ref[...] += part
-
-
-def middle(agg, other, divisor, own, og, wn):
+    own = jnp.dot(xt_ref[...], grad_b, preferred_element_type=F32)
+    neigh = jnp.dot(mean_turned.astype(BF16), grad_b, preferred_element_type=F32)
+    first = ids_ref[at] == 0
+    keep_ref[:width] = jnp.where(first, own, neigh)
+    send_ref[:width] = jnp.where(first, neigh, own)
+    bias = jnp.sum(pre_grad.reshape(rows // 64, 64, width), axis=0)
+    keep_ref[width:] = bias
+    send_ref[width:] = bias
+
+
+def middle(at, ids, agg, other, divisor, own, og, wn, x_turned):
     rows, width = own.shape
-    blk = 256
-    turned = pl.BlockSpec((width, blk), lambda i: (0, i))
-    plain = pl.BlockSpec((blk, width), lambda i: (i, 0))
-    weight = pl.BlockSpec((width, width), lambda i: (0, 0))
     act = jax.ShapeDtypeStruct((rows, width), BF16)
     return pl.pallas_call(
-        middle_kernel,
-        grid=(rows // blk,),
-        in_specs=[
-            turned, turned, pl.BlockSpec((1, blk), lambda i: (0, i)), plain, plain, weight,
-        ],
-        out_specs=[plain] * 4 + [pl.BlockSpec((64, width), lambda i: (0, 0))],
-        out_shape=[act] * 4 + [jax.ShapeDtypeStruct((64, width), F32)],
+        partial(middle_kernel, at),
+        in_specs=[smem_spec()] + [vmem_spec()] * 7,
+        out_specs=[vmem_spec()] * 5,
+        out_shape=[act] * 3 + [jax.ShapeDtypeStruct((width + 64, width), F32)] * 2,
         compiler_params=pltpu.CompilerParams(vmem_limit_bytes=VMEM_LIMIT),
         cost_estimate=BRIEF,
         name="layer",
-    )(agg, other, divisor, own, og, wn)
+    )(ids, agg, other, divisor, own, og, wn, x_turned)
 
 
 def backward_kernel(cols, sides, block_rows, has_acc, ids_ref, table_ref, masks_ref, after_ref, *refs):
@@ -292,31 +283,14 @@
     )(*args)
 
 
-def weight_kernel(at, ids_ref, x_ref, mean_ref, gb_ref, bias_ref, own_ref, *rest):
-    sends, sums = rest[:3], rest[3]
-    width = gb_ref.shape[1]
-    grad = gb_ref[...]
-    sums[:width] = jnp.dot(x_ref[...].T, grad, preferred_element_type=F32)
-    sums[width : 2 * width] = jnp.dot(mean_ref[...].T, grad, preferred_element_type=F32)
-    sums[2 * width :] = bias_ref[...]
-    rows, extra = width // 4, bias_ref.shape[0] // 4
+def quarter_kernel(at, ids_ref, keep_ref, got_ref, own_ref, *sends):
+    extra = keep_ref.shape[0] - 256 * (keep_ref.shape[0] // 256)
+    rows, extra = (keep_ref.shape[0] - extra) // 4, extra // 4
     for x, out in enumerate((own_ref,) + sends):
         quarter = ids_ref[at + x]
-        for base, count, to in ((0, rows, 0), (width, rows, rows), (2 * width, extra, 2 * rows)):
-            start = pl.multiple_of(base + quarter * count, 16)
-            out[to : to + count] = sums[pl.ds(start, count)].astype(out.dtype)
-
-
-def quad_sum_kernel(at, ids_ref, own_ref, one_ref, two_ref, three_ref, keep_ref, send_ref):
-    total = own_ref[...] + one_ref[...].astype(F32)
-    total = total + (two_ref[...].astype(F32) + three_ref[...].astype(F32))
-    extra = keep_ref.shape[0] * 2 - own_ref.shape[0]
-    rows = keep_ref.shape[0] - extra
-    first = ids_ref[at] == 0
-    keep_ref[:rows] = jnp.where(first, total[:rows], total[rows : 2 * rows])
-    send_ref[:rows] = jnp.where(first, total[rows : 2 * rows], total[:rows])
-    keep_ref[rows:] = total[2 * rows :]
-    send_ref[rows:] = total[2 * rows :]
+        for base, count, to in ((0, rows, 0), (4 * rows, extra, rows)):
+            here = pl.ds(pl.multiple_of(base + quarter * count, 16), count)
+            out[to : to + count] = (keep_ref[here] + got_ref[here]).astype(out.dtype)
 
 
 def join_kernel(at, ids_ref, *refs):
@@ -383,8 +357,8 @@
     degree = lax.dynamic_index_in_dim(degree, side, 0, False) + sent_degree
     divisor = jnp.maximum(degree, 1.0)
 
+    row_total = block_rows * 128
     forward = partial(forward_mm, ids=ids, table=table, masks=masks, block_rows=block_rows, tblk=1024)
-    row_total = block_rows * 128
     from_left = from_right = node_features
     pieces, cols, acc = [node_features], [(0, 0)], None
     early = (node_features, weight_self, bias_term, out_grad, ids, divisor)
@@ -396,9 +370,10 @@
         else:
             next_left = lax.ppermute(from_left[:half], "row", clockwise)
             next_right = lax.ppermute(from_right[half:], "row", counter)
-        acc = forward(
+        acc, *rest = forward(
             pieces, cols, None, acc=acc, out_rows=row_total, out_dtype=F32, name="forward_step"
         )
+        x_turned = rest[0] if rest else x_turned
         if s == 2:
             x_now, ws_now, b_now, og_now, ids_now, div_now = early
             own_part = jnp.dot(x_now, ws_now, preferred_element_type=F32) + b_now
@@ -413,8 +388,8 @@
     mine = last_forward(pieces, at_side, ids, far_tiles, acc, F32, "forward_keep")
     mine, received = lax.optimization_barrier((mine, received))
 
-    mean, node_out, grad_b, mean_grad, bias_part = middle(
-        mine, received, divisor, own_part, wide_out_grad, weight_neigh
+    node_out, grad_b, mean_grad, keep, sent = middle(
+        at_side, ids, mine, received, divisor, own_part, wide_out_grad, weight_neigh, x_turned
     )
     other_grad = lax.ppermute(mean_grad, "col", swap)
 
@@ -435,37 +410,33 @@
         return [lax.ppermute(part, axis, [(r, r ^ x) for r in range(n)]) for x, part in parts]
 
     def start_quad(parts):
-        quarter = 2 * (width // 4) + 16
         own, *sends = small_call(
-            partial(weight_kernel, at_quad), "weight_grads",
-            [array(quarter, F32)] + [array(quarter, BF16)] * 3, (ids,) + parts,
-            scratch=[pltpu.VMEM((2 * width + 64, width), F32)],
+            partial(quarter_kernel, at_quad), "weight_quarters",
+            [array(width // 4 + 16, F32)] + [array(width // 4 + 16, BF16)] * 3, (ids,) + parts,
         )
         return [own] + to_quad(list(enumerate(sends, 1)))
 
-    def to_core(parts):
-        keep, send = small_call(
-            partial(quad_sum_kernel, at_side), "quad_sums", [array(width // 4 + 16, F32)] * 2,
-            (ids,) + tuple(parts),
-        )
-        return [keep, lax.ppermute(send, "col", swap)]
+    def rounded_sum(parts):
+        total = parts[0].astype(F32)
+        for part in parts[1:]:
+            total = total + part.astype(F32)
+        return total.astype(BF16)
 
     def add_all(b, parts):
-        quarter = parts[0] + parts[1]
+        quarter = rounded_sum(parts)
         return [quarter, lax.ppermute(quarter, "row", [(r, r ^ (1 << b)) for r in range(n)])]
 
     def from_quad(parts):
-        quarter = (parts[0] + parts[1]).astype(BF16)
+        quarter = rounded_sum(parts)
         return [quarter] + to_quad([(x, quarter) for x in (1, 2, 3)])
 
     spread = [[] for _ in range(far)]
     spread[0].append(start_quad)
-    spread[1].append(to_core)
     for b in range(2, bits):
         spread[b - 1].append(partial(add_all, b))
     spread[bits - 1].append(from_quad)
 
-    weights = (node_features, mean, grad_b, bias_part)
+    weights = (keep, lax.ppermute(sent, "col", swap))
     right, left = far_terms[:half], far_terms[half:]
     for s in range(far - 1, -1, -1):
         mean_grad, other_grad = both_grads

time: 114 us -> 109 us (0.956)
  Pallas kernels: 53.2 us -> 42.2 us
  waiting for transfers between devices: 19.3 us -> 25.5 us
    pallas_call x4, Pallas kernels: 19.2 us -> 14.1 us  [backward_mm(): pl.pallas_call(partial(backward_kernel, tuple(cols), tuple(sides), block_...]
    pallas_call x4, Pallas kernels: 20.6 us -> 16.3 us  [forward_mm(): pl.pallas_call(partial(forward_kernel, tuple(cols), side_at, block_rows,...]
    ppermute x4, waiting for transfers between devices: 7.82 us -> 11.8 us  [local(): left = lax.ppermute(left, 'row', counter)]
    ppermute x3, waiting for transfers between devices: 6.74 us -> 9.8 us  [local(): next_left = lax.ppermute(from_left, 'row', clockwise)]
    ppermute x1, waiting for transfers between devices: 1.26 us -> 0.01 us  [local(): weights = (keep, lax.ppermute(sent, 'col', swap))]
    pallas_call x4 -> x3, Pallas kernels: 3.57 us -> 2.54 us  [small_call(): pl.pallas_call(kernel, in_specs=[smem_spec()] + [vmem_spec()] * (len(args...]
  transfers between devices with their start and end apart: 28 -> 28, of which waited for: 12 -> 12; matrix products, arithmetic and copies ran while one was open for 5% -> 5% of each run, Pallas kernels for 42% -> 35%
where the time goes in v5:
time: 109 us
  Pallas kernels  42.2 us (39%)
  starting transfers between devices  28.3 us (26%)
  waiting for transfers between devices  25.5 us (23%)
  local copies, waits for them, and re-layouts  5.74 us (5%)
  other arithmetic  4.9 us (4%)
  between operations  1.7 us (2%)
    pallas_call x4, Pallas kernels, forward_mm(): pl.pallas_call(partial(forward_kernel, tuple(cols), side_at, block_rows,...  16.3 us
    pallas_call x4, Pallas kernels, backward_mm(): pl.pallas_call(partial(backward_kernel, tuple(cols), tuple(sides), block_...  14.1 us
    ppermute x4, waiting for transfers between devices, local(): left = lax.ppermute(left, 'row', counter)  11.8 us
    ppermute x3, waiting for transfers between devices, local(): next_left = lax.ppermute(from_left, 'row', clockwise)  9.8 us
    ppermute x6, starting transfers between devices, to_quad(): lax.ppermute(part, axis, [(r, r ^ x) for r in range(n)])  7.1 us
    ppermute x3, starting transfers between devices, local(): next_left = lax.ppermute(from_left, 'row', clockwise)  6.35 us
    unnamed x20, local copies, waits for them, and re-layouts  4.94 us
    ppermute x4, starting transfers between devices, local(): left = lax.ppermute(left, 'row', counter)  4.56 us
  transfers between devices with their start and end apart: 28, of which 12 were waited for; matrix products, arithmetic and copies ran while one was open for 5% of the time, Pallas kernels for 35%

profile of v5, /device:TPU:0, one launch (start us, length us, event | category | flops | bytes accessed | tf_op | source)
XLA Modules:
  0.0 109.2 jit_solution(8646917174368619729)
XLA Ops:
  0.7 3.1 %collective-permute-start = (bf16[1024,256]{1,0:T(8,128)(2,1)}, bf16[1024,256]{1,0:T(8,128)(2,1)S(1)}, u32[]{:S(2)}, u32[]{:S(2)}) collective-permute-start(bf16[1024,256]{1,0:T(8,128)(2,1)} %refs_0_.1), channel_id=1, source_target_pairs={{0,4},{4,8},{8,12},{12,14},{14,10},{10,6},{6,2},{2,0},{1,5},{5,9},... | collective-permute-start | bytes 1572872 | tf_op jit(solution)/shard_map/ppermute | solution.py:367
  5.1 2.0 %popcnt_reduce_fusion = s32[384,128]{1,0:T(8,128)S(1)} fusion(s32[1,1,384,128,8]{3,4,2,1,0:T(8,128)} %param.13), kind=kLoop, calls=%fused_computation | loop fusion | flops 737280 | bytes 1769472 | tf_op jit(solution)/shard_map/reduce_sum | solution.py:353
  9.4 2.8 %forward_step.4 = (f32[256,2048]{1,0:T(8,128)S(1)}, bf16[256,1024]{1,0:T(8,128)(2,1)S(1)}) custom-call(s32[14]{0:T(128)S(1)} %fusion.7.ids_ref, s32[1024]{0:T(1024)S(1)} %select_reduce_fusion.table_ref, s32[384,8,128]{2,1,0:T(8,128)S(1)} %bitcast.20, bf16[1024,256]{1,0:T(8,128)(2,1)S(1)} %copy-done.4), custom_call_target="tpu_custom_call" | custom-call | flops 1024 | bytes 1024 | tf_op jit(solution)/shard_map/forward_step/pallas_call | solution.py:95
  13.6 2.2 %collective-permute-done.refs_0_ = bf16[1024,256]{1,0:T(8,128)(2,1)S(1)} collective-permute-done((bf16[1024,256]{1,0:T(8,128)(2,1)}, bf16[1024,256]{1,0:T(8,128)(2,1)S(1)}, u32[]{:S(2)}, u32[]{:S(2)}) %collective-permute-start) | collective-permute-done | bytes 524320 | tf_op jit(solution)/shard_map/ppermute | solution.py:367
  15.8 1.8 %collective-permute-start.3 = (bf16[1024,256]{1,0:T(8,128)(2,1)S(1)}, bf16[1024,256]{1,0:T(8,128)(2,1)S(1)}, u32[]{:S(2)}, u32[]{:S(2)}) collective-permute-start(bf16[1024,256]{1,0:T(8,128)(2,1)S(1)} %collective-permute-done.refs_0_), channel_id=1, source_target_pairs={{0,4},{4,8},{8,12},{12,14},{14,10},{10,6},{6,2},{2,0},{1,5},{5,9},... | collective-permute-start | bytes 1572872 | tf_op jit(solution)/shard_map/ppermute | solution.py:367
  17.9 1.6 %copy-done.3 = f32[256,2048]{1,0:T(8,128)S(1)} copy-done((f32[256,2048]{1,0:T(8,128)S(1)}, f32[256,2048]{1,0:T(8,128)}, u32[]{:S(2)}) %copy-start.3) | copy-done | bytes 2097176
  19.4 4.5 %forward_step.5.refs_2_ = f32[256,2048]{1,0:T(8,128)S(1)} custom-call(s32[14]{0:T(128)S(1)} %fusion.7.ids_ref, s32[1024]{0:T(1024)S(1)} %select_reduce_fusion.table_ref, s32[384,8,128]{2,1,0:T(8,128)S(1)} %bitcast.21, bf16[1024,256]{1,0:T(8,128)(2,1)S(1)} %collective-permute-done.refs_0_, bf16[1024,256]{1,0:T(8,128)(2,1)S(1)} %collective-permute-done.2.refs_1_, ...), custom_call_target="tpu_custom_call" | custom-call | flops 1024 | bytes 1024 | tf_op jit(solution)/shard_map/forward_step/pallas_call | solution.py:95
  24.0 1.7 %far_tiles.1.tiles_ref = bf16[1024,2048]{1,0:T(8,128)(2,1)S(1)} custom-call(s32[14]{0:T(128)S(1)} %fusion.7.ids_ref, s32[1024]{0:T(1024)S(1)} %select_reduce_fusion.table_ref, s32[384,8,128]{2,1,0:T(8,128)S(1)} %bitcast.22), custom_call_target="tpu_custom_call" | custom-call | flops 1024 | bytes 1024 | tf_op jit(solution)/shard_map/far_tiles/pallas_call | solution.py:115
  27.0 1.9 %collective-permute-done.3.refs_0_ = bf16[1024,256]{1,0:T(8,128)(2,1)S(1)} collective-permute-done((bf16[1024,256]{1,0:T(8,128)(2,1)S(1)}, bf16[1024,256]{1,0:T(8,128)(2,1)S(1)}, u32[]{:S(2)}, u32[]{:S(2)}) %collective-permute-start.3) | collective-permute-done | bytes 524320 | tf_op jit(solution)/shard_map/ppermute | solution.py:367
  31.0 4.5 %forward_step.6.refs_2_ = f32[256,2048]{1,0:T(8,128)S(1)} custom-call(s32[14]{0:T(128)S(1)} %fusion.7.ids_ref, s32[1024]{0:T(1024)S(1)} %select_reduce_fusion.table_ref, s32[384,8,128]{2,1,0:T(8,128)S(1)} %bitcast.23, bf16[1024,256]{1,0:T(8,128)(2,1)S(1)} %collective-permute-done.3.refs_0_, bf16[1024,256]{1,0:T(8,128)(2,1)S(1)} %collective-permute-done.4.refs_1_, ...), custom_call_target="tpu_custom_call" | custom-call | flops 1024 | bytes 1024 | tf_op jit(solution)/shard_map/forward_step/pallas_call | solution.py:95
  35.5 5.6 %collective-permute-done.5.refs_0_ = bf16[1024,256]{1,0:T(8,128)(2,1)S(1)} collective-permute-done((bf16[1024,256]{1,0:T(8,128)(2,1)S(1)}, bf16[1024,256]{1,0:T(8,128)(2,1)S(1)}, u32[]{:S(2)}, u32[]{:S(2)}) %collective-permute-start.5) | collective-permute-done | bytes 524320 | tf_op jit(solution)/shard_map/ppermute | solution.py:367
  43.5 4.5 %forward_step.7.acc_ref = f32[256,2048]{1,0:T(8,128)S(1)} custom-call(s32[14]{0:T(128)S(1)} %fusion.7.ids_ref, s32[1024]{0:T(1024)S(1)} %select_reduce_fusion.table_ref, s32[384,8,128]{2,1,0:T(8,128)S(1)} %bitcast.24, bf16[1024,256]{1,0:T(8,128)(2,1)S(1)} %collective-permute-done.5.refs_0_, bf16[1024,256]{1,0:T(8,128)(2,1)S(1)} %collective-permute-done.6.refs_1_, ...), custom_call_target="tpu_custom_call" | custom-call | flops 1024 | bytes 1024 | tf_op jit(solution)/shard_map/forward_step/pallas_call | solution.py:95
  52.4 2.5 %layer.1 = (bf16[1024,256]{1,0:T(8,128)(2,1)}, bf16[1024,256]{1,0:T(8,128)(2,1)S(1)}, bf16[1024,256]{1,0:T(8,128)(2,1)S(1)}, f32[320,256]{1,0:T(8,128)S(1)}, f32[320,256]{1,0:T(8,128)S(1)}) custom-call(s32[14]{0:T(128)S(1)} %fusion.7.ids_ref, f32[256,1024]{1,0:T(8,128)S(1)} %forward_keep.1.agg_ref, bf16[256,1024]{1,0:T(8,128)(2,1)S(1)} %collective-permute-done.9.other_ref, ...), custom_call_target="tpu_custom_call" | custom-call | flops 1024 | bytes 1024 | tf_op jit(solution)/shard_map/layer/pallas_call | solution.py:211
  60.2 4.0 %backward_step.3 = bf16[2048,256]{1,0:T(8,128)(2,1)S(1)} custom-call(s32[14]{0:T(128)S(1)} %fusion.7.ids_ref, s32[1024]{0:T(1024)S(1)} %select_reduce_fusion.table_ref, s32[384,8,128]{2,1,0:T(8,128)S(1)} %bitcast.25, bf16[1024,256]{1,0:T(8,128)(2,1)S(1)} %get-tuple-element.173.grad_ref.after_ref.refs_0_, ...), custom_call_target="tpu_custom_call" | custom-call | flops 8589934592 | bytes 3670016 | tf_op jit(solution)/shard_map/backward_step/pallas_call | solution.py:254
  66.8 1.5 %collective-permute-start.16 = (bf16[80,256]{1,0:T(8,128)(2,1)S(1)}, bf16[80,256]{1,0:T(8,128)(2,1)S(1)}, u32[]{:S(2)}, u32[]{:S(2)}) collective-permute-start(bf16[80,256]{1,0:T(8,128)(2,1)S(1)} %get-tuple-element.156), channel_id=1, source_target_pairs={{0,6},{2,4},{4,2},{6,0},{8,14},{10,12},{12,10},{14,8},{1,7},{3,5},... | collective-permute-start | bytes 122888 | tf_op jit(solution)/shard_map/ppermute | solution.py:410
  70.6 3.9 %backward_step.4 = bf16[2048,256]{1,0:T(8,128)(2,1)S(1)} custom-call(s32[14]{0:T(128)S(1)} %fusion.7.ids_ref, s32[1024]{0:T(1024)S(1)} %select_reduce_fusion.table_ref, s32[384,8,128]{2,1,0:T(8,128)S(1)} %bitcast.26, bf16[1024,256]{1,0:T(8,128)(2,1)S(1)} %get-tuple-element.173.grad_ref.after_ref.refs_0_, ...), custom_call_target="tpu_custom_call" | custom-call | flops 8589934592 | bytes 3670016 | tf_op jit(solution)/shard_map/backward_step/pallas_call | solution.py:254
  74.6 2.7 %collective-permute-start.19 = (bf16[80,256]{1,0:T(8,128)(2,1)S(1)}, bf16[80,256]{1,0:T(8,128)(2,1)S(1)}, u32[]{:S(2)}, u32[]{:S(2)}) collective-permute-start(bf16[80,256]{1,0:T(8,128)(2,1)S(1)} %add_convert_fusion.8), channel_id=1, source_target_pairs={{0,8},{2,10},{4,12},{6,14},{8,0},{10,2},{12,4},{14,6},{1,9},{3,11}... | collective-permute-start | bytes 122888 | tf_op jit(solution)/shard_map/ppermute | solution.py:427
  77.3 4.8 %collective-permute-done.18 = bf16[1024,256]{1,0:T(8,128)(2,1)S(1)} collective-permute-done((bf16[1024,256]{1,0:T(8,128)(2,1)S(1)}, bf16[1024,256]{1,0:T(8,128)(2,1)S(1)}, u32[]{:S(2)}, u32[]{:S(2)}) %collective-permute-start.18) | collective-permute-done | bytes 524320 | tf_op jit(solution)/shard_map/ppermute | solution.py:447
  82.4 1.6 %collective-permute-start.21 = (bf16[1024,256]{1,0:T(8,128)(2,1)S(1)}, bf16[1024,256]{1,0:T(8,128)(2,1)S(1)}, u32[]{:S(2)}, u32[]{:S(2)}) collective-permute-start(bf16[1024,256]{1,0:T(8,128)(2,1)S(1)} %get-tuple-element.174), channel_id=1, source_target_pairs={{4,0},{8,4},{12,8},{14,12},{10,14},{6,10},{2,6},{0,2},{5,1},{9,5},... | collective-permute-start | bytes 1572872 | tf_op jit(solution)/shard_map/ppermute | solution.py:447
  84.5 4.0 %backward_step.5 = bf16[2048,256]{1,0:T(8,128)(2,1)S(1)} custom-call(s32[14]{0:T(128)S(1)} %fusion.7.ids_ref, s32[1024]{0:T(1024)S(1)} %select_reduce_fusion.table_ref, s32[384,8,128]{2,1,0:T(8,128)S(1)} %bitcast.27, bf16[1024,256]{1,0:T(8,128)(2,1)S(1)} %get-tuple-element.173.grad_ref.after_ref.refs_0_, ...), custom_call_target="tpu_custom_call" | custom-call | flops 8589934592 | bytes 3670016 | tf_op jit(solution)/shard_map/backward_step/pallas_call | solution.py:254
  88.5 2.7 %collective-permute-start.24 = (bf16[80,256]{1,0:T(8,128)(2,1)S(1)}, bf16[80,256]{1,0:T(8,128)(2,1)S(1)}, u32[]{:S(2)}, u32[]{:S(2)}) collective-permute-start(bf16[80,256]{1,0:T(8,128)(2,1)S(1)} %add_convert_fusion.7.refs_0_), channel_id=1, source_target_pairs={{0,6},{2,4},{4,2},{6,0},{8,14},{10,12},{12,10},{14,8},{1,7},{3,5},... | collective-permute-start | bytes 122888 | tf_op jit(solution)/shard_map/ppermute | solution.py:410
  92.1 3.9 %collective-permute-done.21 = bf16[1024,256]{1,0:T(8,128)(2,1)S(1)} collective-permute-done((bf16[1024,256]{1,0:T(8,128)(2,1)S(1)}, bf16[1024,256]{1,0:T(8,128)(2,1)S(1)}, u32[]{:S(2)}, u32[]{:S(2)}) %collective-permute-start.21) | collective-permute-done | bytes 524320 | tf_op jit(solution)/shard_map/ppermute | solution.py:447
  98.6 2.2 %backward_own.1 = f32[1024,256]{1,0:T(8,128)S(1)} custom-call(s32[14]{0:T(128)S(1)} %fusion.7.ids_ref, s32[1024]{0:T(1024)S(1)} %select_reduce_fusion.table_ref, s32[384,8,128]{2,1,0:T(8,128)S(1)} %bitcast.28, bf16[1024,256]{1,0:T(8,128)(2,1)S(1)} %get-tuple-element.173.grad_ref.after_ref.refs_0_, ...), custom_call_target="tpu_custom_call" | custom-call | flops 4294967296 | bytes 2621440 | tf_op jit(solution)/shard_map/backward_own/pallas_call | solution.py:254
  104.6 3.0 %collective-permute-done.26 = bf16[1024,256]{1,0:T(8,128)(2,1)S(1)} collective-permute-done((bf16[1024,256]{1,0:T(8,128)(2,1)S(1)}, bf16[1024,256]{1,0:T(8,128)(2,1)S(1)}, u32[]{:S(2)}, u32[]{:S(2)}) %collective-permute-start.26) | collective-permute-done | bytes 524320 | tf_op jit(solution)/shard_map/ppermute | solution.py:447
  (92 shorter events, 34.4 us)
Async XLA Ops:
  0.7 15.2 %collective-permute-start = (bf16[1024,256]{1,0:T(8,128)(2,1)}, bf16[1024,256]{1,0:T(8,128)(2,1)S(1)}, u32[]{:S(2)}, u32[]{:S(2)}) collective-permute-start(bf16[1024,256]{1,0:T(8,128)(2,1)} %refs_0_.1), channel_id=1, source_target_pairs={{0,4},{4,8},{8,12},{12,14},{14,10},{10,6},{6,2},{2,0},{1,5},{5,9},... | collective-permute-start | bytes 1572872 | tf_op jit(solution)/shard_map/ppermute | solution.py:367
  3.7 13.9 %collective-permute-start.2 = (bf16[1024,256]{1,0:T(8,128)(2,1)}, bf16[1024,256]{1,0:T(8,128)(2,1)S(1)}, u32[]{:S(2)}, u32[]{:S(2)}) collective-permute-start(bf16[1024,256]{1,0:T(8,128)(2,1)} %refs_0_.1), channel_id=1, source_target_pairs={{4,0},{8,4},{12,8},{14,12},{10,14},{6,10},{2,6},{0,2},{5,1},{9,5},... | collective-permute-start | bytes 1572872 | tf_op jit(solution)/shard_map/ppermute | solution.py:368
  15.8 13.1 %collective-permute-start.3 = (bf16[1024,256]{1,0:T(8,128)(2,1)S(1)}, bf16[1024,256]{1,0:T(8,128)(2,1)S(1)}, u32[]{:S(2)}, u32[]{:S(2)}) collective-permute-start(bf16[1024,256]{1,0:T(8,128)(2,1)S(1)} %collective-permute-done.refs_0_), channel_id=1, source_target_pairs={{0,4},{4,8},{8,12},{12,14},{14,10},{10,6},{6,2},{2,0},{1,5},{5,9},... | collective-permute-start | bytes 1572872 | tf_op jit(solution)/shard_map/ppermute | solution.py:367
  17.6 12.8 %collective-permute-start.4 = (bf16[1024,256]{1,0:T(8,128)(2,1)S(1)}, bf16[1024,256]{1,0:T(8,128)(2,1)S(1)}, u32[]{:S(2)}, u32[]{:S(2)}) collective-permute-start(bf16[1024,256]{1,0:T(8,128)(2,1)S(1)} %collective-permute-done.2.refs_1_), channel_id=1, source_target_pairs={{4,0},{8,4},{12,8},{14,12},{10,14},{6,10},{2,6},{0,2},{5,1},{9,5},... | collective-permute-start | bytes 1572872 | tf_op jit(solution)/shard_map/ppermute | solution.py:368
  28.9 12.2 %collective-permute-start.5 = (bf16[1024,256]{1,0:T(8,128)(2,1)S(1)}, bf16[1024,256]{1,0:T(8,128)(2,1)S(1)}, u32[]{:S(2)}, u32[]{:S(2)}) collective-permute-start(bf16[1024,256]{1,0:T(8,128)(2,1)S(1)} %collective-permute-done.3.refs_0_), channel_id=1, source_target_pairs={{0,4},{4,8},{8,12},{12,14},{14,10},{10,6},{6,2},{2,0},{1,5},{5,9},... | collective-permute-start | bytes 1572872 | tf_op jit(solution)/shard_map/ppermute | solution.py:367
  30.4 12.1 %collective-permute-start.6 = (bf16[1024,256]{1,0:T(8,128)(2,1)S(1)}, bf16[1024,256]{1,0:T(8,128)(2,1)S(1)}, u32[]{:S(2)}, u32[]{:S(2)}) collective-permute-start(bf16[1024,256]{1,0:T(8,128)(2,1)S(1)} %collective-permute-done.4.refs_1_), channel_id=1, source_target_pairs={{4,0},{8,4},{12,8},{14,12},{10,14},{6,10},{2,6},{0,2},{5,1},{9,5},... | collective-permute-start | bytes 1572872 | tf_op jit(solution)/shard_map/ppermute | solution.py:368
  41.1 6.9 %collective-permute-start.7 = (bf16[512,256]{1,0:T(8,128)(2,1)S(1)}, bf16[512,256]{1,0:T(8,128)(2,1)S(1)}, u32[]{:S(2)}, u32[]{:S(2)}) collective-permute-start(bf16[512,256]{1,0:T(8,128)(2,1)S(1)} %slice.30), channel_id=1, source_target_pairs={{0,4},{4,8},{8,12},{12,14},{14,10},{10,6},{6,2},{2,0},{1,5},{5,9},... | collective-permute-start | bytes 786440 | tf_op jit(solution)/shard_map/ppermute | solution.py:371
  42.5 6.6 %collective-permute-start.8 = (bf16[512,256]{1,0:T(8,128)(2,1)S(1)}, bf16[512,256]{1,0:T(8,128)(2,1)S(1)}, u32[]{:S(2)}, u32[]{:S(2)}) collective-permute-start(bf16[512,256]{1,0:T(8,128)(2,1)S(1)} %slice.31), channel_id=1, source_target_pairs={{4,0},{8,4},{12,8},{14,12},{10,14},{6,10},{2,6},{0,2},{5,1},{9,5},... | collective-permute-start | bytes 786440 | tf_op jit(solution)/shard_map/ppermute | solution.py:372
  56.3 7.9 %collective-permute-start.11 = (f32[320,256]{1,0:T(8,128)S(1)}, f32[320,256]{1,0:T(8,128)S(1)}, u32[]{:S(2)}, u32[]{:S(2)}) collective-permute-start(f32[320,256]{1,0:T(8,128)S(1)} %get-tuple-element.142), channel_id=1, source_target_pairs={{0,1},{1,0},{2,3},{3,2},{4,5},{5,4},{6,7},{7,6},{8,9},{9,8},{10,11... | collective-permute-start | bytes 983048 | tf_op jit(solution)/shard_map/ppermute | solution.py:439
  58.1 10.2 %collective-permute-start.13 = (bf16[512,256]{1,0:T(8,128)(2,1)S(1)}, bf16[512,256]{1,0:T(8,128)(2,1)S(1)}, u32[]{:S(2)}, u32[]{:S(2)}) collective-permute-start(bf16[512,256]{1,0:T(8,128)(2,1)S(1)} %get-tuple-element.148), channel_id=1, source_target_pairs={{4,0},{8,4},{12,8},{14,12},{10,14},{6,10},{2,6},{0,2},{5,1},{9,5},... | collective-permute-start | bytes 786440 | tf_op jit(solution)/shard_map/ppermute | solution.py:447
  58.9 9.4 %collective-permute-start.12 = (bf16[512,256]{1,0:T(8,128)(2,1)S(1)}, bf16[512,256]{1,0:T(8,128)(2,1)S(1)}, u32[]{:S(2)}, u32[]{:S(2)}) collective-permute-start(bf16[512,256]{1,0:T(8,128)(2,1)S(1)} %get-tuple-element.145), channel_id=1, source_target_pairs={{0,4},{4,8},{8,12},{12,14},{14,10},{10,6},{6,2},{2,0},{1,5},{5,9},... | collective-permute-start | bytes 786440 | tf_op jit(solution)/shard_map/ppermute | solution.py:446
  64.8 9.8 %collective-permute-start.14 = (bf16[80,256]{1,0:T(8,128)(2,1)S(1)}, bf16[80,256]{1,0:T(8,128)(2,1)S(1)}, u32[]{:S(2)}, u32[]{:S(2)}) collective-permute-start(bf16[80,256]{1,0:T(8,128)(2,1)S(1)} %get-tuple-element.154), channel_id=1, source_target_pairs={{0,2},{2,0},{4,6},{6,4},{8,10},{10,8},{12,14},{14,12},{1,3},{3,1},... | collective-permute-start | bytes 122888 | tf_op jit(solution)/shard_map/ppermute | solution.py:410
  65.6 9.0 %collective-permute-start.15 = (bf16[80,256]{1,0:T(8,128)(2,1)S(1)}, bf16[80,256]{1,0:T(8,128)(2,1)S(1)}, u32[]{:S(2)}, u32[]{:S(2)}) collective-permute-start(bf16[80,256]{1,0:T(8,128)(2,1)S(1)} %get-tuple-element.155), channel_id=1, source_target_pairs={{0,4},{2,6},{4,0},{6,2},{8,12},{10,14},{12,8},{14,10},{1,5},{3,7},... | collective-permute-start | bytes 122888 | tf_op jit(solution)/shard_map/ppermute | solution.py:410
  66.8 7.8 %collective-permute-start.16 = (bf16[80,256]{1,0:T(8,128)(2,1)S(1)}, bf16[80,256]{1,0:T(8,128)(2,1)S(1)}, u32[]{:S(2)}, u32[]{:S(2)}) collective-permute-start(bf16[80,256]{1,0:T(8,128)(2,1)S(1)} %get-tuple-element.156), channel_id=1, source_target_pairs={{0,6},{2,4},{4,2},{6,0},{8,14},{10,12},{12,10},{14,8},{1,7},{3,5},... | collective-permute-start | bytes 122888 | tf_op jit(solution)/shard_map/ppermute | solution.py:410
  68.5 13.6 %collective-permute-start.18 = (bf16[1024,256]{1,0:T(8,128)(2,1)S(1)}, bf16[1024,256]{1,0:T(8,128)(2,1)S(1)}, u32[]{:S(2)}, u32[]{:S(2)}) collective-permute-start(bf16[1024,256]{1,0:T(8,128)(2,1)S(1)} %get-tuple-element.162), channel_id=1, source_target_pairs={{4,0},{8,4},{12,8},{14,12},{10,14},{6,10},{2,6},{0,2},{5,1},{9,5},... | collective-permute-start | bytes 1572872 | tf_op jit(solution)/shard_map/ppermute | solution.py:447
  69.3 12.8 %collective-permute-start.17 = (bf16[1024,256]{1,0:T(8,128)(2,1)S(1)}, bf16[1024,256]{1,0:T(8,128)(2,1)S(1)}, u32[]{:S(2)}, u32[]{:S(2)}) collective-permute-start(bf16[1024,256]{1,0:T(8,128)(2,1)S(1)} %get-tuple-element.159), channel_id=1, source_target_pairs={{0,4},{4,8},{8,12},{12,14},{14,10},{10,6},{6,2},{2,0},{1,5},{5,9},... | collective-permute-start | bytes 1572872 | tf_op jit(solution)/shard_map/ppermute | solution.py:446
  74.6 13.8 %collective-permute-start.19 = (bf16[80,256]{1,0:T(8,128)(2,1)S(1)}, bf16[80,256]{1,0:T(8,128)(2,1)S(1)}, u32[]{:S(2)}, u32[]{:S(2)}) collective-permute-start(bf16[80,256]{1,0:T(8,128)(2,1)S(1)} %add_convert_fusion.8), channel_id=1, source_target_pairs={{0,8},{2,10},{4,12},{6,14},{8,0},{10,2},{12,4},{14,6},{1,9},{3,11}... | collective-permute-start | bytes 122888 | tf_op jit(solution)/shard_map/ppermute | solution.py:427
  82.4 13.5 %collective-permute-start.21 = (bf16[1024,256]{1,0:T(8,128)(2,1)S(1)}, bf16[1024,256]{1,0:T(8,128)(2,1)S(1)}, u32[]{:S(2)}, u32[]{:S(2)}) collective-permute-start(bf16[1024,256]{1,0:T(8,128)(2,1)S(1)} %get-tuple-element.174), channel_id=1, source_target_pairs={{4,0},{8,4},{12,8},{14,12},{10,14},{6,10},{2,6},{0,2},{5,1},{9,5},... | collective-permute-start | bytes 1572872 | tf_op jit(solution)/shard_map/ppermute | solution.py:447
  84.1 12.1 %collective-permute-start.20 = (bf16[1024,256]{1,0:T(8,128)(2,1)S(1)}, bf16[1024,256]{1,0:T(8,128)(2,1)S(1)}, u32[]{:S(2)}, u32[]{:S(2)}) collective-permute-start(bf16[1024,256]{1,0:T(8,128)(2,1)S(1)} %get-tuple-element.171), channel_id=1, source_target_pairs={{0,4},{4,8},{8,12},{12,14},{14,10},{10,6},{6,2},{2,0},{1,5},{5,9},... | collective-permute-start | bytes 1572872 | tf_op jit(solution)/shard_map/ppermute | solution.py:446
  88.5 12.7 %collective-permute-start.24 = (bf16[80,256]{1,0:T(8,128)(2,1)S(1)}, bf16[80,256]{1,0:T(8,128)(2,1)S(1)}, u32[]{:S(2)}, u32[]{:S(2)}) collective-permute-start(bf16[80,256]{1,0:T(8,128)(2,1)S(1)} %add_convert_fusion.7.refs_0_), channel_id=1, source_target_pairs={{0,6},{2,4},{4,2},{6,0},{8,14},{10,12},{12,10},{14,8},{1,7},{3,5},... | collective-permute-start | bytes 122888 | tf_op jit(solution)/shard_map/ppermute | solution.py:410
  91.2 10.0 %collective-permute-start.23 = (bf16[80,256]{1,0:T(8,128)(2,1)S(1)}, bf16[80,256]{1,0:T(8,128)(2,1)S(1)}, u32[]{:S(2)}, u32[]{:S(2)}) collective-permute-start(bf16[80,256]{1,0:T(8,128)(2,1)S(1)} %add_convert_fusion.7.refs_0_), channel_id=1, source_target_pairs={{0,4},{2,6},{4,0},{6,2},{8,12},{10,14},{12,8},{14,10},{1,5},{3,7},... | collective-permute-start | bytes 122888 | tf_op jit(solution)/shard_map/ppermute | solution.py:410
  91.6 9.6 %collective-permute-start.22 = (bf16[80,256]{1,0:T(8,128)(2,1)S(1)}, bf16[80,256]{1,0:T(8,128)(2,1)S(1)}, u32[]{:S(2)}, u32[]{:S(2)}) collective-permute-start(bf16[80,256]{1,0:T(8,128)(2,1)S(1)} %add_convert_fusion.7.refs_0_), channel_id=1, source_target_pairs={{0,2},{2,0},{4,6},{6,4},{8,10},{10,8},{12,14},{14,12},{1,3},{3,1},... | collective-permute-start | bytes 122888 | tf_op jit(solution)/shard_map/ppermute | solution.py:410
  96.5 11.1 %collective-permute-start.26 = (bf16[1024,256]{1,0:T(8,128)(2,1)S(1)}, bf16[1024,256]{1,0:T(8,128)(2,1)S(1)}, u32[]{:S(2)}, u32[]{:S(2)}) collective-permute-start(bf16[1024,256]{1,0:T(8,128)(2,1)S(1)} %get-tuple-element.183), channel_id=1, source_target_pairs={{4,0},{8,4},{12,8},{14,12},{10,14},{6,10},{2,6},{0,2},{5,1},{9,5},... | collective-permute-start | bytes 1572872 | tf_op jit(solution)/shard_map/ppermute | solution.py:447
  97.9 10.3 %collective-permute-start.25 = (bf16[1024,256]{1,0:T(8,128)(2,1)S(1)}, bf16[1024,256]{1,0:T(8,128)(2,1)S(1)}, u32[]{:S(2)}, u32[]{:S(2)}) collective-permute-start(bf16[1024,256]{1,0:T(8,128)(2,1)S(1)} %get-tuple-element.182), channel_id=1, source_target_pairs={{0,4},{4,8},{8,12},{12,14},{14,10},{10,6},{6,2},{2,0},{1,5},{5,9},... | collective-permute-start | bytes 1572872 | tf_op jit(solution)/shard_map/ppermute | solution.py:446
  (14 other events, 60.9 us)

commit v6 on v5

--- a/solution.py
+++ b/solution.py
@@ -219,11 +219,29 @@
     )(ids, agg, other, divisor, own, og, wn, x_turned)
 
 
-def backward_kernel(cols, sides, block_rows, has_acc, ids_ref, table_ref, masks_ref, after_ref, *refs):
+def cut_quarters(at, ids_ref, keep_ref, got_ref, outs):
+    width = keep_ref.shape[1]
+    rows, extra = width // 4, (keep_ref.shape[0] - width) // 4
+    for x, out in enumerate(outs):
+        quarter = ids_ref[at + x]
+        for base, count, to in ((0, rows, 0), (width, extra, rows)):
+            here = pl.ds(pl.multiple_of(base + quarter * count, 16), count)
+            out[to : to + count] = (keep_ref[here] + got_ref[here]).astype(out.dtype)
+
+
+def backward_kernel(cols, sides, block_rows, has_acc, cut_at, ids_ref, table_ref, masks_ref, after_ref, *refs):
     del after_ref
     grads = refs[: len(sides)]
     acc_ref = refs[len(sides)] if has_acc else None
-    out_ref, tiles = refs[len(sides) + int(has_acc) :]
+    if cut_at is None:
+        out_ref, tiles = refs[len(sides) + int(has_acc) :]
+    else:
+        keep_ref, got_ref, out_ref, *quarters, tiles = refs[len(sides) + int(has_acc) :]
+
+        @pl.when(pl.program_id(0) == 0)
+        def _():
+            cut_quarters(cut_at, ids_ref, keep_ref, got_ref, quarters)
+
     piece_rows = out_ref.shape[0]
     rows = grads[0].shape[0]
     per_side = rows // 128
@@ -247,19 +265,26 @@
     out_ref[...] = total.astype(out_ref.dtype)
 
 
-def backward_mm(cols, grads, sides, after, ids, table, masks, acc, piece_rows, block_rows, out_dtype, name):
+def backward_mm(cols, grads, sides, after, ids, table, masks, acc, piece_rows, block_rows, out_dtype, name,
+    cut_at=None, weights=()):
     rows, width = grads[0].shape
-    args = [ids, table, masks, after] + list(grads) + ([] if acc is None else [acc])
+    args = [ids, table, masks, after] + list(grads) + ([] if acc is None else [acc]) + list(weights)
     piece = pl.BlockSpec((piece_rows, width), lambda p: (p, 0))
-    return pl.pallas_call(
-        partial(backward_kernel, tuple(cols), tuple(sides), block_rows, acc is not None),
+    out_specs, out_shape = [piece], [jax.ShapeDtypeStruct((len(cols) * piece_rows, width), out_dtype)]
+    if weights:
+        quarter = (weights[0].shape[0] // 4, width)
+        out_specs += [vmem_spec()] * 4
+        out_shape += [jax.ShapeDtypeStruct(quarter, F32)] + [jax.ShapeDtypeStruct(quarter, BF16)] * 3
+    outs = pl.pallas_call(
+        partial(backward_kernel, tuple(cols), tuple(sides), block_rows, acc is not None, cut_at),
         grid=(len(cols),),
         in_specs=[smem_spec(), smem_spec(), vmem_spec(), pl.BlockSpec(memory_space=pl.ANY)]
         + [vmem_spec()] * len(grads)
-        + ([] if acc is None else [piece]),
-        out_specs=piece,
+        + ([] if acc is None else [piece])
+        + [vmem_spec()] * len(weights),
+        out_specs=out_specs,
         scratch_shapes=[pltpu.VMEM((piece_rows, len(grads) * rows), BF16)],
-        out_shape=jax.ShapeDtypeStruct((len(cols) * piece_rows, width), out_dtype),
+        out_shape=out_shape,
         compiler_params=pltpu.CompilerParams(vmem_limit_bytes=VMEM_LIMIT),
         cost_estimate=pl.CostEstimate(
             flops=8 * len(cols) * piece_rows * rows * len(grads) * width,
@@ -268,6 +293,7 @@
         ),
         name=name,
     )(*args)
+    return outs if weights else outs[0]
 
 
 def small_call(kernel, name, out_shape, args, scratch=()):
@@ -281,16 +307,6 @@
         cost_estimate=BRIEF,
         name=name,
     )(*args)
-
-
-def quarter_kernel(at, ids_ref, keep_ref, got_ref, own_ref, *sends):
-    extra = keep_ref.shape[0] - 256 * (keep_ref.shape[0] // 256)
-    rows, extra = (keep_ref.shape[0] - extra) // 4, extra // 4
-    for x, out in enumerate((own_ref,) + sends):
-        quarter = ids_ref[at + x]
-        for base, count, to in ((0, rows, 0), (4 * rows, extra, rows)):
-            here = pl.ds(pl.multiple_of(base + quarter * count, 16), count)
-            out[to : to + count] = (keep_ref[here] + got_ref[here]).astype(out.dtype)
 
 
 def join_kernel(at, ids_ref, *refs):
@@ -410,11 +426,7 @@
         return [lax.ppermute(part, axis, [(r, r ^ x) for r in range(n)]) for x, part in parts]
 
     def start_quad(parts):
-        own, *sends = small_call(
-            partial(quarter_kernel, at_quad), "weight_quarters",
-            [array(width // 4 + 16, F32)] + [array(width // 4 + 16, BF16)] * 3, (ids,) + parts,
-        )
-        return [own] + to_quad(list(enumerate(sends, 1)))
+        return [parts[0]] + to_quad(list(enumerate(parts[1:], 1)))
 
     def rounded_sum(parts):
         total = parts[0].astype(F32)
@@ -446,9 +458,13 @@
         right = lax.ppermute(right, "row", clockwise)
         left = lax.ppermute(left, "row", counter)
         if s > 0:
+            first = s == far - 1
             terms = backward(
-                [s, n - s], grads, both_sides, grads[0], acc=None, out_dtype=BF16, name="backward_step"
+                [s, n - s], grads, both_sides, grads[0], acc=None, out_dtype=BF16, name="backward_step",
+                cut_at=at_quad if first else None, weights=weights if first else (),
             )
+            if first:
+                terms, *weights = terms
         else:
             terms = backward(
                 [0], grads, both_sides, grads[0], acc=None, out_dtype=F32, name="backward_own"

time: 109 us -> 109 us (level)
    ppermute x4, waiting for transfers between devices: 0.79 us -> 2.44 us  [local(): right = lax.ppermute(right, 'row', clockwise)]
    ppermute x4, waiting for transfers between devices: 11.8 us -> 10.5 us  [local(): left = lax.ppermute(left, 'row', counter)]
    pallas_call x3 -> x2, Pallas kernels: 2.54 us -> 1.94 us  [small_call(): pl.pallas_call(kernel, in_specs=[smem_spec()] + [vmem_spec()] * (len(args...]
where the time goes in v6:
time: 109 us
  Pallas kernels  41.5 us (38%)
  starting transfers between devices  28.3 us (26%)
  waiting for transfers between devices  26 us (24%)
  local copies, waits for them, and re-layouts  5.74 us (5%)
  other arithmetic  4.84 us (4%)
  between operations  1.69 us (2%)
    pallas_call x4, Pallas kernels, forward_mm(): pl.pallas_call(partial(forward_kernel, tuple(cols), side_at, block_rows,...  16.2 us
    pallas_call x4, Pallas kernels, backward_mm(): pl.pallas_call(partial(backward_kernel, tuple(cols), tuple(sides), block_...  14.1 us
    ppermute x4, waiting for transfers between devices, local(): left = lax.ppermute(left, 'row', counter)  10.5 us
    ppermute x3, waiting for transfers between devices, local(): next_left = lax.ppermute(from_left, 'row', clockwise)  9.85 us
    ppermute x6, starting transfers between devices, to_quad(): lax.ppermute(part, axis, [(r, r ^ x) for r in range(n)])  7.19 us
    ppermute x3, starting transfers between devices, local(): next_left = lax.ppermute(from_left, 'row', clockwise)  6.35 us
    unnamed x20, local copies, waits for them, and re-layouts  4.94 us
    ppermute x4, starting transfers between devices, local(): right = lax.ppermute(right, 'row', clockwise)  4.65 us
  transfers between devices with their start and end apart: 28, of which 12 were waited for; matrix products, arithmetic and copies ran while one was open for 5% of the time, Pallas kernels for 35%

profile of v6, /device:TPU:0, one launch (start us, length us, event | category | flops | bytes accessed | tf_op | source)
XLA Modules:
  0.0 108.9 jit_solution(931659823123095090)
XLA Ops:
  0.7 3.1 %collective-permute-start = (bf16[1024,256]{1,0:T(8,128)(2,1)}, bf16[1024,256]{1,0:T(8,128)(2,1)S(1)}, u32[]{:S(2)}, u32[]{:S(2)}) collective-permute-start(bf16[1024,256]{1,0:T(8,128)(2,1)} %refs_0_.1), channel_id=1, source_target_pairs={{0,4},{4,8},{8,12},{12,14},{14,10},{10,6},{6,2},{2,0},{1,5},{5,9},... | collective-permute-start | bytes 1572872 | tf_op jit(solution)/shard_map/ppermute | solution.py:383
  5.1 2.0 %popcnt_reduce_fusion = s32[384,128]{1,0:T(8,128)S(1)} fusion(s32[1,1,384,128,8]{3,4,2,1,0:T(8,128)} %param.13), kind=kLoop, calls=%fused_computation | loop fusion | flops 737280 | bytes 1769472 | tf_op jit(solution)/shard_map/reduce_sum | solution.py:369
  9.4 2.8 %forward_step.4 = (f32[256,2048]{1,0:T(8,128)S(1)}, bf16[256,1024]{1,0:T(8,128)(2,1)S(1)}) custom-call(s32[14]{0:T(128)S(1)} %fusion.7.ids_ref, s32[1024]{0:T(1024)S(1)} %select_reduce_fusion.table_ref, s32[384,8,128]{2,1,0:T(8,128)S(1)} %bitcast.20, bf16[1024,256]{1,0:T(8,128)(2,1)S(1)} %copy-done.4), custom_call_target="tpu_custom_call" | custom-call | flops 1024 | bytes 1024 | tf_op jit(solution)/shard_map/forward_step/pallas_call | solution.py:95
  13.6 2.3 %collective-permute-done.refs_0_ = bf16[1024,256]{1,0:T(8,128)(2,1)S(1)} collective-permute-done((bf16[1024,256]{1,0:T(8,128)(2,1)}, bf16[1024,256]{1,0:T(8,128)(2,1)S(1)}, u32[]{:S(2)}, u32[]{:S(2)}) %collective-permute-start) | collective-permute-done | bytes 524320 | tf_op jit(solution)/shard_map/ppermute | solution.py:383
  15.8 1.8 %collective-permute-start.3 = (bf16[1024,256]{1,0:T(8,128)(2,1)S(1)}, bf16[1024,256]{1,0:T(8,128)(2,1)S(1)}, u32[]{:S(2)}, u32[]{:S(2)}) collective-permute-start(bf16[1024,256]{1,0:T(8,128)(2,1)S(1)} %collective-permute-done.refs_0_), channel_id=1, source_target_pairs={{0,4},{4,8},{8,12},{12,14},{14,10},{10,6},{6,2},{2,0},{1,5},{5,9},... | collective-permute-start | bytes 1572872 | tf_op jit(solution)/shard_map/ppermute | solution.py:383
  17.9 1.6 %copy-done.3 = f32[256,2048]{1,0:T(8,128)S(1)} copy-done((f32[256,2048]{1,0:T(8,128)S(1)}, f32[256,2048]{1,0:T(8,128)}, u32[]{:S(2)}) %copy-start.3) | copy-done | bytes 2097176
  19.4 4.5 %forward_step.5.refs_2_ = f32[256,2048]{1,0:T(8,128)S(1)} custom-call(s32[14]{0:T(128)S(1)} %fusion.7.ids_ref, s32[1024]{0:T(1024)S(1)} %select_reduce_fusion.table_ref, s32[384,8,128]{2,1,0:T(8,128)S(1)} %bitcast.21, bf16[1024,256]{1,0:T(8,128)(2,1)S(1)} %collective-permute-done.refs_0_, bf16[1024,256]{1,0:T(8,128)(2,1)S(1)} %collective-permute-done.2.refs_1_, ...), custom_call_target="tpu_custom_call" | custom-call | flops 1024 | bytes 1024 | tf_op jit(solution)/shard_map/forward_step/pallas_call | solution.py:95
  24.0 1.7 %far_tiles.1.tiles_ref = bf16[1024,2048]{1,0:T(8,128)(2,1)S(1)} custom-call(s32[14]{0:T(128)S(1)} %fusion.7.ids_ref, s32[1024]{0:T(1024)S(1)} %select_reduce_fusion.table_ref, s32[384,8,128]{2,1,0:T(8,128)S(1)} %bitcast.22), custom_call_target="tpu_custom_call" | custom-call | flops 1024 | bytes 1024 | tf_op jit(solution)/shard_map/far_tiles/pallas_call | solution.py:115
  27.0 1.9 %collective-permute-done.3.refs_0_ = bf16[1024,256]{1,0:T(8,128)(2,1)S(1)} collective-permute-done((bf16[1024,256]{1,0:T(8,128)(2,1)S(1)}, bf16[1024,256]{1,0:T(8,128)(2,1)S(1)}, u32[]{:S(2)}, u32[]{:S(2)}) %collective-permute-start.3) | collective-permute-done | bytes 524320 | tf_op jit(solution)/shard_map/ppermute | solution.py:383
  31.0 4.5 %forward_step.6.refs_2_ = f32[256,2048]{1,0:T(8,128)S(1)} custom-call(s32[14]{0:T(128)S(1)} %fusion.7.ids_ref, s32[1024]{0:T(1024)S(1)} %select_reduce_fusion.table_ref, s32[384,8,128]{2,1,0:T(8,128)S(1)} %bitcast.23, bf16[1024,256]{1,0:T(8,128)(2,1)S(1)} %collective-permute-done.3.refs_0_, bf16[1024,256]{1,0:T(8,128)(2,1)S(1)} %collective-permute-done.4.refs_1_, ...), custom_call_target="tpu_custom_call" | custom-call | flops 1024 | bytes 1024 | tf_op jit(solution)/shard_map/forward_step/pallas_call | solution.py:95
  35.5 5.7 %collective-permute-done.5.refs_0_ = bf16[1024,256]{1,0:T(8,128)(2,1)S(1)} collective-permute-done((bf16[1024,256]{1,0:T(8,128)(2,1)S(1)}, bf16[1024,256]{1,0:T(8,128)(2,1)S(1)}, u32[]{:S(2)}, u32[]{:S(2)}) %collective-permute-start.5) | collective-permute-done | bytes 524320 | tf_op jit(solution)/shard_map/ppermute | solution.py:383
  43.5 4.5 %forward_step.7.acc_ref = f32[256,2048]{1,0:T(8,128)S(1)} custom-call(s32[14]{0:T(128)S(1)} %fusion.7.ids_ref, s32[1024]{0:T(1024)S(1)} %select_reduce_fusion.table_ref, s32[384,8,128]{2,1,0:T(8,128)S(1)} %bitcast.24, bf16[1024,256]{1,0:T(8,128)(2,1)S(1)} %collective-permute-done.5.refs_0_, bf16[1024,256]{1,0:T(8,128)(2,1)S(1)} %collective-permute-done.6.refs_1_, ...), custom_call_target="tpu_custom_call" | custom-call | flops 1024 | bytes 1024 | tf_op jit(solution)/shard_map/forward_step/pallas_call | solution.py:95
  52.4 2.5 %layer.1 = (bf16[1024,256]{1,0:T(8,128)(2,1)}, bf16[1024,256]{1,0:T(8,128)(2,1)S(1)}, bf16[1024,256]{1,0:T(8,128)(2,1)S(1)}, f32[320,256]{1,0:T(8,128)S(1)}, f32[320,256]{1,0:T(8,128)S(1)}) custom-call(s32[14]{0:T(128)S(1)} %fusion.7.ids_ref, f32[256,1024]{1,0:T(8,128)S(1)} %forward_keep.1.agg_ref, bf16[256,1024]{1,0:T(8,128)(2,1)S(1)} %collective-permute-done.9.other_ref, ...), custom_call_target="tpu_custom_call" | custom-call | flops 1024 | bytes 1024 | tf_op jit(solution)/shard_map/layer/pallas_call | solution.py:211
  60.2 4.0 %backward_step.3 = (bf16[2048,256]{1,0:T(8,128)(2,1)S(1)}, f32[80,256]{1,0:T(8,128)S(1)}, bf16[80,256]{1,0:T(8,128)(2,1)S(1)}, bf16[80,256]{1,0:T(8,128)(2,1)S(1)}, bf16[80,256]{1,0:T(8,128)(2,1)S(1)}) custom-call(s32[14]{0:T(128)S(1)} %fusion.7.ids_ref, s32[1024]{0:T(1024)S(1)} %select_reduce_fusion.table_ref, s32[384,8,128]{2,1,0:T(8,128)S(1)} %bitcast.25, ...), custom_call_target="tpu_custom_call" | custom-call | flops 8589934592 | bytes 3670016 | tf_op jit(solution)/shard_map/backward_step/pallas_call | solution.py:278
  70.0 3.9 %backward_step.4 = bf16[2048,256]{1,0:T(8,128)(2,1)S(1)} custom-call(s32[14]{0:T(128)S(1)} %fusion.7.ids_ref, s32[1024]{0:T(1024)S(1)} %select_reduce_fusion.table_ref, s32[384,8,128]{2,1,0:T(8,128)S(1)} %bitcast.26, bf16[1024,256]{1,0:T(8,128)(2,1)S(1)} %get-tuple-element.169.grad_ref.after_ref.refs_0_, ...), custom_call_target="tpu_custom_call" | custom-call | flops 8589934592 | bytes 3670016 | tf_op jit(solution)/shard_map/backward_step/pallas_call | solution.py:278
  74.1 2.7 %collective-permute-start.19 = (bf16[80,256]{1,0:T(8,128)(2,1)S(1)}, bf16[80,256]{1,0:T(8,128)(2,1)S(1)}, u32[]{:S(2)}, u32[]{:S(2)}) collective-permute-start(bf16[80,256]{1,0:T(8,128)(2,1)S(1)} %add_convert_fusion.8), channel_id=1, source_target_pairs={{0,8},{2,10},{4,12},{6,14},{8,0},{10,2},{12,4},{14,6},{1,9},{3,11}... | collective-permute-start | bytes 122888 | tf_op jit(solution)/shard_map/ppermute | solution.py:439
  76.7 4.8 %collective-permute-done.18 = bf16[1024,256]{1,0:T(8,128)(2,1)S(1)} collective-permute-done((bf16[1024,256]{1,0:T(8,128)(2,1)S(1)}, bf16[1024,256]{1,0:T(8,128)(2,1)S(1)}, u32[]{:S(2)}, u32[]{:S(2)}) %collective-permute-start.18) | collective-permute-done | bytes 524320 | tf_op jit(solution)/shard_map/ppermute | solution.py:459
  81.8 1.9 %collective-permute-start.21 = (bf16[1024,256]{1,0:T(8,128)(2,1)S(1)}, bf16[1024,256]{1,0:T(8,128)(2,1)S(1)}, u32[]{:S(2)}, u32[]{:S(2)}) collective-permute-start(bf16[1024,256]{1,0:T(8,128)(2,1)S(1)} %get-tuple-element.170), channel_id=1, source_target_pairs={{4,0},{8,4},{12,8},{14,12},{10,14},{6,10},{2,6},{0,2},{5,1},{9,5},... | collective-permute-start | bytes 1572872 | tf_op jit(solution)/shard_map/ppermute | solution.py:459
  83.9 3.9 %backward_step.5 = bf16[2048,256]{1,0:T(8,128)(2,1)S(1)} custom-call(s32[14]{0:T(128)S(1)} %fusion.7.ids_ref, s32[1024]{0:T(1024)S(1)} %select_reduce_fusion.table_ref, s32[384,8,128]{2,1,0:T(8,128)S(1)} %bitcast.27, bf16[1024,256]{1,0:T(8,128)(2,1)S(1)} %get-tuple-element.169.grad_ref.after_ref.refs_0_, ...), custom_call_target="tpu_custom_call" | custom-call | flops 8589934592 | bytes 3670016 | tf_op jit(solution)/shard_map/backward_step/pallas_call | solution.py:278
  87.9 3.0 %collective-permute-start.24 = (bf16[80,256]{1,0:T(8,128)(2,1)S(1)}, bf16[80,256]{1,0:T(8,128)(2,1)S(1)}, u32[]{:S(2)}, u32[]{:S(2)}) collective-permute-start(bf16[80,256]{1,0:T(8,128)(2,1)S(1)} %add_convert_fusion.7.refs_0_), channel_id=1, source_target_pairs={{0,6},{2,4},{4,2},{6,0},{8,14},{10,12},{12,10},{14,8},{1,7},{3,5},... | collective-permute-start | bytes 122888 | tf_op jit(solution)/shard_map/ppermute | solution.py:426
  91.5 3.9 %collective-permute-done.21 = bf16[1024,256]{1,0:T(8,128)(2,1)S(1)} collective-permute-done((bf16[1024,256]{1,0:T(8,128)(2,1)S(1)}, bf16[1024,256]{1,0:T(8,128)(2,1)S(1)}, u32[]{:S(2)}, u32[]{:S(2)}) %collective-permute-start.21) | collective-permute-done | bytes 524320 | tf_op jit(solution)/shard_map/ppermute | solution.py:459
  97.4 1.8 %collective-permute-start.25 = (bf16[1024,256]{1,0:T(8,128)(2,1)S(1)}, bf16[1024,256]{1,0:T(8,128)(2,1)S(1)}, u32[]{:S(2)}, u32[]{:S(2)}) collective-permute-start(bf16[1024,256]{1,0:T(8,128)(2,1)S(1)} %get-tuple-element.178), channel_id=1, source_target_pairs={{0,4},{4,8},{8,12},{12,14},{14,10},{10,6},{6,2},{2,0},{1,5},{5,9},... | collective-permute-start | bytes 1572872 | tf_op jit(solution)/shard_map/ppermute | solution.py:458
  99.3 2.2 %backward_own.1 = f32[1024,256]{1,0:T(8,128)S(1)} custom-call(s32[14]{0:T(128)S(1)} %fusion.7.ids_ref, s32[1024]{0:T(1024)S(1)} %select_reduce_fusion.table_ref, s32[384,8,128]{2,1,0:T(8,128)S(1)} %bitcast.28, bf16[1024,256]{1,0:T(8,128)(2,1)S(1)} %get-tuple-element.169.grad_ref.after_ref.refs_0_, ...), custom_call_target="tpu_custom_call" | custom-call | flops 4294967296 | bytes 2621440 | tf_op jit(solution)/shard_map/backward_own/pallas_call | solution.py:278
  105.3 1.8 %collective-permute-done.26 = bf16[1024,256]{1,0:T(8,128)(2,1)S(1)} collective-permute-done((bf16[1024,256]{1,0:T(8,128)(2,1)S(1)}, bf16[1024,256]{1,0:T(8,128)(2,1)S(1)}, u32[]{:S(2)}, u32[]{:S(2)}) %collective-permute-start.26) | collective-permute-done | bytes 524320 | tf_op jit(solution)/shard_map/ppermute | solution.py:459
  (91 shorter events, 34.6 us)
Async XLA Ops:
  0.7 15.2 %collective-permute-start = (bf16[1024,256]{1,0:T(8,128)(2,1)}, bf16[1024,256]{1,0:T(8,128)(2,1)S(1)}, u32[]{:S(2)}, u32[]{:S(2)}) collective-permute-start(bf16[1024,256]{1,0:T(8,128)(2,1)} %refs_0_.1), channel_id=1, source_target_pairs={{0,4},{4,8},{8,12},{12,14},{14,10},{10,6},{6,2},{2,0},{1,5},{5,9},... | collective-permute-start | bytes 1572872 | tf_op jit(solution)/shard_map/ppermute | solution.py:383
  3.7 13.9 %collective-permute-start.2 = (bf16[1024,256]{1,0:T(8,128)(2,1)}, bf16[1024,256]{1,0:T(8,128)(2,1)S(1)}, u32[]{:S(2)}, u32[]{:S(2)}) collective-permute-start(bf16[1024,256]{1,0:T(8,128)(2,1)} %refs_0_.1), channel_id=1, source_target_pairs={{4,0},{8,4},{12,8},{14,12},{10,14},{6,10},{2,6},{0,2},{5,1},{9,5},... | collective-permute-start | bytes 1572872 | tf_op jit(solution)/shard_map/ppermute | solution.py:384
  7.3 6.3 %collective-permute-start.1 = (f32[1,1024]{1,0:T(1,128)S(1)}, f32[1,1024]{1,0:T(1,128)S(1)}, u32[]{:S(2)}, u32[]{:S(2)}) collective-permute-start(f32[1,1024]{1,0:T(1,128)S(1)} %dynamic-slice_bitcast_fusion), channel_id=1, source_target_pairs={{0,1},{1,0},{2,3},{3,2},{4,5},{5,4},{6,7},{7,6},{8,9},{9,8},{10,11... | collective-permute-start | bytes 12296 | tf_op jit(solution)/shard_map/ppermute | solution.py:372
  15.8 13.1 %collective-permute-start.3 = (bf16[1024,256]{1,0:T(8,128)(2,1)S(1)}, bf16[1024,256]{1,0:T(8,128)(2,1)S(1)}, u32[]{:S(2)}, u32[]{:S(2)}) collective-permute-start(bf16[1024,256]{1,0:T(8,128)(2,1)S(1)} %collective-permute-done.refs_0_), channel_id=1, source_target_pairs={{0,4},{4,8},{8,12},{12,14},{14,10},{10,6},{6,2},{2,0},{1,5},{5,9},... | collective-permute-start | bytes 1572872 | tf_op jit(solution)/shard_map/ppermute | solution.py:383
  17.6 12.8 %collective-permute-start.4 = (bf16[1024,256]{1,0:T(8,128)(2,1)S(1)}, bf16[1024,256]{1,0:T(8,128)(2,1)S(1)}, u32[]{:S(2)}, u32[]{:S(2)}) collective-permute-start(bf16[1024,256]{1,0:T(8,128)(2,1)S(1)} %collective-permute-done.2.refs_1_), channel_id=1, source_target_pairs={{4,0},{8,4},{12,8},{14,12},{10,14},{6,10},{2,6},{0,2},{5,1},{9,5},... | collective-permute-start | bytes 1572872 | tf_op jit(solution)/shard_map/ppermute | solution.py:384
  28.9 12.2 %collective-permute-start.5 = (bf16[1024,256]{1,0:T(8,128)(2,1)S(1)}, bf16[1024,256]{1,0:T(8,128)(2,1)S(1)}, u32[]{:S(2)}, u32[]{:S(2)}) collective-permute-start(bf16[1024,256]{1,0:T(8,128)(2,1)S(1)} %collective-permute-done.3.refs_0_), channel_id=1, source_target_pairs={{0,4},{4,8},{8,12},{12,14},{14,10},{10,6},{6,2},{2,0},{1,5},{5,9},... | collective-permute-start | bytes 1572872 | tf_op jit(solution)/shard_map/ppermute | solution.py:383
  30.4 12.1 %collective-permute-start.6 = (bf16[1024,256]{1,0:T(8,128)(2,1)S(1)}, bf16[1024,256]{1,0:T(8,128)(2,1)S(1)}, u32[]{:S(2)}, u32[]{:S(2)}) collective-permute-start(bf16[1024,256]{1,0:T(8,128)(2,1)S(1)} %collective-permute-done.4.refs_1_), channel_id=1, source_target_pairs={{4,0},{8,4},{12,8},{14,12},{10,14},{6,10},{2,6},{0,2},{5,1},{9,5},... | collective-permute-start | bytes 1572872 | tf_op jit(solution)/shard_map/ppermute | solution.py:384
  41.1 6.8 %collective-permute-start.7 = (bf16[512,256]{1,0:T(8,128)(2,1)S(1)}, bf16[512,256]{1,0:T(8,128)(2,1)S(1)}, u32[]{:S(2)}, u32[]{:S(2)}) collective-permute-start(bf16[512,256]{1,0:T(8,128)(2,1)S(1)} %slice.30), channel_id=1, source_target_pairs={{0,4},{4,8},{8,12},{12,14},{14,10},{10,6},{6,2},{2,0},{1,5},{5,9},... | collective-permute-start | bytes 786440 | tf_op jit(solution)/shard_map/ppermute | solution.py:387
  42.5 6.6 %collective-permute-start.8 = (bf16[512,256]{1,0:T(8,128)(2,1)S(1)}, bf16[512,256]{1,0:T(8,128)(2,1)S(1)}, u32[]{:S(2)}, u32[]{:S(2)}) collective-permute-start(bf16[512,256]{1,0:T(8,128)(2,1)S(1)} %slice.31), channel_id=1, source_target_pairs={{4,0},{8,4},{12,8},{14,12},{10,14},{6,10},{2,6},{0,2},{5,1},{9,5},... | collective-permute-start | bytes 786440 | tf_op jit(solution)/shard_map/ppermute | solution.py:388
  58.1 9.6 %collective-permute-start.13 = (bf16[512,256]{1,0:T(8,128)(2,1)S(1)}, bf16[512,256]{1,0:T(8,128)(2,1)S(1)}, u32[]{:S(2)}, u32[]{:S(2)}) collective-permute-start(bf16[512,256]{1,0:T(8,128)(2,1)S(1)} %get-tuple-element.146), channel_id=1, source_target_pairs={{4,0},{8,4},{12,8},{14,12},{10,14},{6,10},{2,6},{0,2},{5,1},{9,5},... | collective-permute-start | bytes 786440 | tf_op jit(solution)/shard_map/ppermute | solution.py:459
  58.9 8.8 %collective-permute-start.12 = (bf16[512,256]{1,0:T(8,128)(2,1)S(1)}, bf16[512,256]{1,0:T(8,128)(2,1)S(1)}, u32[]{:S(2)}, u32[]{:S(2)}) collective-permute-start(bf16[512,256]{1,0:T(8,128)(2,1)S(1)} %get-tuple-element.143), channel_id=1, source_target_pairs={{0,4},{4,8},{8,12},{12,14},{14,10},{10,6},{6,2},{2,0},{1,5},{5,9},... | collective-permute-start | bytes 786440 | tf_op jit(solution)/shard_map/ppermute | solution.py:458
  64.2 9.8 %collective-permute-start.14 = (bf16[80,256]{1,0:T(8,128)(2,1)S(1)}, bf16[80,256]{1,0:T(8,128)(2,1)S(1)}, u32[]{:S(2)}, u32[]{:S(2)}) collective-permute-start(bf16[80,256]{1,0:T(8,128)(2,1)S(1)} %get-tuple-element.150), channel_id=1, source_target_pairs={{0,2},{2,0},{4,6},{6,4},{8,10},{10,8},{12,14},{14,12},{1,3},{3,1},... | collective-permute-start | bytes 122888 | tf_op jit(solution)/shard_map/ppermute | solution.py:426
  65.0 9.0 %collective-permute-start.15 = (bf16[80,256]{1,0:T(8,128)(2,1)S(1)}, bf16[80,256]{1,0:T(8,128)(2,1)S(1)}, u32[]{:S(2)}, u32[]{:S(2)}) collective-permute-start(bf16[80,256]{1,0:T(8,128)(2,1)S(1)} %get-tuple-element.151), channel_id=1, source_target_pairs={{0,4},{2,6},{4,0},{6,2},{8,12},{10,14},{12,8},{14,10},{1,5},{3,7},... | collective-permute-start | bytes 122888 | tf_op jit(solution)/shard_map/ppermute | solution.py:426
  66.2 7.8 %collective-permute-start.16 = (bf16[80,256]{1,0:T(8,128)(2,1)S(1)}, bf16[80,256]{1,0:T(8,128)(2,1)S(1)}, u32[]{:S(2)}, u32[]{:S(2)}) collective-permute-start(bf16[80,256]{1,0:T(8,128)(2,1)S(1)} %get-tuple-element.152), channel_id=1, source_target_pairs={{0,6},{2,4},{4,2},{6,0},{8,14},{10,12},{12,10},{14,8},{1,7},{3,5},... | collective-permute-start | bytes 122888 | tf_op jit(solution)/shard_map/ppermute | solution.py:426
  68.0 13.6 %collective-permute-start.18 = (bf16[1024,256]{1,0:T(8,128)(2,1)S(1)}, bf16[1024,256]{1,0:T(8,128)(2,1)S(1)}, u32[]{:S(2)}, u32[]{:S(2)}) collective-permute-start(bf16[1024,256]{1,0:T(8,128)(2,1)S(1)} %get-tuple-element.158), channel_id=1, source_target_pairs={{4,0},{8,4},{12,8},{14,12},{10,14},{6,10},{2,6},{0,2},{5,1},{9,5},... | collective-permute-start | bytes 1572872 | tf_op jit(solution)/shard_map/ppermute | solution.py:459
  68.8 12.8 %collective-permute-start.17 = (bf16[1024,256]{1,0:T(8,128)(2,1)S(1)}, bf16[1024,256]{1,0:T(8,128)(2,1)S(1)}, u32[]{:S(2)}, u32[]{:S(2)}) collective-permute-start(bf16[1024,256]{1,0:T(8,128)(2,1)S(1)} %get-tuple-element.155), channel_id=1, source_target_pairs={{0,4},{4,8},{8,12},{12,14},{14,10},{10,6},{6,2},{2,0},{1,5},{5,9},... | collective-permute-start | bytes 1572872 | tf_op jit(solution)/shard_map/ppermute | solution.py:458
  74.1 13.8 %collective-permute-start.19 = (bf16[80,256]{1,0:T(8,128)(2,1)S(1)}, bf16[80,256]{1,0:T(8,128)(2,1)S(1)}, u32[]{:S(2)}, u32[]{:S(2)}) collective-permute-start(bf16[80,256]{1,0:T(8,128)(2,1)S(1)} %add_convert_fusion.8), channel_id=1, source_target_pairs={{0,8},{2,10},{4,12},{6,14},{8,0},{10,2},{12,4},{14,6},{1,9},{3,11}... | collective-permute-start | bytes 122888 | tf_op jit(solution)/shard_map/ppermute | solution.py:439
  81.8 13.6 %collective-permute-start.21 = (bf16[1024,256]{1,0:T(8,128)(2,1)S(1)}, bf16[1024,256]{1,0:T(8,128)(2,1)S(1)}, u32[]{:S(2)}, u32[]{:S(2)}) collective-permute-start(bf16[1024,256]{1,0:T(8,128)(2,1)S(1)} %get-tuple-element.170), channel_id=1, source_target_pairs={{4,0},{8,4},{12,8},{14,12},{10,14},{6,10},{2,6},{0,2},{5,1},{9,5},... | collective-permute-start | bytes 1572872 | tf_op jit(solution)/shard_map/ppermute | solution.py:459
  83.7 13.2 %collective-permute-start.20 = (bf16[1024,256]{1,0:T(8,128)(2,1)S(1)}, bf16[1024,256]{1,0:T(8,128)(2,1)S(1)}, u32[]{:S(2)}, u32[]{:S(2)}) collective-permute-start(bf16[1024,256]{1,0:T(8,128)(2,1)S(1)} %get-tuple-element.167), channel_id=1, source_target_pairs={{0,4},{4,8},{8,12},{12,14},{14,10},{10,6},{6,2},{2,0},{1,5},{5,9},... | collective-permute-start | bytes 1572872 | tf_op jit(solution)/shard_map/ppermute | solution.py:458
  87.9 14.0 %collective-permute-start.24 = (bf16[80,256]{1,0:T(8,128)(2,1)S(1)}, bf16[80,256]{1,0:T(8,128)(2,1)S(1)}, u32[]{:S(2)}, u32[]{:S(2)}) collective-permute-start(bf16[80,256]{1,0:T(8,128)(2,1)S(1)} %add_convert_fusion.7.refs_0_), channel_id=1, source_target_pairs={{0,6},{2,4},{4,2},{6,0},{8,14},{10,12},{12,10},{14,8},{1,7},{3,5},... | collective-permute-start | bytes 122888 | tf_op jit(solution)/shard_map/ppermute | solution.py:426
  90.9 11.0 %collective-permute-start.23 = (bf16[80,256]{1,0:T(8,128)(2,1)S(1)}, bf16[80,256]{1,0:T(8,128)(2,1)S(1)}, u32[]{:S(2)}, u32[]{:S(2)}) collective-permute-start(bf16[80,256]{1,0:T(8,128)(2,1)S(1)} %add_convert_fusion.7.refs_0_), channel_id=1, source_target_pairs={{0,4},{2,6},{4,0},{6,2},{8,12},{10,14},{12,8},{14,10},{1,5},{3,7},... | collective-permute-start | bytes 122888 | tf_op jit(solution)/shard_map/ppermute | solution.py:426
  91.3 10.6 %collective-permute-start.22 = (bf16[80,256]{1,0:T(8,128)(2,1)S(1)}, bf16[80,256]{1,0:T(8,128)(2,1)S(1)}, u32[]{:S(2)}, u32[]{:S(2)}) collective-permute-start(bf16[80,256]{1,0:T(8,128)(2,1)S(1)} %add_convert_fusion.7.refs_0_), channel_id=1, source_target_pairs={{0,2},{2,0},{4,6},{6,4},{8,10},{10,8},{12,14},{14,12},{1,3},{3,1},... | collective-permute-start | bytes 122888 | tf_op jit(solution)/shard_map/ppermute | solution.py:426
  97.2 9.8 %collective-permute-start.26 = (bf16[1024,256]{1,0:T(8,128)(2,1)S(1)}, bf16[1024,256]{1,0:T(8,128)(2,1)S(1)}, u32[]{:S(2)}, u32[]{:S(2)}) collective-permute-start(bf16[1024,256]{1,0:T(8,128)(2,1)S(1)} %get-tuple-element.179), channel_id=1, source_target_pairs={{4,0},{8,4},{12,8},{14,12},{10,14},{6,10},{2,6},{0,2},{5,1},{9,5},... | collective-permute-start | bytes 1572872 | tf_op jit(solution)/shard_map/ppermute | solution.py:459
  97.4 10.5 %collective-permute-start.25 = (bf16[1024,256]{1,0:T(8,128)(2,1)S(1)}, bf16[1024,256]{1,0:T(8,128)(2,1)S(1)}, u32[]{:S(2)}, u32[]{:S(2)}) collective-permute-start(bf16[1024,256]{1,0:T(8,128)(2,1)S(1)} %get-tuple-element.178), channel_id=1, source_target_pairs={{0,4},{4,8},{8,12},{12,14},{14,10},{10,6},{6,2},{2,0},{1,5},{5,9},... | collective-permute-start | bytes 1572872 | tf_op jit(solution)/shard_map/ppermute | solution.py:458
  (14 other events, 59.8 us)

commit v7 on v5

--- a/solution.py
+++ b/solution.py
@@ -407,7 +407,10 @@
         return jax.ShapeDtypeStruct((rows, width), dtype)
 
     def to_quad(parts, axis="row"):
-        return [lax.ppermute(part, axis, [(r, r ^ x) for r in range(n)]) for x, part in parts]
+        sent = {
+            x: lax.ppermute(part, axis, [(r, r ^ x) for r in range(n)]) for x, part in reversed(parts)
+        }
+        return [sent[x] for x, _ in parts]
 
     def start_quad(parts):
         own, *sends = small_call(

time: 109 us -> 109 us (level)
  no operation moved by 1% of the time
where the time goes in v7:
time: 109 us
  Pallas kernels  42.2 us (39%)
  starting transfers between devices  28.3 us (26%)
  waiting for transfers between devices  25.6 us (23%)
  local copies, waits for them, and re-layouts  5.74 us (5%)
  other arithmetic  4.9 us (4%)
  between operations  1.7 us (2%)
    pallas_call x4, Pallas kernels, forward_mm(): pl.pallas_call(partial(forward_kernel, tuple(cols), side_at, block_rows,...  16.3 us
    pallas_call x4, Pallas kernels, backward_mm(): pl.pallas_call(partial(backward_kernel, tuple(cols), tuple(sides), block_...  14.1 us
    ppermute x4, waiting for transfers between devices, local(): left = lax.ppermute(left, 'row', counter)  11.8 us
    ppermute x3, waiting for transfers between devices, local(): next_left = lax.ppermute(from_left, 'row', clockwise)  9.83 us
    ppermute x6, starting transfers between devices, to_quad(): lax.ppermute(part, axis, [(r, r ^ x) for r in range(n)])  7.1 us
    ppermute x3, starting transfers between devices, local(): next_left = lax.ppermute(from_left, 'row', clockwise)  6.35 us
    unnamed x20, local copies, waits for them, and re-layouts  4.94 us
    ppermute x4, starting transfers between devices, local(): left = lax.ppermute(left, 'row', counter)  4.57 us
  transfers between devices with their start and end apart: 28, of which 12 were waited for; matrix products, arithmetic and copies ran while one was open for 5% of the time, Pallas kernels for 35%

profile of v7, /device:TPU:0, one launch (start us, length us, event | category | flops | bytes accessed | tf_op | source)
XLA Modules:
  0.0 109.1 jit_solution(8646917174368619729)
XLA Ops:
  0.7 3.1 %collective-permute-start = (bf16[1024,256]{1,0:T(8,128)(2,1)}, bf16[1024,256]{1,0:T(8,128)(2,1)S(1)}, u32[]{:S(2)}, u32[]{:S(2)}) collective-permute-start(bf16[1024,256]{1,0:T(8,128)(2,1)} %refs_0_.1), channel_id=1, source_target_pairs={{0,4},{4,8},{8,12},{12,14},{14,10},{10,6},{6,2},{2,0},{1,5},{5,9},... | collective-permute-start | bytes 1572872 | tf_op jit(solution)/shard_map/ppermute | solution.py:367
  5.1 2.0 %popcnt_reduce_fusion = s32[384,128]{1,0:T(8,128)S(1)} fusion(s32[1,1,384,128,8]{3,4,2,1,0:T(8,128)} %param.13), kind=kLoop, calls=%fused_computation | loop fusion | flops 737280 | bytes 1769472 | tf_op jit(solution)/shard_map/reduce_sum | solution.py:353
  9.4 2.8 %forward_step.4 = (f32[256,2048]{1,0:T(8,128)S(1)}, bf16[256,1024]{1,0:T(8,128)(2,1)S(1)}) custom-call(s32[14]{0:T(128)S(1)} %fusion.7.ids_ref, s32[1024]{0:T(1024)S(1)} %select_reduce_fusion.table_ref, s32[384,8,128]{2,1,0:T(8,128)S(1)} %bitcast.20, bf16[1024,256]{1,0:T(8,128)(2,1)S(1)} %copy-done.4), custom_call_target="tpu_custom_call" | custom-call | flops 1024 | bytes 1024 | tf_op jit(solution)/shard_map/forward_step/pallas_call | solution.py:95
  13.6 2.2 %collective-permute-done.refs_0_ = bf16[1024,256]{1,0:T(8,128)(2,1)S(1)} collective-permute-done((bf16[1024,256]{1,0:T(8,128)(2,1)}, bf16[1024,256]{1,0:T(8,128)(2,1)S(1)}, u32[]{:S(2)}, u32[]{:S(2)}) %collective-permute-start) | collective-permute-done | bytes 524320 | tf_op jit(solution)/shard_map/ppermute | solution.py:367
  15.8 1.8 %collective-permute-start.3 = (bf16[1024,256]{1,0:T(8,128)(2,1)S(1)}, bf16[1024,256]{1,0:T(8,128)(2,1)S(1)}, u32[]{:S(2)}, u32[]{:S(2)}) collective-permute-start(bf16[1024,256]{1,0:T(8,128)(2,1)S(1)} %collective-permute-done.refs_0_), channel_id=1, source_target_pairs={{0,4},{4,8},{8,12},{12,14},{14,10},{10,6},{6,2},{2,0},{1,5},{5,9},... | collective-permute-start | bytes 1572872 | tf_op jit(solution)/shard_map/ppermute | solution.py:367
  17.9 1.6 %copy-done.3 = f32[256,2048]{1,0:T(8,128)S(1)} copy-done((f32[256,2048]{1,0:T(8,128)S(1)}, f32[256,2048]{1,0:T(8,128)}, u32[]{:S(2)}) %copy-start.3) | copy-done | bytes 2097176
  19.4 4.5 %forward_step.5.refs_2_ = f32[256,2048]{1,0:T(8,128)S(1)} custom-call(s32[14]{0:T(128)S(1)} %fusion.7.ids_ref, s32[1024]{0:T(1024)S(1)} %select_reduce_fusion.table_ref, s32[384,8,128]{2,1,0:T(8,128)S(1)} %bitcast.21, bf16[1024,256]{1,0:T(8,128)(2,1)S(1)} %collective-permute-done.refs_0_, bf16[1024,256]{1,0:T(8,128)(2,1)S(1)} %collective-permute-done.2.refs_1_, ...), custom_call_target="tpu_custom_call" | custom-call | flops 1024 | bytes 1024 | tf_op jit(solution)/shard_map/forward_step/pallas_call | solution.py:95
  24.0 1.7 %far_tiles.1.tiles_ref = bf16[1024,2048]{1,0:T(8,128)(2,1)S(1)} custom-call(s32[14]{0:T(128)S(1)} %fusion.7.ids_ref, s32[1024]{0:T(1024)S(1)} %select_reduce_fusion.table_ref, s32[384,8,128]{2,1,0:T(8,128)S(1)} %bitcast.22), custom_call_target="tpu_custom_call" | custom-call | flops 1024 | bytes 1024 | tf_op jit(solution)/shard_map/far_tiles/pallas_call | solution.py:115
  27.0 1.9 %collective-permute-done.3.refs_0_ = bf16[1024,256]{1,0:T(8,128)(2,1)S(1)} collective-permute-done((bf16[1024,256]{1,0:T(8,128)(2,1)S(1)}, bf16[1024,256]{1,0:T(8,128)(2,1)S(1)}, u32[]{:S(2)}, u32[]{:S(2)}) %collective-permute-start.3) | collective-permute-done | bytes 524320 | tf_op jit(solution)/shard_map/ppermute | solution.py:367
  31.0 4.5 %forward_step.6.refs_2_ = f32[256,2048]{1,0:T(8,128)S(1)} custom-call(s32[14]{0:T(128)S(1)} %fusion.7.ids_ref, s32[1024]{0:T(1024)S(1)} %select_reduce_fusion.table_ref, s32[384,8,128]{2,1,0:T(8,128)S(1)} %bitcast.23, bf16[1024,256]{1,0:T(8,128)(2,1)S(1)} %collective-permute-done.3.refs_0_, bf16[1024,256]{1,0:T(8,128)(2,1)S(1)} %collective-permute-done.4.refs_1_, ...), custom_call_target="tpu_custom_call" | custom-call | flops 1024 | bytes 1024 | tf_op jit(solution)/shard_map/forward_step/pallas_call | solution.py:95
  35.5 5.7 %collective-permute-done.5.refs_0_ = bf16[1024,256]{1,0:T(8,128)(2,1)S(1)} collective-permute-done((bf16[1024,256]{1,0:T(8,128)(2,1)S(1)}, bf16[1024,256]{1,0:T(8,128)(2,1)S(1)}, u32[]{:S(2)}, u32[]{:S(2)}) %collective-permute-start.5) | collective-permute-done | bytes 524320 | tf_op jit(solution)/shard_map/ppermute | solution.py:367
  43.5 4.5 %forward_step.7.acc_ref = f32[256,2048]{1,0:T(8,128)S(1)} custom-call(s32[14]{0:T(128)S(1)} %fusion.7.ids_ref, s32[1024]{0:T(1024)S(1)} %select_reduce_fusion.table_ref, s32[384,8,128]{2,1,0:T(8,128)S(1)} %bitcast.24, bf16[1024,256]{1,0:T(8,128)(2,1)S(1)} %collective-permute-done.5.refs_0_, bf16[1024,256]{1,0:T(8,128)(2,1)S(1)} %collective-permute-done.6.refs_1_, ...), custom_call_target="tpu_custom_call" | custom-call | flops 1024 | bytes 1024 | tf_op jit(solution)/shard_map/forward_step/pallas_call | solution.py:95
  52.4 2.5 %layer.1 = (bf16[1024,256]{1,0:T(8,128)(2,1)}, bf16[1024,256]{1,0:T(8,128)(2,1)S(1)}, bf16[1024,256]{1,0:T(8,128)(2,1)S(1)}, f32[320,256]{1,0:T(8,128)S(1)}, f32[320,256]{1,0:T(8,128)S(1)}) custom-call(s32[14]{0:T(128)S(1)} %fusion.7.ids_ref, f32[256,1024]{1,0:T(8,128)S(1)} %forward_keep.1.agg_ref, bf16[256,1024]{1,0:T(8,128)(2,1)S(1)} %collective-permute-done.9.other_ref, ...), custom_call_target="tpu_custom_call" | custom-call | flops 1024 | bytes 1024 | tf_op jit(solution)/shard_map/layer/pallas_call | solution.py:211
  60.2 3.9 %backward_step.3 = bf16[2048,256]{1,0:T(8,128)(2,1)S(1)} custom-call(s32[14]{0:T(128)S(1)} %fusion.7.ids_ref, s32[1024]{0:T(1024)S(1)} %select_reduce_fusion.table_ref, s32[384,8,128]{2,1,0:T(8,128)S(1)} %bitcast.25, bf16[1024,256]{1,0:T(8,128)(2,1)S(1)} %get-tuple-element.173.grad_ref.after_ref.refs_0_, ...), custom_call_target="tpu_custom_call" | custom-call | flops 8589934592 | bytes 3670016 | tf_op jit(solution)/shard_map/backward_step/pallas_call | solution.py:254
  66.8 1.5 %collective-permute-start.16 = (bf16[80,256]{1,0:T(8,128)(2,1)S(1)}, bf16[80,256]{1,0:T(8,128)(2,1)S(1)}, u32[]{:S(2)}, u32[]{:S(2)}) collective-permute-start(bf16[80,256]{1,0:T(8,128)(2,1)S(1)} %get-tuple-element.156), channel_id=1, source_target_pairs={{0,6},{2,4},{4,2},{6,0},{8,14},{10,12},{12,10},{14,8},{1,7},{3,5},... | collective-permute-start | bytes 122888 | tf_op jit(solution)/shard_map/ppermute | solution.py:411
  70.6 4.0 %backward_step.4 = bf16[2048,256]{1,0:T(8,128)(2,1)S(1)} custom-call(s32[14]{0:T(128)S(1)} %fusion.7.ids_ref, s32[1024]{0:T(1024)S(1)} %select_reduce_fusion.table_ref, s32[384,8,128]{2,1,0:T(8,128)S(1)} %bitcast.26, bf16[1024,256]{1,0:T(8,128)(2,1)S(1)} %get-tuple-element.173.grad_ref.after_ref.refs_0_, ...), custom_call_target="tpu_custom_call" | custom-call | flops 8589934592 | bytes 3670016 | tf_op jit(solution)/shard_map/backward_step/pallas_call | solution.py:254
  74.6 2.7 %collective-permute-start.19 = (bf16[80,256]{1,0:T(8,128)(2,1)S(1)}, bf16[80,256]{1,0:T(8,128)(2,1)S(1)}, u32[]{:S(2)}, u32[]{:S(2)}) collective-permute-start(bf16[80,256]{1,0:T(8,128)(2,1)S(1)} %add_convert_fusion.8), channel_id=1, source_target_pairs={{0,8},{2,10},{4,12},{6,14},{8,0},{10,2},{12,4},{14,6},{1,9},{3,11}... | collective-permute-start | bytes 122888 | tf_op jit(solution)/shard_map/ppermute | solution.py:430
  77.3 4.8 %collective-permute-done.18 = bf16[1024,256]{1,0:T(8,128)(2,1)S(1)} collective-permute-done((bf16[1024,256]{1,0:T(8,128)(2,1)S(1)}, bf16[1024,256]{1,0:T(8,128)(2,1)S(1)}, u32[]{:S(2)}, u32[]{:S(2)}) %collective-permute-start.18) | collective-permute-done | bytes 524320 | tf_op jit(solution)/shard_map/ppermute | solution.py:450
  82.4 1.6 %collective-permute-start.21 = (bf16[1024,256]{1,0:T(8,128)(2,1)S(1)}, bf16[1024,256]{1,0:T(8,128)(2,1)S(1)}, u32[]{:S(2)}, u32[]{:S(2)}) collective-permute-start(bf16[1024,256]{1,0:T(8,128)(2,1)S(1)} %get-tuple-element.174), channel_id=1, source_target_pairs={{4,0},{8,4},{12,8},{14,12},{10,14},{6,10},{2,6},{0,2},{5,1},{9,5},... | collective-permute-start | bytes 1572872 | tf_op jit(solution)/shard_map/ppermute | solution.py:450
  84.5 3.9 %backward_step.5 = bf16[2048,256]{1,0:T(8,128)(2,1)S(1)} custom-call(s32[14]{0:T(128)S(1)} %fusion.7.ids_ref, s32[1024]{0:T(1024)S(1)} %select_reduce_fusion.table_ref, s32[384,8,128]{2,1,0:T(8,128)S(1)} %bitcast.27, bf16[1024,256]{1,0:T(8,128)(2,1)S(1)} %get-tuple-element.173.grad_ref.after_ref.refs_0_, ...), custom_call_target="tpu_custom_call" | custom-call | flops 8589934592 | bytes 3670016 | tf_op jit(solution)/shard_map/backward_step/pallas_call | solution.py:254
  88.5 2.7 %collective-permute-start.24 = (bf16[80,256]{1,0:T(8,128)(2,1)S(1)}, bf16[80,256]{1,0:T(8,128)(2,1)S(1)}, u32[]{:S(2)}, u32[]{:S(2)}) collective-permute-start(bf16[80,256]{1,0:T(8,128)(2,1)S(1)} %add_convert_fusion.7.refs_0_), channel_id=1, source_target_pairs={{0,6},{2,4},{4,2},{6,0},{8,14},{10,12},{12,10},{14,8},{1,7},{3,5},... | collective-permute-start | bytes 122888 | tf_op jit(solution)/shard_map/ppermute | solution.py:411
  92.0 3.9 %collective-permute-done.21 = bf16[1024,256]{1,0:T(8,128)(2,1)S(1)} collective-permute-done((bf16[1024,256]{1,0:T(8,128)(2,1)S(1)}, bf16[1024,256]{1,0:T(8,128)(2,1)S(1)}, u32[]{:S(2)}, u32[]{:S(2)}) %collective-permute-start.21) | collective-permute-done | bytes 524320 | tf_op jit(solution)/shard_map/ppermute | solution.py:450
  98.5 2.2 %backward_own.1 = f32[1024,256]{1,0:T(8,128)S(1)} custom-call(s32[14]{0:T(128)S(1)} %fusion.7.ids_ref, s32[1024]{0:T(1024)S(1)} %select_reduce_fusion.table_ref, s32[384,8,128]{2,1,0:T(8,128)S(1)} %bitcast.28, bf16[1024,256]{1,0:T(8,128)(2,1)S(1)} %get-tuple-element.173.grad_ref.after_ref.refs_0_, ...), custom_call_target="tpu_custom_call" | custom-call | flops 4294967296 | bytes 2621440 | tf_op jit(solution)/shard_map/backward_own/pallas_call | solution.py:254
  104.5 3.1 %collective-permute-done.26 = bf16[1024,256]{1,0:T(8,128)(2,1)S(1)} collective-permute-done((bf16[1024,256]{1,0:T(8,128)(2,1)S(1)}, bf16[1024,256]{1,0:T(8,128)(2,1)S(1)}, u32[]{:S(2)}, u32[]{:S(2)}) %collective-permute-start.26) | collective-permute-done | bytes 524320 | tf_op jit(solution)/shard_map/ppermute | solution.py:450
  (92 shorter events, 34.3 us)
Async XLA Ops:
  0.7 15.2 %collective-permute-start = (bf16[1024,256]{1,0:T(8,128)(2,1)}, bf16[1024,256]{1,0:T(8,128)(2,1)S(1)}, u32[]{:S(2)}, u32[]{:S(2)}) collective-permute-start(bf16[1024,256]{1,0:T(8,128)(2,1)} %refs_0_.1), channel_id=1, source_target_pairs={{0,4},{4,8},{8,12},{12,14},{14,10},{10,6},{6,2},{2,0},{1,5},{5,9},... | collective-permute-start | bytes 1572872 | tf_op jit(solution)/shard_map/ppermute | solution.py:367
  3.7 13.9 %collective-permute-start.2 = (bf16[1024,256]{1,0:T(8,128)(2,1)}, bf16[1024,256]{1,0:T(8,128)(2,1)S(1)}, u32[]{:S(2)}, u32[]{:S(2)}) collective-permute-start(bf16[1024,256]{1,0:T(8,128)(2,1)} %refs_0_.1), channel_id=1, source_target_pairs={{4,0},{8,4},{12,8},{14,12},{10,14},{6,10},{2,6},{0,2},{5,1},{9,5},... | collective-permute-start | bytes 1572872 | tf_op jit(solution)/shard_map/ppermute | solution.py:368
  15.8 13.1 %collective-permute-start.3 = (bf16[1024,256]{1,0:T(8,128)(2,1)S(1)}, bf16[1024,256]{1,0:T(8,128)(2,1)S(1)}, u32[]{:S(2)}, u32[]{:S(2)}) collective-permute-start(bf16[1024,256]{1,0:T(8,128)(2,1)S(1)} %collective-permute-done.refs_0_), channel_id=1, source_target_pairs={{0,4},{4,8},{8,12},{12,14},{14,10},{10,6},{6,2},{2,0},{1,5},{5,9},... | collective-permute-start | bytes 1572872 | tf_op jit(solution)/shard_map/ppermute | solution.py:367
  17.6 12.8 %collective-permute-start.4 = (bf16[1024,256]{1,0:T(8,128)(2,1)S(1)}, bf16[1024,256]{1,0:T(8,128)(2,1)S(1)}, u32[]{:S(2)}, u32[]{:S(2)}) collective-permute-start(bf16[1024,256]{1,0:T(8,128)(2,1)S(1)} %collective-permute-done.2.refs_1_), channel_id=1, source_target_pairs={{4,0},{8,4},{12,8},{14,12},{10,14},{6,10},{2,6},{0,2},{5,1},{9,5},... | collective-permute-start | bytes 1572872 | tf_op jit(solution)/shard_map/ppermute | solution.py:368
  28.9 12.2 %collective-permute-start.5 = (bf16[1024,256]{1,0:T(8,128)(2,1)S(1)}, bf16[1024,256]{1,0:T(8,128)(2,1)S(1)}, u32[]{:S(2)}, u32[]{:S(2)}) collective-permute-start(bf16[1024,256]{1,0:T(8,128)(2,1)S(1)} %collective-permute-done.3.refs_0_), channel_id=1, source_target_pairs={{0,4},{4,8},{8,12},{12,14},{14,10},{10,6},{6,2},{2,0},{1,5},{5,9},... | collective-permute-start | bytes 1572872 | tf_op jit(solution)/shard_map/ppermute | solution.py:367
  30.4 12.1 %collective-permute-start.6 = (bf16[1024,256]{1,0:T(8,128)(2,1)S(1)}, bf16[1024,256]{1,0:T(8,128)(2,1)S(1)}, u32[]{:S(2)}, u32[]{:S(2)}) collective-permute-start(bf16[1024,256]{1,0:T(8,128)(2,1)S(1)} %collective-permute-done.4.refs_1_), channel_id=1, source_target_pairs={{4,0},{8,4},{12,8},{14,12},{10,14},{6,10},{2,6},{0,2},{5,1},{9,5},... | collective-permute-start | bytes 1572872 | tf_op jit(solution)/shard_map/ppermute | solution.py:368
  41.1 6.9 %collective-permute-start.7 = (bf16[512,256]{1,0:T(8,128)(2,1)S(1)}, bf16[512,256]{1,0:T(8,128)(2,1)S(1)}, u32[]{:S(2)}, u32[]{:S(2)}) collective-permute-start(bf16[512,256]{1,0:T(8,128)(2,1)S(1)} %slice.30), channel_id=1, source_target_pairs={{0,4},{4,8},{8,12},{12,14},{14,10},{10,6},{6,2},{2,0},{1,5},{5,9},... | collective-permute-start | bytes 786440 | tf_op jit(solution)/shard_map/ppermute | solution.py:371
  42.5 6.6 %collective-permute-start.8 = (bf16[512,256]{1,0:T(8,128)(2,1)S(1)}, bf16[512,256]{1,0:T(8,128)(2,1)S(1)}, u32[]{:S(2)}, u32[]{:S(2)}) collective-permute-start(bf16[512,256]{1,0:T(8,128)(2,1)S(1)} %slice.31), channel_id=1, source_target_pairs={{4,0},{8,4},{12,8},{14,12},{10,14},{6,10},{2,6},{0,2},{5,1},{9,5},... | collective-permute-start | bytes 786440 | tf_op jit(solution)/shard_map/ppermute | solution.py:372
  56.3 7.9 %collective-permute-start.11 = (f32[320,256]{1,0:T(8,128)S(1)}, f32[320,256]{1,0:T(8,128)S(1)}, u32[]{:S(2)}, u32[]{:S(2)}) collective-permute-start(f32[320,256]{1,0:T(8,128)S(1)} %get-tuple-element.142), channel_id=1, source_target_pairs={{0,1},{1,0},{2,3},{3,2},{4,5},{5,4},{6,7},{7,6},{8,9},{9,8},{10,11... | collective-permute-start | bytes 983048 | tf_op jit(solution)/shard_map/ppermute | solution.py:442
  58.1 10.2 %collective-permute-start.13 = (bf16[512,256]{1,0:T(8,128)(2,1)S(1)}, bf16[512,256]{1,0:T(8,128)(2,1)S(1)}, u32[]{:S(2)}, u32[]{:S(2)}) collective-permute-start(bf16[512,256]{1,0:T(8,128)(2,1)S(1)} %get-tuple-element.148), channel_id=1, source_target_pairs={{4,0},{8,4},{12,8},{14,12},{10,14},{6,10},{2,6},{0,2},{5,1},{9,5},... | collective-permute-start | bytes 786440 | tf_op jit(solution)/shard_map/ppermute | solution.py:450
  58.9 9.4 %collective-permute-start.12 = (bf16[512,256]{1,0:T(8,128)(2,1)S(1)}, bf16[512,256]{1,0:T(8,128)(2,1)S(1)}, u32[]{:S(2)}, u32[]{:S(2)}) collective-permute-start(bf16[512,256]{1,0:T(8,128)(2,1)S(1)} %get-tuple-element.145), channel_id=1, source_target_pairs={{0,4},{4,8},{8,12},{12,14},{14,10},{10,6},{6,2},{2,0},{1,5},{5,9},... | collective-permute-start | bytes 786440 | tf_op jit(solution)/shard_map/ppermute | solution.py:449
  64.8 9.8 %collective-permute-start.14 = (bf16[80,256]{1,0:T(8,128)(2,1)S(1)}, bf16[80,256]{1,0:T(8,128)(2,1)S(1)}, u32[]{:S(2)}, u32[]{:S(2)}) collective-permute-start(bf16[80,256]{1,0:T(8,128)(2,1)S(1)} %get-tuple-element.154), channel_id=1, source_target_pairs={{0,2},{2,0},{4,6},{6,4},{8,10},{10,8},{12,14},{14,12},{1,3},{3,1},... | collective-permute-start | bytes 122888 | tf_op jit(solution)/shard_map/ppermute | solution.py:411
  65.6 9.0 %collective-permute-start.15 = (bf16[80,256]{1,0:T(8,128)(2,1)S(1)}, bf16[80,256]{1,0:T(8,128)(2,1)S(1)}, u32[]{:S(2)}, u32[]{:S(2)}) collective-permute-start(bf16[80,256]{1,0:T(8,128)(2,1)S(1)} %get-tuple-element.155), channel_id=1, source_target_pairs={{0,4},{2,6},{4,0},{6,2},{8,12},{10,14},{12,8},{14,10},{1,5},{3,7},... | collective-permute-start | bytes 122888 | tf_op jit(solution)/shard_map/ppermute | solution.py:411
  66.8 7.8 %collective-permute-start.16 = (bf16[80,256]{1,0:T(8,128)(2,1)S(1)}, bf16[80,256]{1,0:T(8,128)(2,1)S(1)}, u32[]{:S(2)}, u32[]{:S(2)}) collective-permute-start(bf16[80,256]{1,0:T(8,128)(2,1)S(1)} %get-tuple-element.156), channel_id=1, source_target_pairs={{0,6},{2,4},{4,2},{6,0},{8,14},{10,12},{12,10},{14,8},{1,7},{3,5},... | collective-permute-start | bytes 122888 | tf_op jit(solution)/shard_map/ppermute | solution.py:411
  68.5 13.6 %collective-permute-start.18 = (bf16[1024,256]{1,0:T(8,128)(2,1)S(1)}, bf16[1024,256]{1,0:T(8,128)(2,1)S(1)}, u32[]{:S(2)}, u32[]{:S(2)}) collective-permute-start(bf16[1024,256]{1,0:T(8,128)(2,1)S(1)} %get-tuple-element.162), channel_id=1, source_target_pairs={{4,0},{8,4},{12,8},{14,12},{10,14},{6,10},{2,6},{0,2},{5,1},{9,5},... | collective-permute-start | bytes 1572872 | tf_op jit(solution)/shard_map/ppermute | solution.py:450
  69.3 12.8 %collective-permute-start.17 = (bf16[1024,256]{1,0:T(8,128)(2,1)S(1)}, bf16[1024,256]{1,0:T(8,128)(2,1)S(1)}, u32[]{:S(2)}, u32[]{:S(2)}) collective-permute-start(bf16[1024,256]{1,0:T(8,128)(2,1)S(1)} %get-tuple-element.159), channel_id=1, source_target_pairs={{0,4},{4,8},{8,12},{12,14},{14,10},{10,6},{6,2},{2,0},{1,5},{5,9},... | collective-permute-start | bytes 1572872 | tf_op jit(solution)/shard_map/ppermute | solution.py:449
  74.6 13.8 %collective-permute-start.19 = (bf16[80,256]{1,0:T(8,128)(2,1)S(1)}, bf16[80,256]{1,0:T(8,128)(2,1)S(1)}, u32[]{:S(2)}, u32[]{:S(2)}) collective-permute-start(bf16[80,256]{1,0:T(8,128)(2,1)S(1)} %add_convert_fusion.8), channel_id=1, source_target_pairs={{0,8},{2,10},{4,12},{6,14},{8,0},{10,2},{12,4},{14,6},{1,9},{3,11}... | collective-permute-start | bytes 122888 | tf_op jit(solution)/shard_map/ppermute | solution.py:430
  82.4 13.5 %collective-permute-start.21 = (bf16[1024,256]{1,0:T(8,128)(2,1)S(1)}, bf16[1024,256]{1,0:T(8,128)(2,1)S(1)}, u32[]{:S(2)}, u32[]{:S(2)}) collective-permute-start(bf16[1024,256]{1,0:T(8,128)(2,1)S(1)} %get-tuple-element.174), channel_id=1, source_target_pairs={{4,0},{8,4},{12,8},{14,12},{10,14},{6,10},{2,6},{0,2},{5,1},{9,5},... | collective-permute-start | bytes 1572872 | tf_op jit(solution)/shard_map/ppermute | solution.py:450
  84.1 12.1 %collective-permute-start.20 = (bf16[1024,256]{1,0:T(8,128)(2,1)S(1)}, bf16[1024,256]{1,0:T(8,128)(2,1)S(1)}, u32[]{:S(2)}, u32[]{:S(2)}) collective-permute-start(bf16[1024,256]{1,0:T(8,128)(2,1)S(1)} %get-tuple-element.171), channel_id=1, source_target_pairs={{0,4},{4,8},{8,12},{12,14},{14,10},{10,6},{6,2},{2,0},{1,5},{5,9},... | collective-permute-start | bytes 1572872 | tf_op jit(solution)/shard_map/ppermute | solution.py:449
  88.5 12.7 %collective-permute-start.24 = (bf16[80,256]{1,0:T(8,128)(2,1)S(1)}, bf16[80,256]{1,0:T(8,128)(2,1)S(1)}, u32[]{:S(2)}, u32[]{:S(2)}) collective-permute-start(bf16[80,256]{1,0:T(8,128)(2,1)S(1)} %add_convert_fusion.7.refs_0_), channel_id=1, source_target_pairs={{0,6},{2,4},{4,2},{6,0},{8,14},{10,12},{12,10},{14,8},{1,7},{3,5},... | collective-permute-start | bytes 122888 | tf_op jit(solution)/shard_map/ppermute | solution.py:411
  91.2 10.0 %collective-permute-start.23 = (bf16[80,256]{1,0:T(8,128)(2,1)S(1)}, bf16[80,256]{1,0:T(8,128)(2,1)S(1)}, u32[]{:S(2)}, u32[]{:S(2)}) collective-permute-start(bf16[80,256]{1,0:T(8,128)(2,1)S(1)} %add_convert_fusion.7.refs_0_), channel_id=1, source_target_pairs={{0,4},{2,6},{4,0},{6,2},{8,12},{10,14},{12,8},{14,10},{1,5},{3,7},... | collective-permute-start | bytes 122888 | tf_op jit(solution)/shard_map/ppermute | solution.py:411
  91.6 9.6 %collective-permute-start.22 = (bf16[80,256]{1,0:T(8,128)(2,1)S(1)}, bf16[80,256]{1,0:T(8,128)(2,1)S(1)}, u32[]{:S(2)}, u32[]{:S(2)}) collective-permute-start(bf16[80,256]{1,0:T(8,128)(2,1)S(1)} %add_convert_fusion.7.refs_0_), channel_id=1, source_target_pairs={{0,2},{2,0},{4,6},{6,4},{8,10},{10,8},{12,14},{14,12},{1,3},{3,1},... | collective-permute-start | bytes 122888 | tf_op jit(solution)/shard_map/ppermute | solution.py:411
  96.5 11.1 %collective-permute-start.26 = (bf16[1024,256]{1,0:T(8,128)(2,1)S(1)}, bf16[1024,256]{1,0:T(8,128)(2,1)S(1)}, u32[]{:S(2)}, u32[]{:S(2)}) collective-permute-start(bf16[1024,256]{1,0:T(8,128)(2,1)S(1)} %get-tuple-element.183), channel_id=1, source_target_pairs={{4,0},{8,4},{12,8},{14,12},{10,14},{6,10},{2,6},{0,2},{5,1},{9,5},... | collective-permute-start | bytes 1572872 | tf_op jit(solution)/shard_map/ppermute | solution.py:450
  97.8 10.3 %collective-permute-start.25 = (bf16[1024,256]{1,0:T(8,128)(2,1)S(1)}, bf16[1024,256]{1,0:T(8,128)(2,1)S(1)}, u32[]{:S(2)}, u32[]{:S(2)}) collective-permute-start(bf16[1024,256]{1,0:T(8,128)(2,1)S(1)} %get-tuple-element.182), channel_id=1, source_target_pairs={{0,4},{4,8},{8,12},{12,14},{14,10},{10,6},{6,2},{2,0},{1,5},{5,9},... | collective-permute-start | bytes 1572872 | tf_op jit(solution)/shard_map/ppermute | solution.py:449
  (14 other events, 60.9 us)
